TPU v7x, 32 devices: a whole 2x2x4 slice. The times are simulated.
32 devices in a mesh: groups: 2 (over x), tracks: 8 (over z, y), frames: 2 (over core).
Axes of the slice: x: 2, y: 2, z: 4, core: 2. Of those that a mesh axis runs over, the one named last changes fastest.
Arguments:
- tokens: bfloat16 [256, 256, 384], P(('groups', 'tracks'), 'frames'), parts along dimension 0, may hold values from -6 to 6
- first_frame: int32 [256], P(('groups', 'tracks')), parts along dimension 0, may hold values from 0 to 127
- visible: int32 [256, 256], P(('groups', 'tracks')), parts along dimension 0, may hold values 0 or 1
- time_qkv: bfloat16 [384, 1152], replicated, may hold values from -0.3125 to 0.3125
- time_output: bfloat16 [384, 384], replicated, may hold values from -0.3125 to 0.3125
- expand: bfloat16 [384, 1536], replicated, may hold values from -0.3125 to 0.3125
- shrink: bfloat16 [1536, 384], replicated, may hold values from -0.15625 to 0.15625
- virtual_init: bfloat16 [64, 384], replicated, may hold values from -6 to 6
- cross_query: bfloat16 [384, 384], replicated, may hold values from -0.3125 to 0.3125
- cross_kv: bfloat16 [384, 768], replicated, may hold values from -0.3125 to 0.3125
- cross_output: bfloat16 [384, 384], replicated, may hold values from -1.25 to 1.25
- self_qkv: bfloat16 [384, 1152], replicated, may hold values from -0.3125 to 0.3125
- self_output: bfloat16 [384, 384], replicated, may hold values from -0.625 to 0.625
- back_query: bfloat16 [384, 384], replicated, may hold values from -0.3125 to 0.3125
- back_kv: bfloat16 [384, 768], replicated, may hold values from -0.3125 to 0.3125
- back_output: bfloat16 [384, 384], replicated, may hold values from -1.25 to 1.25
Outputs:
- tracked: bfloat16 [256, 256, 384], P(('groups', 'tracks'), 'frames'), parts along dimension 0
There are 2 independent parts, one for each index of `groups`. A program takes and returns all parts, laid end to end along the dimension named above; an argument that names none is the same for every part. Nothing has to cross between parts.
Inputs may be any that keep to these rules, and one draw needn't show every extreme that they name: `first_frame`: each track's first frame.
All inputs are finite; a program needn't handle non-finite values. No bound on the sum of `visible` on one device may be relied on, other than what follows from the above.
Results may differ from a plain program's by a relative error of at most 0.0095.
Values may be sent and summed in bfloat16 or wider, within the bound.
No kernel may reach another device: no remote copies, remote signals or barrier semaphores. Data moves between devices by JAX's collectives and lax.ppermute only.
A program may use at most 128 MiB of HBM per device.

v0:
```python
import functools

import jax
import jax.numpy as jnp
from jax import lax
from jax.experimental import pallas as pl
from jax.experimental.pallas import tpu as pltpu
from jax.sharding import PartitionSpec as P

HEADS = 8
HALF = HEADS // 2
EPS = 1e-06
BF = jnp.bfloat16
F32 = jnp.float32
VMEM = 62 * 1024 * 1024


def dot(a, b):
    return lax.dot_general(a, b, (((1,), (0,)), ((), ())), preferred_element_type=F32)


def dot_t(a, b):
    return lax.dot_general(a, b, (((1,), (1,)), ((), ())), preferred_element_type=F32)


def normed(x, scale=None):
    r = lax.rsqrt(jnp.mean(x * x, axis=-1, keepdims=True) + EPS)
    return x * (r if scale is None else r * scale)


def gelu(x):
    c = 0.7978845608028654
    h = 0.5 * x
    return h + h * jnp.tanh(x * (c + (c * 0.044715) * (x * x)))


def iota(rows, columns, axis):
    return lax.broadcasted_iota(jnp.int32, (rows, columns), axis)


def within(lane, start, count):
    return (lane >= start) & (lane < start + count)


class Lanes:
    def __init__(self, d):
        self.d = d
        self.head = d // HEADS
        self.width = -(-HALF * self.head // 128) * 128
        self.over = 2 * self.width - d
        self.spare = self.width - HALF * self.head
        assert self.spare >= 16 * HALF and self.over == 128 and self.spare <= 64
        self.begin = (0, d - self.width)
        self.first = (0, self.spare)
        self.sums = (HALF * self.head, 0)

    def cut(self, x, w):
        return x[:, self.begin[w] : self.begin[w] + self.width]

    def heads(self, rows, w):
        lane = iota(rows, self.width, 1)
        return [jnp.where(within(lane, self.first[w] + h * self.head, self.head), 1.0, 0.0).astype(BF) for h in range(HALF)]

    def sum_lanes(self, rows, w):
        lane = iota(rows, self.width, 1)
        return [jnp.where(within(lane, self.sums[w] + 16 * h, 16), 1.0, 0.0).astype(BF) for h in range(HALF)]

    def with_ones(self, v, w):
        lane = iota(v.shape[0], self.width, 1)
        return jnp.where(within(lane, self.first[w], HALF * self.head), self.cut(v, w), 1.0)

    def choose(self, o, rows, w):
        lane = iota(rows, self.width, 1)
        out = o[:rows]
        for h in range(1, HALF):
            own = within(lane, self.first[w] + h * self.head, self.head) | within(lane, self.sums[w] + 16 * h, 16)
            out = jnp.where(own, o[h * rows : (h + 1) * rows], out)
        return out

    def divide(self, low, high):
        rows = low.shape[0]
        lane = iota(rows, 128, 1)
        cut = self.width - self.over
        low_part, high_part = low[:, cut:], high[:, : self.over]
        split = self.over - self.spare
        sums = 1.0 / jnp.where(lane < split, high_part, low_part)
        pieces = [low[:, i : i + 128] for i in range(0, cut, 128)]
        pieces.append(jnp.where(lane < split, low_part, high_part))
        pieces += [high[:, i : i + 128] for i in range(self.over, self.width, 128)]
        out = []
        for i, piece in enumerate(pieces):
            head = (lane + 128 * i) // self.head
            spot = jnp.where(head < HALF, self.sums[0] - cut + 16 * head, self.sums[1] + 16 * (head - HALF))
            out.append(piece * jnp.take_along_axis(sums, spot, axis=1))
        return jnp.concatenate(out, axis=1).astype(BF)


def settle(own, other, usable, qkv_ref, out_w_ref, expand_ref, shrink_ref):
    tracks = len(usable)
    d = own.shape[1]
    half = own.shape[0] // tracks
    lanes = Lanes(d)
    own_norm = normed(own).astype(BF)
    query = normed(dot(own_norm, qkv_ref[:, :d]), lanes.head**-0.5).astype(BF)
    both = dot(jnp.concatenate([own_norm, normed(other).astype(BF)], axis=0), qkv_ref[:, d:])
    key = normed(both[:, :d]).astype(BF)
    value = both[:, d:]
    masks = [lanes.heads(half, w) for w in range(2)]
    mixed = []
    for i in range(tracks):
        mine = slice(i * half, (i + 1) * half)
        away = slice((tracks + i) * half, (tracks + i + 1) * half)
        k = jnp.concatenate([key[mine], key[away]], axis=0)
        v = jnp.concatenate([value[mine], value[away]], axis=0)
        pair = []
        for w in range(2):
            q = lanes.cut(query[mine], w)
            scores = dot_t(jnp.concatenate([q * m for m in masks[w]], axis=0), lanes.cut(k, w))
            weights = jnp.exp(scores).astype(BF)
            use = jnp.concatenate([usable[i]] * (lanes.width // 128), axis=1)
            o = dot(weights, (lanes.with_ones(v, w) * use).astype(BF))
            pair.append(lanes.choose(o, half, w))
        mixed.append(lanes.divide(*pair))
    middle = own + dot(jnp.concatenate(mixed, axis=0), out_w_ref[...])
    hidden = gelu(dot(normed(middle).astype(BF), expand_ref[...])).astype(BF)
    return (middle + dot(hidden, shrink_ref[...])).astype(BF)


def usable_columns(core, first, seen):
    length = seen.shape[1]
    frame = iota(1, length, 1)
    use = (frame >= first) & ((seen == 1) | (frame == first))
    use = jnp.where(use, 1.0, 0.0)
    low, high = use[:, : length // 2], use[:, length // 2 :]
    use = jnp.concatenate([jnp.where(core == 0, low, high), jnp.where(core == 0, high, low)], axis=1)
    return jnp.transpose(jnp.broadcast_to(use, (128, length)), (1, 0))


def time_kernel(tps, begin, info_ref, first_ref, visible_ref, own_ref, other_ref, *refs):
    weights, outs, kept_ref = refs[:4], refs[4:-1], refs[-1]
    half, d = own_ref.shape[1:]
    step = pl.program_id(0)
    usable = []
    for i in range(tps):
        track = begin + step * tps + i
        usable.append(usable_columns(info_ref[0], first_ref[track], visible_ref[pl.ds(track, 1), :]))
    own = own_ref[...].reshape(tps * half, d).astype(F32)
    other = other_ref[...].reshape(tps * half, d).astype(F32)
    settled = settle(own, other, usable, *weights)
    if len(outs[0].shape) == 3 and len(outs) == 1 and outs[0].shape[1] == half:
        outs[0][...] = settled.reshape(tps, half, d)
        return
    pieces = len(outs) > 1
    spots = len(outs) if pieces else outs[0].shape[0]
    rows = half // spots
    if not pieces:
        for t in range(spots):
            for i in range(tps):
                at = i * half + t * rows
                outs[0][t, i * rows : (i + 1) * rows, :] = settled[at : at + rows]
        return
    kept_ref[...] = settled
    for k in range(spots):
        t = lax.rem(info_ref[1] + k, spots)
        for i in range(tps):
            at = pl.multiple_of(i * half + t * rows, rows)
            outs[k][i * rows : (i + 1) * rows, :] = kept_ref[pl.ds(at, rows), :]


def full(shape):
    return pl.BlockSpec(shape, lambda *_: (0,) * len(shape))


def time_part(tokens, other, first_frame, visible, info, weights, spots, form, begin, count, after):
    _, half, d = tokens.shape
    rows = half // spots
    tps = 2
    if form == "tracks":
        shapes, blocks = [(count, half, d)], [pl.BlockSpec((tps, half, d), lambda i, *_: (i, 0, 0))]
    elif form == "dense":
        shapes, blocks = [(spots, count * rows, d)], [pl.BlockSpec((spots, tps * rows, d), lambda i, *_: (0, i, 0))]
    else:
        shapes, blocks = [(count * rows, d)] * spots, [pl.BlockSpec((tps * rows, d), lambda i, *_: (i, 0))] * spots
    total = count * half
    block = pl.BlockSpec((tps, half, d), lambda i, *_: (i, 0, 0))
    kernel = functools.partial(time_kernel, tps, begin)
    extra = [] if after is None else [after]
    if extra:
        inner = kernel

        def kernel(info_ref, first_ref, after_ref, *refs):
            inner(info_ref, first_ref, *refs)

    return pl.pallas_call(
        kernel,
        out_shape=[jax.ShapeDtypeStruct(s, BF) for s in shapes],
        grid_spec=pltpu.PrefetchScalarGridSpec(
            num_scalar_prefetch=2,
            grid=(count // tps,),
            in_specs=[pl.BlockSpec(memory_space=pl.ANY)] * len(extra)
            + [full(visible.shape), pl.BlockSpec((tps, half, d), lambda i, *_: (begin // tps + i, 0, 0)), block]
            + [full(w.shape) for w in weights],
            out_specs=blocks,
            scratch_shapes=[pltpu.VMEM((tps * half, d), BF)],
        ),
        compiler_params=pltpu.CompilerParams(vmem_limit_bytes=VMEM),
        cost_estimate=pl.CostEstimate(flops=total * 5_000_000, bytes_accessed=total * d * 4, transcendentals=total * 3600),
        name="time_part",
    )(info, first_frame, *extra, visible, tokens, other, *weights)


def gather_matrix(out_rows, in_rows, source):
    r, c = iota(out_rows, in_rows, 0), iota(out_rows, in_rows, 1)
    return jnp.where(c == source(r), 1.0, 0.0).astype(BF)


class Server:
    def __init__(self, weights):
        init_ref, cq_ref, self.ckv, self.co, self.sqkv, self.so, self.bq, self.bkv, self.bo = weights
        self.init = init_ref[...].astype(F32)
        self.virt, self.d = self.init.shape
        self.lanes = lanes = Lanes(self.d)
        self.tau = lanes.head**-0.5
        vq = normed(dot(normed(self.init).astype(BF), cq_ref[...]), self.tau).astype(BF)
        self.masks = [lanes.heads(self.virt, w) for w in range(2)]
        self.sums = [lanes.sum_lanes(self.virt, w) for w in range(2)]
        self.stacked = [
            jnp.concatenate([lanes.cut(vq, w) * m for m in self.masks[w]], axis=0) for w in range(2)
        ]

    def attend(self, query, key, value):
        lanes, pair = self.lanes, []
        for w in range(2):
            k, v = lanes.cut(key, w), lanes.cut(value, w)
            ks = jnp.concatenate([k * m for m in self.masks[w]], axis=0)
            vs = jnp.concatenate([v * m + s for m, s in zip(self.masks[w], self.sums[w])], axis=0)
            pair.append(dot(jnp.exp(dot_t(lanes.cut(query, w), ks)).astype(BF), vs))
        return pair

    def divide(self, pairs):
        return self.lanes.divide(*[jnp.concatenate([p[w] for p in pairs], axis=0) for w in range(2)])

    def run(self, settled, frames):
        d, lanes, virt = self.d, self.lanes, self.virt
        tracks = settled.shape[0] // frames
        settled_norm = normed(settled).astype(BF)
        crossed = dot(settled_norm, self.ckv[...])
        track_key = normed(crossed[:, :d]).astype(BF)
        track_value = crossed[:, d:]
        track_query = normed(dot(settled_norm, self.bq[...]), self.tau).astype(BF)
        ones = [lanes.with_ones(track_value, w).astype(BF) for w in range(2)]
        pairs = []
        for f in range(frames):
            rows = slice(f * tracks, (f + 1) * tracks)
            pair = []
            for w in range(2):
                p = jnp.exp(dot_t(self.stacked[w], lanes.cut(track_key[rows], w))).astype(BF)
                pair.append(lanes.choose(dot(p, ones[w][rows]), virt, w))
            pairs.append(pair)
        virtual = jnp.concatenate([self.init] * frames, axis=0) + dot(self.divide(pairs), self.co[...])
        selfed = dot(normed(virtual).astype(BF), self.sqkv[...])
        query = normed(selfed[:, :d], self.tau).astype(BF)
        key = normed(selfed[:, d : 2 * d]).astype(BF)
        value = selfed[:, 2 * d :].astype(BF)
        at = [slice(f * virt, (f + 1) * virt) for f in range(frames)]
        mixed = self.divide([self.attend(query[r], key[r], value[r]) for r in at])
        virtual = virtual + dot(mixed, self.so[...])
        backed = dot(normed(virtual).astype(BF), self.bkv[...])
        key = normed(backed[:, :d]).astype(BF)
        value = backed[:, d:].astype(BF)
        mixed = self.divide(
            [self.attend(track_query[f * tracks : (f + 1) * tracks], key[r], value[r]) for f, r in enumerate(at)]
        )
        return (settled + dot(mixed, self.bo[...])).astype(BF)


def rows_kernel(frames, block, group, x_ref, *refs):
    weights, out_ref, rows_ref = refs[:-2], refs[-2], refs[-1]
    total = x_ref.shape[0]
    tracks = total // frames
    part = group // frames
    there = gather_matrix(group, group, lambda r: (r % part) * frames + r // part)
    for g in range(total // group):
        moved = dot(there, x_ref[g * group : (g + 1) * group, :]).astype(BF)
        for f in range(frames):
            rows_ref[f * tracks + g * part : f * tracks + (g + 1) * part, :] = moved[f * part : (f + 1) * part]
    server = Server(weights)

    def body(b, carry):
        at = pl.ds(pl.multiple_of(b * (block * tracks), block * tracks), block * tracks)
        rows_ref[at, :] = server.run(rows_ref[at, :].astype(F32), block)
        return carry

    lax.fori_loop(0, frames // block, body, 0)
    back = gather_matrix(group, group, lambda r: (r % frames) * part + r // frames)
    for g in range(total // group):
        moved = jnp.concatenate(
            [rows_ref[f * tracks + g * part : f * tracks + (g + 1) * part, :] for f in range(frames)], axis=0
        )
        out_ref[g * group : (g + 1) * group, :] = dot(back, moved).astype(BF)


def rows_part(x, frames, weights):
    return pl.pallas_call(
        functools.partial(rows_kernel, frames, min(frames, 4), max(256, 16 * frames)),
        out_shape=jax.ShapeDtypeStruct(x.shape, BF),
        grid=(1,),
        in_specs=[full(a.shape) for a in (x, *weights)],
        out_specs=full(x.shape),
        scratch_shapes=[pltpu.VMEM(x.shape, BF)],
        compiler_params=pltpu.CompilerParams(vmem_limit_bytes=VMEM),
        name="rows_part",
    )(x, *weights)


def frames_kernel(spots, begin, frames, block, pieces, info_ref, dense_ref, *refs):
    xs, weights = refs[:spots], refs[spots : spots + 9]
    outs, rows_ref = refs[spots + 9 : -1], refs[-1]
    depth = dense_ref.shape[1] + xs[0].shape[0]
    span = pieces
    both = depth // span
    tracks = spots * both
    pick = gather_matrix(frames * both, depth, lambda r: (r % both) * span + begin + r // both)
    for k in range(spots):
        rows = jnp.concatenate([dense_ref[lax.rem(info_ref[1] + spots - k, spots)], xs[k][...]], axis=0)
        moved = dot(pick, rows).astype(BF)
        for f in range(frames):
            rows_ref[f * tracks + k * both : f * tracks + (k + 1) * both, :] = moved[f * both : (f + 1) * both]
    server = Server(weights)

    def body(b, carry):
        at = pl.ds(pl.multiple_of(b * (block * tracks), block * tracks), block * tracks)
        tracked = server.run(rows_ref[at, :].astype(F32), block)
        for f in range(block):
            to = pl.ds(pl.multiple_of((b * block + f) * both, both), both)
            for k in range(spots):
                rows = tracked[f * tracks + k * both : f * tracks + (k + 1) * both]
                if len(outs) > 1:
                    outs[k][to, :] = rows
                else:
                    outs[0][lax.rem(info_ref[1] + spots - k, spots), to, :] = rows
        return carry

    lax.fori_loop(0, frames // block, body, 0)


def frames_part(dense, xs, info, span, form, begin, frames, block, weights):
    spots, _, d = dense.shape
    both = (dense.shape[1] + xs[0].shape[0]) // span
    if form == "dense":
        shapes = [(spots, frames * both, d)]
    else:
        shapes = [(frames * both, d)] * spots
    rows = frames * spots * both
    return pl.pallas_call(
        functools.partial(frames_kernel, spots, begin, frames, block, span),
        out_shape=[jax.ShapeDtypeStruct(s, BF) for s in shapes],
        grid_spec=pltpu.PrefetchScalarGridSpec(
            num_scalar_prefetch=1,
            grid=(1,),
            in_specs=[full(a.shape) for a in (dense, *xs, *weights)],
            out_specs=[full(s) for s in shapes],
            scratch_shapes=[pltpu.VMEM((rows, d), BF)],
        ),
        compiler_params=pltpu.CompilerParams(vmem_limit_bytes=VMEM),
        cost_estimate=pl.CostEstimate(flops=rows * 10_000_000, bytes_accessed=rows * d * 4, transcendentals=rows * 2000),
        name="frames_part",
    )(info, dense, *xs, *weights)


def home_kernel(spots, info_ref, dense_ref, *refs):
    xs, out_ref = refs[:-1], refs[-1]
    tracks, _, d = out_ref.shape
    depth = dense_ref.shape[1] + xs[0].shape[0]
    span = depth // tracks
    pick = gather_matrix(depth, depth, lambda r: (r % span) * tracks + r // span)
    for k in range(spots):
        t = lax.rem(info_ref[1] + k, spots)
        rows = jnp.concatenate([dense_ref[t], xs[k][...]], axis=0)
        at = pl.ds(pl.multiple_of(t * span, span), span)
        out_ref[:, at, :] = dot(pick, rows).astype(BF).reshape(tracks, span, d)


def home(dense, xs, info, tracks):
    spots, _, d = dense.shape
    out = (tracks, spots * (dense.shape[1] + xs[0].shape[0]) // tracks, d)
    return pl.pallas_call(
        functools.partial(home_kernel, spots),
        out_shape=jax.ShapeDtypeStruct(out, BF),
        grid_spec=pltpu.PrefetchScalarGridSpec(
            num_scalar_prefetch=1,
            grid=(1,),
            in_specs=[full(a.shape) for a in (dense, *xs)],
            out_specs=full(out),
        ),
        compiler_params=pltpu.CompilerParams(vmem_limit_bytes=VMEM),
        name="home",
    )(info, dense, *xs)


def exchange(x):
    return lax.all_to_all(x, "tracks", split_axis=0, concat_axis=0, tiled=True)


def swap_cores(x):
    return lax.ppermute(x, "frames", [(0, 1), (1, 0)])


def shift(xs, spots, sign):
    return [xs[0]] + [
        lax.ppermute(xs[k], "tracks", [(i, (i + sign * k) % spots) for i in range(spots)]) for k in range(1, spots)
    ]


def simple(spots, tokens, first_frame, visible, info, time_weights, virtual_weights):
    tracks, half, d = tokens.shape
    rows = half // spots
    (settled,) = time_part(
        tokens, swap_cores(tokens), first_frame, visible, info, time_weights, spots, "tracks", 0, tracks, None
    )
    settled = jnp.transpose(settled.reshape(tracks, spots, rows, d), (1, 0, 2, 3))
    tracked = rows_part(exchange(settled).reshape(-1, d), rows, virtual_weights)
    joined = exchange(tracked.reshape(spots, tracks, rows, d))
    return jnp.transpose(joined, (1, 0, 2, 3)).reshape(tracks, half, d)


def pipelined(spots, tokens, first_frame, visible, info, time_weights, virtual_weights):
    tracks, half, d = tokens.shape
    rows = half // spots
    n = FIRST_TRACKS
    common = (first_frame, visible, info, time_weights, spots)
    (dense,) = time_part(tokens, swap_cores(tokens[:n]), *common, "dense", 0, n, None)
    pieces = time_part(tokens, swap_cores(tokens[n:]), *common, "pieces", n, tracks - n, dense)
    dense = exchange(dense)
    pieces = shift(pieces, spots, 1)
    m = FIRST_FRAMES
    (first,) = frames_part(dense, pieces, info, rows, "dense", 0, m, BLOCK, virtual_weights)
    rest = frames_part(dense, pieces, info, rows, "pieces", m, rows - m, BLOCK, virtual_weights)
    return home(exchange(first), shift(rest, spots, -1), info, tracks)


def per_device(spots, tokens, first_frame, visible, *weights):
    tracks, half, _ = tokens.shape
    rows = half // spots
    fits = tracks % 16 == 0 and rows % 16 == 0 and FIRST_TRACKS < tracks and FIRST_FRAMES < rows
    info = jnp.stack([lax.axis_index("frames"), lax.axis_index("tracks")]).astype(jnp.int32)
    run = pipelined if fits else simple
    return run(spots, tokens, first_frame, visible, info, weights[:4], weights[4:])


FIRST_TRACKS = 8
FIRST_FRAMES = 8
BLOCK = 4


def solution(mesh):
    rows = ("groups", "tracks")
    placed = (P(rows, "frames", None), P(rows), P(rows, None)) + (P(),) * 13
    return jax.shard_map(
        functools.partial(per_device, mesh.shape["tracks"]),
        mesh=mesh,
        in_specs=placed,
        out_specs=P(rows, "frames", None),
        check_vma=False,
    )
```

profile of v0, /device:TPU:0, one launch (start us, length us, event | category | flops | bytes accessed | tf_op | source)
XLA Modules:
  0.0 133.9 jit_solution(944084617950247018)
XLA Ops:
  0.0 1.6 %fusion = (bf16[8,128,384]{2,1,0:T(8,128)(2,1)S(1)}, bf16[8,128,384]{2,1,0:T(8,128)(2,1)S(1)}) fusion(bf16[16,128,384]{2,1,0:T(8,128)(2,1)} %refs_1_.3), kind=kLoop, calls=%fused_computation.1 | loop fusion | bytes 3145728 | tf_op jit(solution)/shard_map/slice | solution.py:433
  1.6 0.5 collective-permute-start
  2.1 0.1 collective-permute-start.1
  2.2 0.6 pad_add_fusion.info_ref
  2.8 1.5 %collective-permute-done.other_ref = bf16[8,128,384]{2,1,0:T(8,128)(2,1)S(1)} collective-permute-done((bf16[8,128,384]{2,1,0:T(8,128)(2,1)S(1)}, bf16[8,128,384]{2,1,0:T(8,128)(2,1)S(1)}, u32[]{:S(2)}, u32[]{:S(2)}) %collective-permute-start) | collective-permute-done | bytes 786464 | tf_op jit(solution)/shard_map/ppermute | solution.py:406
  4.3 0.9 copy-done.9
  5.2 15.5 %time_part.2.after_ref = bf16[8,128,384]{2,1,0:T(8,128)(2,1)} custom-call(s32[2]{0:T(128)} %pad_add_fusion.info_ref, s32[16]{0:T(128)} %first_ref.3, s32[16,256]{1,0:T(8,128)} %refs_0_.3, bf16[16,128,384]{2,1,0:T(8,128)(2,1)} %refs_1_.3, bf16[8,128,384]{2,1,0:T(8,128)(2,1)} %copy-done.9, bf16[384,1152]{1,0:T(8,128)(2,1)} %refs_3_.3, ...), custom_call_target="tpu_custom_call" | custom-call | flops 5120000000 | bytes 1572864 | tf_op jit(solution)/shard_map/time_part/pallas_call | solution.py:194
  20.7 7.2 %all-to-all-start = ((bf16[8,128,384]{2,1,0:T(8,128)(2,1)}), bf16[8,128,384]{2,1,0:T(8,128)(2,1)S(1)}, u32[]{:S(2)}, u32[]{:S(2)}) async-start(bf16[8,128,384]{2,1,0:T(8,128)(2,1)} %time_part.2.after_ref), calls=%async_computation | async-start | bytes 1572864 | tf_op jit(solution)/shard_map/all_to_all | solution.py:402
  27.9 0.0 collective-permute-done.1.refs_2_
  27.9 15.7 %time_part.3 = (bf16[128,384]{1,0:T(8,128)(2,1)}, bf16[128,384]{1,0:T(8,128)(2,1)}, bf16[128,384]{1,0:T(8,128)(2,1)}, bf16[128,384]{1,0:T(8,128)(2,1)}, bf16[128...) custom-call(s32[2]{0:T(128)} %pad_add_fusion.info_ref, ...), custom_call_target="tpu_custom_call" | custom-call | flops 5120000000 | bytes 1572864 | tf_op jit(solution)/shard_map/time_part/pallas_call | solution.py:194
  43.6 2.1 %collective-permute-start.2 = (bf16[128,384]{1,0:T(8,128)(2,1)}, bf16[128,384]{1,0:T(8,128)(2,1)S(1)}, u32[]{:S(2)}, u32[]{:S(2)}) collective-permute-start(bf16[128,384]{1,0:T(8,128)(2,1)} %get-tuple-element.22), channel_id=1, source_target_pairs={{0,2},{2,4},{4,6},{6,8},{8,10},{10,12},{12,14},{14,0},{1,3},{3,5},... | collective-permute-start | bytes 294920 | tf_op jit(solution)/shard_map/ppermute | solution.py:411
  45.7 1.5 %collective-permute-start.3 = (bf16[128,384]{1,0:T(8,128)(2,1)}, bf16[128,384]{1,0:T(8,128)(2,1)S(1)}, u32[]{:S(2)}, u32[]{:S(2)}) collective-permute-start(bf16[128,384]{1,0:T(8,128)(2,1)} %get-tuple-element.23), channel_id=1, source_target_pairs={{0,4},{2,6},{4,8},{6,10},{8,12},{10,14},{12,0},{14,2},{1,5},{3,7},... | collective-permute-start | bytes 294920 | tf_op jit(solution)/shard_map/ppermute | solution.py:411
  47.2 2.4 %collective-permute-start.4 = (bf16[128,384]{1,0:T(8,128)(2,1)}, bf16[128,384]{1,0:T(8,128)(2,1)S(1)}, u32[]{:S(2)}, u32[]{:S(2)}) collective-permute-start(bf16[128,384]{1,0:T(8,128)(2,1)} %get-tuple-element.24), channel_id=1, source_target_pairs={{0,6},{2,8},{4,10},{6,12},{8,14},{10,0},{12,2},{14,4},{1,7},{3,9},... | collective-permute-start | bytes 294920 | tf_op jit(solution)/shard_map/ppermute | solution.py:411
  49.5 1.5 %collective-permute-start.5 = (bf16[128,384]{1,0:T(8,128)(2,1)}, bf16[128,384]{1,0:T(8,128)(2,1)S(1)}, u32[]{:S(2)}, u32[]{:S(2)}) collective-permute-start(bf16[128,384]{1,0:T(8,128)(2,1)} %get-tuple-element.25), channel_id=1, source_target_pairs={{0,8},{2,10},{4,12},{6,14},{8,0},{10,2},{12,4},{14,6},{1,9},{3,11}... | collective-permute-start | bytes 294920 | tf_op jit(solution)/shard_map/ppermute | solution.py:411
  51.0 2.4 %collective-permute-start.6 = (bf16[128,384]{1,0:T(8,128)(2,1)}, bf16[128,384]{1,0:T(8,128)(2,1)S(1)}, u32[]{:S(2)}, u32[]{:S(2)}) collective-permute-start(bf16[128,384]{1,0:T(8,128)(2,1)} %get-tuple-element.26), channel_id=1, source_target_pairs={{0,10},{2,12},{4,14},{6,0},{8,2},{10,4},{12,6},{14,8},{1,11},{3,13... | collective-permute-start | bytes 294920 | tf_op jit(solution)/shard_map/ppermute | solution.py:411
  53.4 0.0 collective-permute-done.2.refs_1_
  53.4 1.5 %collective-permute-start.7 = (bf16[128,384]{1,0:T(8,128)(2,1)}, bf16[128,384]{1,0:T(8,128)(2,1)S(1)}, u32[]{:S(2)}, u32[]{:S(2)}) collective-permute-start(bf16[128,384]{1,0:T(8,128)(2,1)} %get-tuple-element.27), channel_id=1, source_target_pairs={{0,12},{2,14},{4,0},{6,2},{8,4},{10,6},{12,8},{14,10},{1,13},{3,15... | collective-permute-start | bytes 294920 | tf_op jit(solution)/shard_map/ppermute | solution.py:411
  54.8 0.0 collective-permute-done.3.refs_2_
  54.8 1.5 %collective-permute-start.8 = (bf16[128,384]{1,0:T(8,128)(2,1)}, bf16[128,384]{1,0:T(8,128)(2,1)S(1)}, u32[]{:S(2)}, u32[]{:S(2)}) collective-permute-start(bf16[128,384]{1,0:T(8,128)(2,1)} %get-tuple-element.28), channel_id=1, source_target_pairs={{0,14},{2,0},{4,2},{6,4},{8,6},{10,8},{12,10},{14,12},{1,15},{3,1}... | collective-permute-start | bytes 294920 | tf_op jit(solution)/shard_map/ppermute | solution.py:411
  56.3 3.6 %collective-permute-done.4.refs_3_ = bf16[128,384]{1,0:T(8,128)(2,1)S(1)} collective-permute-done((bf16[128,384]{1,0:T(8,128)(2,1)}, bf16[128,384]{1,0:T(8,128)(2,1)S(1)}, u32[]{:S(2)}, u32[]{:S(2)}) %collective-permute-start.4) | collective-permute-done | bytes 98336 | tf_op jit(solution)/shard_map/ppermute | solution.py:411
  59.9 1.0 collective-permute-done.5.refs_4_
  61.0 0.0 collective-permute-done.6.refs_5_
  61.0 0.0 collective-permute-done.7.refs_6_
  61.0 0.0 collective-permute-done.8.refs_7_
  61.0 0.0 all-to-all-done.dense_ref
  61.0 0.0 copy-start.1
  61.0 0.5 copy-done.13
  61.6 0.0 copy-done.14
  61.6 0.0 copy-done.15
  61.7 0.0 copy-done.16
  61.7 0.3 copy-done.1
  62.0 17.6 %frames_part.2 = bf16[8,128,384]{2,1,0:T(8,128)(2,1)} custom-call(s32[2]{0:T(128)} %pad_add_fusion.info_ref, bf16[8,128,384]{2,1,0:T(8,128)(2,1)} %copy-done.1, bf16[128,384]{1,0:T(8,128)(2,1)} %get-tuple-element.21.refs_0_, bf16[128,384]{1,0:T(8,128)(2,1)} %copy-done.10, bf16[128,384]{1,0:T(8,128)(2,1)} %copy-done.11, bf16[128,384]{1,0:T(8,128)(2,1)} %copy-done.12, ...), custom_call_target="tpu_custom_call" | custom-call | flops 10240000000 | bytes 1572864 | tf_op jit(solution)/shard_map/frames_part/pallas_call | solution.py:355
  79.6 9.9 %all-to-all-start.1 = ((bf16[8,128,384]{2,1,0:T(8,128)(2,1)}), bf16[8,128,384]{2,1,0:T(8,128)(2,1)S(1)}, u32[]{:S(2)}, u32[]{:S(2)}) async-start(bf16[8,128,384]{2,1,0:T(8,128)(2,1)} %frames_part.2), calls=%async_computation.1 | async-start | bytes 1572864 | tf_op jit(solution)/shard_map/all_to_all | solution.py:402
  89.5 17.6 %frames_part.3 = (bf16[128,384]{1,0:T(8,128)(2,1)}, bf16[128,384]{1,0:T(8,128)(2,1)}, bf16[128,384]{1,0:T(8,128)(2,1)}, bf16[128,384]{1,0:T(8,128)(2,1)}, bf16[1...) custom-call(s32[2]{0:T(128)} %pad_add_fusion.info_ref, ...), custom_call_target="tpu_custom_call" | custom-call | flops 10240000000 | bytes 1572864 | tf_op jit(solution)/shard_map/frames_part/pallas_call | solution.py:355
  107.1 3.9 %collective-permute-start.10 = (bf16[128,384]{1,0:T(8,128)(2,1)}, bf16[128,384]{1,0:T(8,128)(2,1)S(1)}, u32[]{:S(2)}, u32[]{:S(2)}) collective-permute-start(bf16[128,384]{1,0:T(8,128)(2,1)} %get-tuple-element.31), channel_id=1, source_target_pairs={{0,12},{2,14},{4,0},{6,2},{8,4},{10,6},{12,8},{14,10},{1,13},{3,15... | collective-permute-start | bytes 294920 | tf_op jit(solution)/shard_map/ppermute | solution.py:411
  110.9 0.6 collective-permute-start.11
  111.5 3.3 %collective-permute-start.12 = (bf16[128,384]{1,0:T(8,128)(2,1)}, bf16[128,384]{1,0:T(8,128)(2,1)S(1)}, u32[]{:S(2)}, u32[]{:S(2)}) collective-permute-start(bf16[128,384]{1,0:T(8,128)(2,1)} %get-tuple-element.33), channel_id=1, source_target_pairs={{0,8},{2,10},{4,12},{6,14},{8,0},{10,2},{12,4},{14,6},{1,9},{3,11}... | collective-permute-start | bytes 294920 | tf_op jit(solution)/shard_map/ppermute | solution.py:411
  114.8 0.0 collective-permute-start.13
  114.8 1.1 collective-permute-start.14
  115.9 0.0 collective-permute-done.10.refs_2_
  115.9 1.5 %collective-permute-start.15 = (bf16[128,384]{1,0:T(8,128)(2,1)}, bf16[128,384]{1,0:T(8,128)(2,1)S(1)}, u32[]{:S(2)}, u32[]{:S(2)}) collective-permute-start(bf16[128,384]{1,0:T(8,128)(2,1)} %get-tuple-element.36), channel_id=1, source_target_pairs={{0,2},{2,4},{4,6},{6,8},{8,10},{10,12},{12,14},{14,0},{1,3},{3,5},... | collective-permute-start | bytes 294920 | tf_op jit(solution)/shard_map/ppermute | solution.py:411
  117.4 6.6 %collective-permute-start.9 = (bf16[128,384]{1,0:T(8,128)(2,1)}, bf16[128,384]{1,0:T(8,128)(2,1)S(1)}, u32[]{:S(2)}, u32[]{:S(2)}) collective-permute-start(bf16[128,384]{1,0:T(8,128)(2,1)} %get-tuple-element.30), channel_id=1, source_target_pairs={{0,14},{2,0},{4,2},{6,4},{8,6},{10,8},{12,10},{14,12},{1,15},{3,1}... | collective-permute-start | bytes 294920 | tf_op jit(solution)/shard_map/ppermute | solution.py:411
  124.0 2.0 %collective-permute-done.12.refs_4_ = bf16[128,384]{1,0:T(8,128)(2,1)S(1)} collective-permute-done((bf16[128,384]{1,0:T(8,128)(2,1)}, bf16[128,384]{1,0:T(8,128)(2,1)S(1)}, u32[]{:S(2)}, u32[]{:S(2)}) %collective-permute-start.12) | collective-permute-done | bytes 98336 | tf_op jit(solution)/shard_map/ppermute | solution.py:411
  126.0 2.1 %collective-permute-done.13.refs_5_ = bf16[128,384]{1,0:T(8,128)(2,1)S(1)} collective-permute-done((bf16[128,384]{1,0:T(8,128)(2,1)}, bf16[128,384]{1,0:T(8,128)(2,1)S(1)}, u32[]{:S(2)}, u32[]{:S(2)}) %collective-permute-start.13) | collective-permute-done | bytes 98336 | tf_op jit(solution)/shard_map/ppermute | solution.py:411
  128.1 0.9 collective-permute-done.9.refs_1_
  129.1 0.6 copy-done.8
  129.7 0.3 copy-done
  130.0 3.9 %home.1 = bf16[16,128,384]{2,1,0:T(8,128)(2,1)} custom-call(s32[2]{0:T(128)} %pad_add_fusion.info_ref, bf16[8,128,384]{2,1,0:T(8,128)(2,1)} %copy-done, bf16[128,384]{1,0:T(8,128)(2,1)} %get-tuple-element.29.refs_0_, bf16[128,384]{1,0:T(8,128)(2,1)} %copy-done.8, bf16[128,384]{1,0:T(8,128)(2,1)} %copy-done.2, bf16[128,384]{1,0:T(8,128)(2,1)} %copy-done.3, ...), custom_call_target="tpu_custom_call" | custom-call | tf_op jit(solution)/shard_map/home/pallas_call | solution.py:387
  (29 shorter events, 0.1 us)
Async XLA Ops:
  1.6 2.8 %collective-permute-start = (bf16[8,128,384]{2,1,0:T(8,128)(2,1)S(1)}, bf16[8,128,384]{2,1,0:T(8,128)(2,1)S(1)}, u32[]{:S(2)}, u32[]{:S(2)}) collective-permute-start(bf16[8,128,384]{2,1,0:T(8,128)(2,1)S(1)} %get-tuple-element.38), channel_id=1, source_target_pairs={{0,1},{1,0},{2,3},{3,2},{4,5},{5,4},{6,7},{7,6},{8,9},{9,8},{10,11... | collective-permute-start | bytes 2359304 | tf_op jit(solution)/shard_map/ppermute | solution.py:406
  2.1 25.8 %collective-permute-start.1 = (bf16[8,128,384]{2,1,0:T(8,128)(2,1)S(1)}, bf16[8,128,384]{2,1,0:T(8,128)(2,1)}, u32[]{:S(2)}, u32[]{:S(2)}) collective-permute-start(bf16[8,128,384]{2,1,0:T(8,128)(2,1)S(1)} %get-tuple-element.37), channel_id=1, source_target_pairs={{0,1},{1,0},{2,3},{3,2},{4,5},{5,4},{6,7},{7,6},{8,9},{9,8},{10,11... | collective-permute-start | bytes 2359304 | tf_op jit(solution)/shard_map/ppermute | solution.py:406
  4.3 0.9 copy-start.9
  20.7 40.3 %all-to-all-start = ((bf16[8,128,384]{2,1,0:T(8,128)(2,1)}), bf16[8,128,384]{2,1,0:T(8,128)(2,1)S(1)}, u32[]{:S(2)}, u32[]{:S(2)}) async-start(bf16[8,128,384]{2,1,0:T(8,128)(2,1)} %time_part.2.after_ref), calls=%async_computation | async-start | bytes 1572864 | tf_op jit(solution)/shard_map/all_to_all | solution.py:402
  43.6 9.7 %collective-permute-start.2 = (bf16[128,384]{1,0:T(8,128)(2,1)}, bf16[128,384]{1,0:T(8,128)(2,1)S(1)}, u32[]{:S(2)}, u32[]{:S(2)}) collective-permute-start(bf16[128,384]{1,0:T(8,128)(2,1)} %get-tuple-element.22), channel_id=1, source_target_pairs={{0,2},{2,4},{4,6},{6,8},{8,10},{10,12},{12,14},{14,0},{1,3},{3,5},... | collective-permute-start | bytes 294920 | tf_op jit(solution)/shard_map/ppermute | solution.py:411
  45.7 9.1 %collective-permute-start.3 = (bf16[128,384]{1,0:T(8,128)(2,1)}, bf16[128,384]{1,0:T(8,128)(2,1)S(1)}, u32[]{:S(2)}, u32[]{:S(2)}) collective-permute-start(bf16[128,384]{1,0:T(8,128)(2,1)} %get-tuple-element.23), channel_id=1, source_target_pairs={{0,4},{2,6},{4,8},{6,10},{8,12},{10,14},{12,0},{14,2},{1,5},{3,7},... | collective-permute-start | bytes 294920 | tf_op jit(solution)/shard_map/ppermute | solution.py:411
  47.2 12.8 %collective-permute-start.4 = (bf16[128,384]{1,0:T(8,128)(2,1)}, bf16[128,384]{1,0:T(8,128)(2,1)S(1)}, u32[]{:S(2)}, u32[]{:S(2)}) collective-permute-start(bf16[128,384]{1,0:T(8,128)(2,1)} %get-tuple-element.24), channel_id=1, source_target_pairs={{0,6},{2,8},{4,10},{6,12},{8,14},{10,0},{12,2},{14,4},{1,7},{3,9},... | collective-permute-start | bytes 294920 | tf_op jit(solution)/shard_map/ppermute | solution.py:411
  49.5 11.4 %collective-permute-start.5 = (bf16[128,384]{1,0:T(8,128)(2,1)}, bf16[128,384]{1,0:T(8,128)(2,1)S(1)}, u32[]{:S(2)}, u32[]{:S(2)}) collective-permute-start(bf16[128,384]{1,0:T(8,128)(2,1)} %get-tuple-element.25), channel_id=1, source_target_pairs={{0,8},{2,10},{4,12},{6,14},{8,0},{10,2},{12,4},{14,6},{1,9},{3,11}... | collective-permute-start | bytes 294920 | tf_op jit(solution)/shard_map/ppermute | solution.py:411
  51.0 10.0 %collective-permute-start.6 = (bf16[128,384]{1,0:T(8,128)(2,1)}, bf16[128,384]{1,0:T(8,128)(2,1)S(1)}, u32[]{:S(2)}, u32[]{:S(2)}) collective-permute-start(bf16[128,384]{1,0:T(8,128)(2,1)} %get-tuple-element.26), channel_id=1, source_target_pairs={{0,10},{2,12},{4,14},{6,0},{8,2},{10,4},{12,6},{14,8},{1,11},{3,13... | collective-permute-start | bytes 294920 | tf_op jit(solution)/shard_map/ppermute | solution.py:411
  53.4 7.7 %copy-start.10 = (bf16[128,384]{1,0:T(8,128)(2,1)}, bf16[128,384]{1,0:T(8,128)(2,1)S(1)}, u32[]{:S(2)}) copy-start(bf16[128,384]{1,0:T(8,128)(2,1)S(1)} %collective-permute-done.2.refs_1_) | copy-start | bytes 294916
  53.4 7.6 %collective-permute-start.7 = (bf16[128,384]{1,0:T(8,128)(2,1)}, bf16[128,384]{1,0:T(8,128)(2,1)S(1)}, u32[]{:S(2)}, u32[]{:S(2)}) collective-permute-start(bf16[128,384]{1,0:T(8,128)(2,1)} %get-tuple-element.27), channel_id=1, source_target_pairs={{0,12},{2,14},{4,0},{6,2},{8,4},{10,6},{12,8},{14,10},{1,13},{3,15... | collective-permute-start | bytes 294920 | tf_op jit(solution)/shard_map/ppermute | solution.py:411
  54.8 6.2 %copy-start.11 = (bf16[128,384]{1,0:T(8,128)(2,1)}, bf16[128,384]{1,0:T(8,128)(2,1)S(1)}, u32[]{:S(2)}) copy-start(bf16[128,384]{1,0:T(8,128)(2,1)S(1)} %collective-permute-done.3.refs_2_) | copy-start | bytes 294916
  54.8 6.1 %collective-permute-start.8 = (bf16[128,384]{1,0:T(8,128)(2,1)}, bf16[128,384]{1,0:T(8,128)(2,1)S(1)}, u32[]{:S(2)}, u32[]{:S(2)}) collective-permute-start(bf16[128,384]{1,0:T(8,128)(2,1)} %get-tuple-element.28), channel_id=1, source_target_pairs={{0,14},{2,0},{4,2},{6,4},{8,6},{10,8},{12,10},{14,12},{1,15},{3,1}... | collective-permute-start | bytes 294920 | tf_op jit(solution)/shard_map/ppermute | solution.py:411
  59.9 1.1 copy-start.12
  60.9 0.6 copy-start.13
  61.0 0.7 copy-start.14
  61.0 0.7 copy-start.15
  61.0 0.7 copy-start.16
  61.0 1.0 copy-start.1
  79.6 49.5 %all-to-all-start.1 = ((bf16[8,128,384]{2,1,0:T(8,128)(2,1)}), bf16[8,128,384]{2,1,0:T(8,128)(2,1)S(1)}, u32[]{:S(2)}, u32[]{:S(2)}) async-start(bf16[8,128,384]{2,1,0:T(8,128)(2,1)} %frames_part.2), calls=%async_computation.1 | async-start | bytes 1572864 | tf_op jit(solution)/shard_map/all_to_all | solution.py:402
  107.1 8.8 %collective-permute-start.10 = (bf16[128,384]{1,0:T(8,128)(2,1)}, bf16[128,384]{1,0:T(8,128)(2,1)S(1)}, u32[]{:S(2)}, u32[]{:S(2)}) collective-permute-start(bf16[128,384]{1,0:T(8,128)(2,1)} %get-tuple-element.31), channel_id=1, source_target_pairs={{0,12},{2,14},{4,0},{6,2},{8,4},{10,6},{12,8},{14,10},{1,13},{3,15... | collective-permute-start | bytes 294920 | tf_op jit(solution)/shard_map/ppermute | solution.py:411
  110.9 6.4 %collective-permute-start.11 = (bf16[128,384]{1,0:T(8,128)(2,1)}, bf16[128,384]{1,0:T(8,128)(2,1)S(1)}, u32[]{:S(2)}, u32[]{:S(2)}) collective-permute-start(bf16[128,384]{1,0:T(8,128)(2,1)} %get-tuple-element.32), channel_id=1, source_target_pairs={{0,10},{2,12},{4,14},{6,0},{8,2},{10,4},{12,6},{14,8},{1,11},{3,13... | collective-permute-start | bytes 294920 | tf_op jit(solution)/shard_map/ppermute | solution.py:411
  111.5 14.4 %collective-permute-start.12 = (bf16[128,384]{1,0:T(8,128)(2,1)}, bf16[128,384]{1,0:T(8,128)(2,1)S(1)}, u32[]{:S(2)}, u32[]{:S(2)}) collective-permute-start(bf16[128,384]{1,0:T(8,128)(2,1)} %get-tuple-element.33), channel_id=1, source_target_pairs={{0,8},{2,10},{4,12},{6,14},{8,0},{10,2},{12,4},{14,6},{1,9},{3,11}... | collective-permute-start | bytes 294920 | tf_op jit(solution)/shard_map/ppermute | solution.py:411
  114.8 13.3 %collective-permute-start.13 = (bf16[128,384]{1,0:T(8,128)(2,1)}, bf16[128,384]{1,0:T(8,128)(2,1)S(1)}, u32[]{:S(2)}, u32[]{:S(2)}) collective-permute-start(bf16[128,384]{1,0:T(8,128)(2,1)} %get-tuple-element.34), channel_id=1, source_target_pairs={{0,6},{2,8},{4,10},{6,12},{8,14},{10,0},{12,2},{14,4},{1,7},{3,9},... | collective-permute-start | bytes 294920 | tf_op jit(solution)/shard_map/ppermute | solution.py:411
  114.8 13.3 %collective-permute-start.14 = (bf16[128,384]{1,0:T(8,128)(2,1)}, bf16[128,384]{1,0:T(8,128)(2,1)S(1)}, u32[]{:S(2)}, u32[]{:S(2)}) collective-permute-start(bf16[128,384]{1,0:T(8,128)(2,1)} %get-tuple-element.35), channel_id=1, source_target_pairs={{0,4},{2,6},{4,8},{6,10},{8,12},{10,14},{12,0},{14,2},{1,5},{3,7},... | collective-permute-start | bytes 294920 | tf_op jit(solution)/shard_map/ppermute | solution.py:411
  115.9 13.2 %copy-start.2 = (bf16[128,384]{1,0:T(8,128)(2,1)}, bf16[128,384]{1,0:T(8,128)(2,1)S(1)}, u32[]{:S(2)}) copy-start(bf16[128,384]{1,0:T(8,128)(2,1)S(1)} %collective-permute-done.10.refs_2_) | copy-start | bytes 294916
  115.9 12.2 %collective-permute-start.15 = (bf16[128,384]{1,0:T(8,128)(2,1)}, bf16[128,384]{1,0:T(8,128)(2,1)S(1)}, u32[]{:S(2)}, u32[]{:S(2)}) collective-permute-start(bf16[128,384]{1,0:T(8,128)(2,1)} %get-tuple-element.36), channel_id=1, source_target_pairs={{0,2},{2,4},{4,6},{6,8},{8,10},{10,12},{12,14},{14,0},{1,3},{3,5},... | collective-permute-start | bytes 294920 | tf_op jit(solution)/shard_map/ppermute | solution.py:411
  117.4 11.7 %copy-start.3 = (bf16[128,384]{1,0:T(8,128)(2,1)}, bf16[128,384]{1,0:T(8,128)(2,1)S(1)}, u32[]{:S(2)}) copy-start(bf16[128,384]{1,0:T(8,128)(2,1)S(1)} %collective-permute-done.11.refs_3_) | copy-start | bytes 294916
  117.4 11.7 %collective-permute-start.9 = (bf16[128,384]{1,0:T(8,128)(2,1)}, bf16[128,384]{1,0:T(8,128)(2,1)S(1)}, u32[]{:S(2)}, u32[]{:S(2)}) collective-permute-start(bf16[128,384]{1,0:T(8,128)(2,1)} %get-tuple-element.30), channel_id=1, source_target_pairs={{0,14},{2,0},{4,2},{6,4},{8,6},{10,8},{12,10},{14,12},{1,15},{3,1}... | collective-permute-start | bytes 294920 | tf_op jit(solution)/shard_map/ppermute | solution.py:411
  125.9 3.1 %copy-start.4 = (bf16[128,384]{1,0:T(8,128)(2,1)}, bf16[128,384]{1,0:T(8,128)(2,1)S(1)}, u32[]{:S(2)}) copy-start(bf16[128,384]{1,0:T(8,128)(2,1)S(1)} %collective-permute-done.12.refs_4_) | copy-start | bytes 294916
  128.1 1.0 copy-start.5
  128.1 1.0 copy-start.6
  128.1 1.0 copy-start.7
  129.0 0.6 copy-start.8
  129.1 0.9 copy-start
where the time goes:
time: 134 us
  Pallas kernels  70.4 us (53%)
  starting transfers between devices  47.2 us (35%)
  waiting for transfers between devices  11.2 us (8%)
  local copies, waits for them, and re-layouts  4.27 us (3%)
    pallas_call x2, Pallas kernels, frames_part(): pl.pallas_call(functools.partial(frames_kernel, spots, begin, frames, blo...  35.2 us
    pallas_call x2, Pallas kernels, time_part(): pl.pallas_call(kernel, out_shape=[jax.ShapeDtypeStruct(s, BF) for s in sh...  31.2 us
    ppermute x14, starting transfers between devices, shift(): lax.ppermute(xs[k], 'tracks', [(i, (i + sign * k) % spots) for i in range...  29.5 us
    all_to_all x2, starting transfers between devices, exchange(): return lax.all_to_all(x, 'tracks', split_axis=0, concat_axis=0, tiled=True)  17.1 us
    ppermute x14, waiting for transfers between devices, shift(): lax.ppermute(xs[k], 'tracks', [(i, (i + sign * k) % spots) for i in range...  9.7 us
    pallas_call x1, Pallas kernels, home(): pl.pallas_call(functools.partial(home_kernel, spots), out_shape=jax.Shape...  3.92 us
    unnamed x34, local copies, waits for them, and re-layouts  2.7 us
  transfers between devices with their start and end apart: 18, of which 6 were waited for; matrix products, arithmetic and copies ran while one was open for 0% of the time, Pallas kernels for 36%

commit v1 on v0

--- a/solution.py
+++ b/solution.py
@@ -60,10 +60,6 @@
     def heads(self, rows, w):
         lane = iota(rows, self.width, 1)
         return [jnp.where(within(lane, self.first[w] + h * self.head, self.head), 1.0, 0.0).astype(BF) for h in range(HALF)]
-
-    def sum_lanes(self, rows, w):
-        lane = iota(rows, self.width, 1)
-        return [jnp.where(within(lane, self.sums[w] + 16 * h, 16), 1.0, 0.0).astype(BF) for h in range(HALF)]
 
     def with_ones(self, v, w):
         lane = iota(v.shape[0], self.width, 1)
@@ -123,7 +119,7 @@
         mixed.append(lanes.divide(*pair))
     middle = own + dot(jnp.concatenate(mixed, axis=0), out_w_ref[...])
     hidden = gelu(dot(normed(middle).astype(BF), expand_ref[...])).astype(BF)
-    return (middle + dot(hidden, shrink_ref[...])).astype(BF)
+    return middle + dot(hidden, shrink_ref[...])
 
 
 def usable_columns(core, first, seen):
@@ -136,7 +132,7 @@
     return jnp.transpose(jnp.broadcast_to(use, (128, length)), (1, 0))
 
 
-def time_kernel(tps, begin, info_ref, first_ref, visible_ref, own_ref, other_ref, *refs):
+def time_kernel(tps, begin, form, info_ref, first_ref, visible_ref, own_ref, other_ref, *refs):
     weights, outs, kept_ref = refs[:4], refs[4:-1], refs[-1]
     half, d = own_ref.shape[1:]
     step = pl.program_id(0)
@@ -147,43 +143,45 @@
     own = own_ref[...].reshape(tps * half, d).astype(F32)
     other = other_ref[...].reshape(tps * half, d).astype(F32)
     settled = settle(own, other, usable, *weights)
-    if len(outs[0].shape) == 3 and len(outs) == 1 and outs[0].shape[1] == half:
-        outs[0][...] = settled.reshape(tps, half, d)
+    if form == "tracks":
+        outs[0][...] = settled.astype(BF).reshape(tps, half, d)
         return
-    pieces = len(outs) > 1
-    spots = len(outs) if pieces else outs[0].shape[0]
+    spots = outs[0].shape[0]
     rows = half // spots
-    if not pieces:
-        for t in range(spots):
-            for i in range(tps):
-                at = i * half + t * rows
-                outs[0][t, i * rows : (i + 1) * rows, :] = settled[at : at + rows]
+    last = outs[0].shape[1] // tps
+    first = rows - last
+    for t in range(spots):
+        at = [i * half + t * rows + first for i in range(tps)]
+        outs[0][t] = jnp.concatenate([settled[a : a + last] for a in at], axis=0).astype(BF)
+    if form == "dense":
         return
     kept_ref[...] = settled
     for k in range(spots):
         t = lax.rem(info_ref[1] + k, spots)
-        for i in range(tps):
-            at = pl.multiple_of(i * half + t * rows, rows)
-            outs[k][i * rows : (i + 1) * rows, :] = kept_ref[pl.ds(at, rows), :]
+        at = [pl.multiple_of(i * half + t * rows, 8) for i in range(tps)]
+        outs[1 + k][...] = jnp.concatenate([kept_ref[pl.ds(a, first), :] for a in at], axis=0).astype(BF)
 
 
 def full(shape):
     return pl.BlockSpec(shape, lambda *_: (0,) * len(shape))
 
 
-def time_part(tokens, other, first_frame, visible, info, weights, spots, form, begin, count, after):
+def time_part(tokens, other, first_frame, visible, info, weights, spots, form, first, begin, count, after):
     _, half, d = tokens.shape
     rows = half // spots
-    tps = 2
+    tps = 4
     if form == "tracks":
         shapes, blocks = [(count, half, d)], [pl.BlockSpec((tps, half, d), lambda i, *_: (i, 0, 0))]
-    elif form == "dense":
-        shapes, blocks = [(spots, count * rows, d)], [pl.BlockSpec((spots, tps * rows, d), lambda i, *_: (0, i, 0))]
     else:
-        shapes, blocks = [(count * rows, d)] * spots, [pl.BlockSpec((tps * rows, d), lambda i, *_: (i, 0))] * spots
+        last = rows - first
+        shapes = [(spots, count * last, d)]
+        blocks = [pl.BlockSpec((spots, tps * last, d), lambda i, *_: (0, i, 0))]
+    if form == "split":
+        shapes += [(count * first, d)] * spots
+        blocks += [pl.BlockSpec((tps * first, d), lambda i, *_: (i, 0))] * spots
     total = count * half
     block = pl.BlockSpec((tps, half, d), lambda i, *_: (i, 0, 0))
-    kernel = functools.partial(time_kernel, tps, begin)
+    kernel = functools.partial(time_kernel, tps, begin, form)
     extra = [] if after is None else [after]
     if extra:
         inner = kernel
@@ -201,7 +199,7 @@
             + [full(visible.shape), pl.BlockSpec((tps, half, d), lambda i, *_: (begin // tps + i, 0, 0)), block]
             + [full(w.shape) for w in weights],
             out_specs=blocks,
-            scratch_shapes=[pltpu.VMEM((tps * half, d), BF)],
+            scratch_shapes=[pltpu.VMEM((tps * half, d), F32)],
         ),
         compiler_params=pltpu.CompilerParams(vmem_limit_bytes=VMEM),
         cost_estimate=pl.CostEstimate(flops=total * 5_000_000, bytes_accessed=total * d * 4, transcendentals=total * 3600),
@@ -223,18 +221,17 @@
         self.tau = lanes.head**-0.5
         vq = normed(dot(normed(self.init).astype(BF), cq_ref[...]), self.tau).astype(BF)
         self.masks = [lanes.heads(self.virt, w) for w in range(2)]
-        self.sums = [lanes.sum_lanes(self.virt, w) for w in range(2)]
         self.stacked = [
             jnp.concatenate([lanes.cut(vq, w) * m for m in self.masks[w]], axis=0) for w in range(2)
         ]
 
-    def attend(self, query, key, value):
+    def attend(self, query, key, value, masks):
         lanes, pair = self.lanes, []
         for w in range(2):
-            k, v = lanes.cut(key, w), lanes.cut(value, w)
-            ks = jnp.concatenate([k * m for m in self.masks[w]], axis=0)
-            vs = jnp.concatenate([v * m + s for m, s in zip(self.masks[w], self.sums[w])], axis=0)
-            pair.append(dot(jnp.exp(dot_t(lanes.cut(query, w), ks)).astype(BF), vs))
+            q = lanes.cut(query, w)
+            q = jnp.concatenate([q * m for m in masks[w]], axis=0)
+            p = jnp.exp(dot_t(q, lanes.cut(key, w))).astype(BF)
+            pair.append(lanes.choose(dot(p, value[w]), query.shape[0], w))
         return pair
 
     def divide(self, pairs):
@@ -261,15 +258,19 @@
         selfed = dot(normed(virtual).astype(BF), self.sqkv[...])
         query = normed(selfed[:, :d], self.tau).astype(BF)
         key = normed(selfed[:, d : 2 * d]).astype(BF)
-        value = selfed[:, 2 * d :].astype(BF)
+        value = [lanes.with_ones(selfed[:, 2 * d :], w).astype(BF) for w in range(2)]
         at = [slice(f * virt, (f + 1) * virt) for f in range(frames)]
-        mixed = self.divide([self.attend(query[r], key[r], value[r]) for r in at])
+        mixed = self.divide([self.attend(query[r], key[r], [v[r] for v in value], self.masks) for r in at])
         virtual = virtual + dot(mixed, self.so[...])
         backed = dot(normed(virtual).astype(BF), self.bkv[...])
         key = normed(backed[:, :d]).astype(BF)
-        value = backed[:, d:].astype(BF)
+        value = [lanes.with_ones(backed[:, d:], w).astype(BF) for w in range(2)]
+        masks = [lanes.heads(tracks, w) for w in range(2)]
         mixed = self.divide(
-            [self.attend(track_query[f * tracks : (f + 1) * tracks], key[r], value[r]) for f, r in enumerate(at)]
+            [
+                self.attend(track_query[f * tracks : (f + 1) * tracks], key[r], [v[r] for v in value], masks)
+                for f, r in enumerate(at)
+            ]
         )
         return (settled + dot(mixed, self.bo[...])).astype(BF)
 
@@ -313,47 +314,49 @@
     )(x, *weights)
 
 
-def frames_kernel(spots, begin, frames, block, pieces, info_ref, dense_ref, *refs):
-    xs, weights = refs[:spots], refs[spots : spots + 9]
-    outs, rows_ref = refs[spots + 9 : -1], refs[-1]
-    depth = dense_ref.shape[1] + xs[0].shape[0]
-    span = pieces
-    both = depth // span
+def frames_kernel(spots, n_out, spans, begins, frames, block, info_ref, dense_ref, *refs):
+    n = len(refs) - 10 - n_out
+    xs, weights, outs, rows_ref = refs[:n], refs[n : n + 9], refs[n + 9 : -1], refs[-1]
+    counts = (dense_ref.shape[1] // spans[0], xs[0].shape[-2] // spans[1])
+    both = sum(counts)
     tracks = spots * both
-    pick = gather_matrix(frames * both, depth, lambda r: (r % both) * span + begin + r // both)
+    depth = counts[0] * spans[0] + counts[1] * spans[1]
+
+    def source(r):
+        f, track = r // both, r % both
+        rest = counts[0] * spans[0] + (track - counts[0]) * spans[1] + begins[1] + f
+        return jnp.where(track < counts[0], track * spans[0] + begins[0] + f, rest)
+
+    pick = gather_matrix(frames * both, depth, source)
     for k in range(spots):
-        rows = jnp.concatenate([dense_ref[lax.rem(info_ref[1] + spots - k, spots)], xs[k][...]], axis=0)
+        back = lax.rem(info_ref[1] + spots - k, spots)
+        rows = jnp.concatenate([dense_ref[back], xs[k][...] if n > 1 else xs[0][back]], axis=0)
         moved = dot(pick, rows).astype(BF)
         for f in range(frames):
             rows_ref[f * tracks + k * both : f * tracks + (k + 1) * both, :] = moved[f * both : (f + 1) * both]
     server = Server(weights)
-
-    def body(b, carry):
-        at = pl.ds(pl.multiple_of(b * (block * tracks), block * tracks), block * tracks)
-        tracked = server.run(rows_ref[at, :].astype(F32), block)
+    for b in range(0, frames, block):
+        tracked = server.run(rows_ref[b * tracks : (b + block) * tracks, :].astype(F32), block)
         for f in range(block):
-            to = pl.ds(pl.multiple_of((b * block + f) * both, both), both)
+            to = slice((b + f) * both, (b + f + 1) * both)
             for k in range(spots):
                 rows = tracked[f * tracks + k * both : f * tracks + (k + 1) * both]
                 if len(outs) > 1:
                     outs[k][to, :] = rows
                 else:
                     outs[0][lax.rem(info_ref[1] + spots - k, spots), to, :] = rows
-        return carry
-
-    lax.fori_loop(0, frames // block, body, 0)
-
-
-def frames_part(dense, xs, info, span, form, begin, frames, block, weights):
+
+
+def frames_part(dense, xs, info, spans, begins, form, frames, block, weights):
     spots, _, d = dense.shape
-    both = (dense.shape[1] + xs[0].shape[0]) // span
+    both = dense.shape[1] // spans[0] + xs[0].shape[-2] // spans[1]
     if form == "dense":
         shapes = [(spots, frames * both, d)]
     else:
         shapes = [(frames * both, d)] * spots
     rows = frames * spots * both
     return pl.pallas_call(
-        functools.partial(frames_kernel, spots, begin, frames, block, span),
+        functools.partial(frames_kernel, spots, len(shapes), spans, begins, frames, block),
         out_shape=[jax.ShapeDtypeStruct(s, BF) for s in shapes],
         grid_spec=pltpu.PrefetchScalarGridSpec(
             num_scalar_prefetch=1,
@@ -393,7 +396,7 @@
             in_specs=[full(a.shape) for a in (dense, *xs)],
             out_specs=full(out),
         ),
-        compiler_params=pltpu.CompilerParams(vmem_limit_bytes=VMEM),
+        compiler_params=pltpu.CompilerParams(vmem_limit_bytes=VMEM // 2),
         name="home",
     )(info, dense, *xs)
 
@@ -416,7 +419,7 @@
     tracks, half, d = tokens.shape
     rows = half // spots
     (settled,) = time_part(
-        tokens, swap_cores(tokens), first_frame, visible, info, time_weights, spots, "tracks", 0, tracks, None
+        tokens, swap_cores(tokens), first_frame, visible, info, time_weights, spots, "tracks", 0, 0, tracks, None
     )
     settled = jnp.transpose(settled.reshape(tracks, spots, rows, d), (1, 0, 2, 3))
     tracked = rows_part(exchange(settled).reshape(-1, d), rows, virtual_weights)
@@ -427,22 +430,20 @@
 def pipelined(spots, tokens, first_frame, visible, info, time_weights, virtual_weights):
     tracks, half, d = tokens.shape
     rows = half // spots
-    n = FIRST_TRACKS
+    n, m = FIRST_TRACKS, FIRST_FRAMES
     common = (first_frame, visible, info, time_weights, spots)
-    (dense,) = time_part(tokens, swap_cores(tokens[:n]), *common, "dense", 0, n, None)
-    pieces = time_part(tokens, swap_cores(tokens[n:]), *common, "pieces", n, tracks - n, dense)
-    dense = exchange(dense)
-    pieces = shift(pieces, spots, 1)
-    m = FIRST_FRAMES
-    (first,) = frames_part(dense, pieces, info, rows, "dense", 0, m, BLOCK, virtual_weights)
-    rest = frames_part(dense, pieces, info, rows, "pieces", m, rows - m, BLOCK, virtual_weights)
+    (dense,) = time_part(tokens, swap_cores(tokens[:n]), *common, "dense", 0, 0, n, None)
+    rest, *first = time_part(tokens, swap_cores(tokens[n:]), *common, "split", m, n, tracks - n, dense)
+    dense, first, rest = exchange(dense), shift(first, spots, 1), exchange(rest)
+    (first,) = frames_part(dense, first, info, (rows, m), (0, 0), "dense", m, BLOCK, virtual_weights)
+    rest = frames_part(dense, [rest], info, (rows, rows - m), (m, 0), "pieces", rows - m, BLOCK, virtual_weights)
     return home(exchange(first), shift(rest, spots, -1), info, tracks)
 
 
 def per_device(spots, tokens, first_frame, visible, *weights):
     tracks, half, _ = tokens.shape
     rows = half // spots
-    fits = tracks % 16 == 0 and rows % 16 == 0 and FIRST_TRACKS < tracks and FIRST_FRAMES < rows
+    fits = tracks % 16 == 0 and rows % 16 == 0 and (rows - FIRST_FRAMES) % 8 == 0 and FIRST_TRACKS < tracks and FIRST_FRAMES < rows
     info = jnp.stack([lax.axis_index("frames"), lax.axis_index("tracks")]).astype(jnp.int32)
     run = pipelined if fits else simple
     return run(spots, tokens, first_frame, visible, info, weights[:4], weights[4:])
@@ -450,7 +451,7 @@
 
 FIRST_TRACKS = 8
 FIRST_FRAMES = 8
-BLOCK = 4
+BLOCK = 8
 
 
 def solution(mesh):

time: 134 us -> 119 us (0.89)
  Pallas kernels: 70.4 us -> 56.9 us
  waiting for transfers between devices: 11.2 us -> 7.03 us
  starting transfers between devices: 47.2 us -> 49.2 us
    pallas_call x2, Pallas kernels: 35.2 us -> 26.4 us  [frames_part(): pl.pallas_call(functools.partial(frames_kernel, spots, len(shapes), spans...]
    ppermute x14, waiting for transfers between devices: 9.7 us -> 3.34 us  [shift(): lax.ppermute(xs[k], 'tracks', [(i, (i + sign * k) % spots) for i in range...]
    pallas_call x2, Pallas kernels: 31.2 us -> 28.1 us  [time_part(): pl.pallas_call(kernel, out_shape=[jax.ShapeDtypeStruct(s, BF) for s in sh...]
    ppermute x14, starting transfers between devices: 29.5 us -> 32.1 us  [shift(): lax.ppermute(xs[k], 'tracks', [(i, (i + sign * k) % spots) for i in range...]
    ppermute x2, waiting for transfers between devices: 1.53 us -> 3.68 us  [swap_cores(): return lax.ppermute(x, 'frames', [(0, 1), (1, 0)])]
    pallas_call x1, Pallas kernels: 3.92 us -> 2.38 us  [home(): pl.pallas_call(functools.partial(home_kernel, spots), out_shape=jax.Shape...]
    all_to_all x2 -> x3, starting transfers between devices: 17.1 us -> 16.6 us  [exchange(): return lax.all_to_all(x, 'tracks', split_axis=0, concat_axis=0, tiled=True)]
    unnamed x34 -> x24, local copies, waits for them, and re-layouts: 2.7 us -> 2.37 us
  transfers between devices with their start and end apart: 18 -> 19, of which waited for: 6 -> 6; matrix products, arithmetic and copies ran while one was open for 0% -> 1% of each run, Pallas kernels for 36% -> 34%
where the time goes in v1:
time: 119 us; the launch traced here: 118 us
  Pallas kernels  56.9 us (48%)
  starting transfers between devices  49.2 us (41%)
  waiting for transfers between devices  7.03 us (6%)
  local copies, waits for them, and re-layouts  3.94 us (3%)
    ppermute x14, starting transfers between devices, shift(): lax.ppermute(xs[k], 'tracks', [(i, (i + sign * k) % spots) for i in range...  32.1 us
    pallas_call x2, Pallas kernels, time_part(): pl.pallas_call(kernel, out_shape=[jax.ShapeDtypeStruct(s, BF) for s in sh...  28.1 us
    pallas_call x2, Pallas kernels, frames_part(): pl.pallas_call(functools.partial(frames_kernel, spots, len(shapes), spans...  26.4 us
    all_to_all x3, starting transfers between devices, exchange(): return lax.all_to_all(x, 'tracks', split_axis=0, concat_axis=0, tiled=True)  16.6 us
    ppermute x2, waiting for transfers between devices, swap_cores(): return lax.ppermute(x, 'frames', [(0, 1), (1, 0)])  3.68 us
    ppermute x14, waiting for transfers between devices, shift(): lax.ppermute(xs[k], 'tracks', [(i, (i + sign * k) % spots) for i in range...  3.34 us
    pallas_call x1, Pallas kernels, home(): pl.pallas_call(functools.partial(home_kernel, spots), out_shape=jax.Shape...  2.38 us
  transfers between devices with their start and end apart: 19, of which 6 were waited for; matrix products, arithmetic and copies ran while one was open for 1% of the time, Pallas kernels for 34%

profile of v1, /device:TPU:0, one launch (start us, length us, event | category | flops | bytes accessed | tf_op | source)
XLA Modules:
  0.0 117.8 jit_solution(12696793472336716823)
XLA Ops:
  0.0 1.6 %fusion = (bf16[8,128,384]{2,1,0:T(8,128)(2,1)S(1)}, bf16[8,128,384]{2,1,0:T(8,128)(2,1)S(1)}) fusion(bf16[16,128,384]{2,1,0:T(8,128)(2,1)} %refs_1_.4), kind=kLoop, calls=%fused_computation.1 | loop fusion | bytes 3145728 | tf_op jit(solution)/shard_map/slice | solution.py:436
  1.6 0.5 collective-permute-start
  2.1 0.6 pad_add_fusion.info_ref
  2.7 1.3 %collective-permute-done.other_ref = bf16[8,128,384]{2,1,0:T(8,128)(2,1)S(1)} collective-permute-done((bf16[8,128,384]{2,1,0:T(8,128)(2,1)S(1)}, bf16[8,128,384]{2,1,0:T(8,128)(2,1)S(1)}, u32[]{:S(2)}, u32[]{:S(2)}) %collective-permute-start) | collective-permute-done | bytes 786464 | tf_op jit(solution)/shard_map/ppermute | solution.py:409
  4.0 0.9 copy-done.4
  4.9 14.0 %time_part.2.after_ref = bf16[8,128,384]{2,1,0:T(8,128)(2,1)} custom-call(s32[2]{0:T(128)} %pad_add_fusion.info_ref, s32[16]{0:T(128)} %first_ref.3, s32[16,256]{1,0:T(8,128)} %refs_0_.3, bf16[16,128,384]{2,1,0:T(8,128)(2,1)} %refs_1_.4, bf16[8,128,384]{2,1,0:T(8,128)(2,1)} %copy-done.4, bf16[384,1152]{1,0:T(8,128)(2,1)} %refs_3_.4, ...), custom_call_target="tpu_custom_call" | custom-call | flops 5120000000 | bytes 1572864 | tf_op jit(solution)/shard_map/time_part/pallas_call | solution.py:192
  18.9 7.2 %all-to-all-start = ((bf16[8,128,384]{2,1,0:T(8,128)(2,1)}), bf16[8,128,384]{2,1,0:T(8,128)(2,1)S(1)}, u32[]{:S(2)}, u32[]{:S(2)}) async-start(bf16[8,128,384]{2,1,0:T(8,128)(2,1)} %time_part.2.after_ref), calls=%async_computation | async-start | bytes 1572864 | tf_op jit(solution)/shard_map/all_to_all | solution.py:405
  26.1 0.0 collective-permute-start.1
  26.1 2.4 %collective-permute-done.1.refs_2_ = bf16[8,128,384]{2,1,0:T(8,128)(2,1)} collective-permute-done((bf16[8,128,384]{2,1,0:T(8,128)(2,1)S(1)}, bf16[8,128,384]{2,1,0:T(8,128)(2,1)}, u32[]{:S(2)}, u32[]{:S(2)}) %collective-permute-start.1) | collective-permute-done | bytes 786464 | tf_op jit(solution)/shard_map/ppermute | solution.py:409
  28.5 14.1 %time_part.3 = (bf16[8,64,384]{2,1,0:T(8,128)(2,1)}, bf16[64,384]{1,0:T(8,128)(2,1)}, bf16[64,384]{1,0:T(8,128)(2,1)}, bf16[64,384]{1,0:T(8,128)(2,1)}, bf16[64,...) custom-call(s32[2]{0:T(128)} %pad_add_fusion.info_ref, ...), custom_call_target="tpu_custom_call" | custom-call | flops 5120000000 | bytes 1572864 | tf_op jit(solution)/shard_map/time_part/pallas_call | solution.py:192
  42.6 2.1 %collective-permute-start.2 = (bf16[64,384]{1,0:T(8,128)(2,1)}, bf16[64,384]{1,0:T(8,128)(2,1)S(1)}, u32[]{:S(2)}, u32[]{:S(2)}) collective-permute-start(bf16[64,384]{1,0:T(8,128)(2,1)} %get-tuple-element.23), channel_id=1, source_target_pairs={{0,2},{2,4},{4,6},{6,8},{8,10},{10,12},{12,14},{14,0},{1,3},{3,5},... | collective-permute-start | bytes 147464 | tf_op jit(solution)/shard_map/ppermute | solution.py:414
  44.7 1.5 %collective-permute-start.3 = (bf16[64,384]{1,0:T(8,128)(2,1)}, bf16[64,384]{1,0:T(8,128)(2,1)S(1)}, u32[]{:S(2)}, u32[]{:S(2)}) collective-permute-start(bf16[64,384]{1,0:T(8,128)(2,1)} %get-tuple-element.24), channel_id=1, source_target_pairs={{0,4},{2,6},{4,8},{6,10},{8,12},{10,14},{12,0},{14,2},{1,5},{3,7},... | collective-permute-start | bytes 147464 | tf_op jit(solution)/shard_map/ppermute | solution.py:414
  46.1 2.4 %collective-permute-start.4 = (bf16[64,384]{1,0:T(8,128)(2,1)}, bf16[64,384]{1,0:T(8,128)(2,1)S(1)}, u32[]{:S(2)}, u32[]{:S(2)}) collective-permute-start(bf16[64,384]{1,0:T(8,128)(2,1)} %get-tuple-element.25), channel_id=1, source_target_pairs={{0,6},{2,8},{4,10},{6,12},{8,14},{10,0},{12,2},{14,4},{1,7},{3,9},... | collective-permute-start | bytes 147464 | tf_op jit(solution)/shard_map/ppermute | solution.py:414
  48.5 1.5 %collective-permute-start.5 = (bf16[64,384]{1,0:T(8,128)(2,1)}, bf16[64,384]{1,0:T(8,128)(2,1)S(1)}, u32[]{:S(2)}, u32[]{:S(2)}) collective-permute-start(bf16[64,384]{1,0:T(8,128)(2,1)} %get-tuple-element.26), channel_id=1, source_target_pairs={{0,8},{2,10},{4,12},{6,14},{8,0},{10,2},{12,4},{14,6},{1,9},{3,11}... | collective-permute-start | bytes 147464 | tf_op jit(solution)/shard_map/ppermute | solution.py:414
  50.0 2.4 %collective-permute-start.6 = (bf16[64,384]{1,0:T(8,128)(2,1)}, bf16[64,384]{1,0:T(8,128)(2,1)S(1)}, u32[]{:S(2)}, u32[]{:S(2)}) collective-permute-start(bf16[64,384]{1,0:T(8,128)(2,1)} %get-tuple-element.27), channel_id=1, source_target_pairs={{0,10},{2,12},{4,14},{6,0},{8,2},{10,4},{12,6},{14,8},{1,11},{3,13... | collective-permute-start | bytes 147464 | tf_op jit(solution)/shard_map/ppermute | solution.py:414
  52.3 0.0 collective-permute-done.2.refs_1_
  52.3 1.5 %collective-permute-start.7 = (bf16[64,384]{1,0:T(8,128)(2,1)}, bf16[64,384]{1,0:T(8,128)(2,1)S(1)}, u32[]{:S(2)}, u32[]{:S(2)}) collective-permute-start(bf16[64,384]{1,0:T(8,128)(2,1)} %get-tuple-element.28), channel_id=1, source_target_pairs={{0,12},{2,14},{4,0},{6,2},{8,4},{10,6},{12,8},{14,10},{1,13},{3,15... | collective-permute-start | bytes 147464 | tf_op jit(solution)/shard_map/ppermute | solution.py:414
  53.8 0.0 collective-permute-done.3.refs_2_
  53.8 1.5 %collective-permute-start.8 = (bf16[64,384]{1,0:T(8,128)(2,1)}, bf16[64,384]{1,0:T(8,128)(2,1)S(1)}, u32[]{:S(2)}, u32[]{:S(2)}) collective-permute-start(bf16[64,384]{1,0:T(8,128)(2,1)} %get-tuple-element.29), channel_id=1, source_target_pairs={{0,14},{2,0},{4,2},{6,4},{8,6},{10,8},{12,10},{14,12},{1,15},{3,1}... | collective-permute-start | bytes 147464 | tf_op jit(solution)/shard_map/ppermute | solution.py:414
  55.3 0.0 all-to-all-done.dense_ref
  55.3 3.6 %all-to-all-start.2 = ((bf16[8,64,384]{2,1,0:T(8,128)(2,1)}), bf16[8,64,384]{2,1,0:T(8,128)(2,1)S(1)}, u32[]{:S(2)}, u32[]{:S(2)}) async-start(bf16[8,64,384]{2,1,0:T(8,128)(2,1)} %get-tuple-element.30), calls=%async_computation.2 | async-start | bytes 786432 | tf_op jit(solution)/shard_map/all_to_all | solution.py:405
  58.9 0.0 collective-permute-done.4.refs_3_
  58.9 0.0 collective-permute-done.5.refs_4_
  58.9 0.0 collective-permute-done.6.refs_5_
  59.0 0.0 collective-permute-done.7.refs_6_
  59.0 0.5 copy-done.7
  59.5 0.0 copy-done.8
  59.6 0.0 copy-done.9
  59.6 0.0 copy-done.10
  59.6 0.0 copy-done.11
  59.6 13.2 %frames_part.2 = bf16[8,128,384]{2,1,0:T(8,128)(2,1)} custom-call(s32[2]{0:T(128)} %pad_add_fusion.info_ref, bf16[8,128,384]{2,1,0:T(8,128)(2,1)} %copy-done.2, bf16[64,384]{1,0:T(8,128)(2,1)} %get-tuple-element.22.refs_0_, bf16[64,384]{1,0:T(8,128)(2,1)} %copy-done.5, bf16[64,384]{1,0:T(8,128)(2,1)} %copy-done.6, bf16[64,384]{1,0:T(8,128)(2,1)} %copy-done.7, ...), custom_call_target="tpu_custom_call" | custom-call | flops 10240000000 | bytes 1572864 | tf_op jit(solution)/shard_map/frames_part/pallas_call | solution.py:358
  72.9 0.0 all-to-all-done.2.refs_0_
  72.9 5.7 %all-to-all-start.1 = ((bf16[8,128,384]{2,1,0:T(8,128)(2,1)}), bf16[8,128,384]{2,1,0:T(8,128)(2,1)S(1)}, u32[]{:S(2)}, u32[]{:S(2)}) async-start(bf16[8,128,384]{2,1,0:T(8,128)(2,1)} %frames_part.2), calls=%async_computation.1 | async-start | bytes 1572864 | tf_op jit(solution)/shard_map/all_to_all | solution.py:405
  78.6 13.2 %frames_part.3 = (bf16[128,384]{1,0:T(8,128)(2,1)}, bf16[128,384]{1,0:T(8,128)(2,1)}, bf16[128,384]{1,0:T(8,128)(2,1)}, bf16[128,384]{1,0:T(8,128)(2,1)}, bf16[1...) custom-call(s32[2]{0:T(128)} %pad_add_fusion.info_ref, ...), custom_call_target="tpu_custom_call" | custom-call | flops 10240000000 | bytes 1572864 | tf_op jit(solution)/shard_map/frames_part/pallas_call | solution.py:358
  91.8 4.7 %collective-permute-start.9 = (bf16[128,384]{1,0:T(8,128)(2,1)}, bf16[128,384]{1,0:T(8,128)(2,1)S(1)}, u32[]{:S(2)}, u32[]{:S(2)}) collective-permute-start(bf16[128,384]{1,0:T(8,128)(2,1)} %get-tuple-element.32), channel_id=1, source_target_pairs={{0,14},{2,0},{4,2},{6,4},{8,6},{10,8},{12,10},{14,12},{1,15},{3,1}... | collective-permute-start | bytes 294920 | tf_op jit(solution)/shard_map/ppermute | solution.py:414
  96.5 0.6 collective-permute-start.10
  97.1 0.0 collective-permute-start.11
  97.1 2.9 %collective-permute-start.12 = (bf16[128,384]{1,0:T(8,128)(2,1)}, bf16[128,384]{1,0:T(8,128)(2,1)S(1)}, u32[]{:S(2)}, u32[]{:S(2)}) collective-permute-start(bf16[128,384]{1,0:T(8,128)(2,1)} %get-tuple-element.35), channel_id=1, source_target_pairs={{0,8},{2,10},{4,12},{6,14},{8,0},{10,2},{12,4},{14,6},{1,9},{3,11}... | collective-permute-start | bytes 294920 | tf_op jit(solution)/shard_map/ppermute | solution.py:414
  100.0 0.1 collective-permute-done.9.refs_1_
  100.1 1.9 %collective-permute-start.14 = (bf16[128,384]{1,0:T(8,128)(2,1)}, bf16[128,384]{1,0:T(8,128)(2,1)S(1)}, u32[]{:S(2)}, u32[]{:S(2)}) collective-permute-start(bf16[128,384]{1,0:T(8,128)(2,1)} %get-tuple-element.37), channel_id=1, source_target_pairs={{0,4},{2,6},{4,8},{6,10},{8,12},{10,14},{12,0},{14,2},{1,5},{3,7},... | collective-permute-start | bytes 294920 | tf_op jit(solution)/shard_map/ppermute | solution.py:414
  102.0 0.4 collective-permute-done.10.refs_2_
  102.5 9.2 %collective-permute-start.15 = (bf16[128,384]{1,0:T(8,128)(2,1)}, bf16[128,384]{1,0:T(8,128)(2,1)S(1)}, u32[]{:S(2)}, u32[]{:S(2)}) collective-permute-start(bf16[128,384]{1,0:T(8,128)(2,1)} %get-tuple-element.38), channel_id=1, source_target_pairs={{0,2},{2,4},{4,6},{6,8},{8,10},{10,12},{12,14},{14,0},{1,3},{3,5},... | collective-permute-start | bytes 294920 | tf_op jit(solution)/shard_map/ppermute | solution.py:414
  111.7 2.1 %collective-permute-done.12.refs_4_ = bf16[128,384]{1,0:T(8,128)(2,1)S(1)} collective-permute-done((bf16[128,384]{1,0:T(8,128)(2,1)}, bf16[128,384]{1,0:T(8,128)(2,1)S(1)}, u32[]{:S(2)}, u32[]{:S(2)}) %collective-permute-start.12) | collective-permute-done | bytes 98336 | tf_op jit(solution)/shard_map/ppermute | solution.py:414
  113.8 0.8 collective-permute-done.13.refs_5_
  114.5 0.0 collective-permute-done.15.refs_7_
  114.6 0.0 all-to-all-done.1.dense_ref
  114.6 0.9 copy-done
  115.5 2.4 %home.1 = bf16[16,128,384]{2,1,0:T(8,128)(2,1)} custom-call(s32[2]{0:T(128)S(1)} %copy-done.1, bf16[8,128,384]{2,1,0:T(8,128)(2,1)S(1)} %all-to-all-done.1.dense_ref, bf16[128,384]{1,0:T(8,128)(2,1)S(1)} %copy-done, bf16[128,384]{1,0:T(8,128)(2,1)S(1)} %collective-permute-done.9.refs_1_, bf16[128,384]{1,0:T(8,128)(2,1)S(1)} %collective-permute-done.10.refs_2_, ...), custom_call_target="tpu_custom_call" | custom-call | tf_op jit(solution)/shard_map/home/pallas_call | solution.py:390
  (21 shorter events, 0.0 us)
Async XLA Ops:
  1.6 2.4 %collective-permute-start = (bf16[8,128,384]{2,1,0:T(8,128)(2,1)S(1)}, bf16[8,128,384]{2,1,0:T(8,128)(2,1)S(1)}, u32[]{:S(2)}, u32[]{:S(2)}) collective-permute-start(bf16[8,128,384]{2,1,0:T(8,128)(2,1)S(1)} %get-tuple-element.40), channel_id=1, source_target_pairs={{0,1},{1,0},{2,3},{3,2},{4,5},{5,4},{6,7},{7,6},{8,9},{9,8},{10,11... | collective-permute-start | bytes 2359304 | tf_op jit(solution)/shard_map/ppermute | solution.py:409
  4.0 0.9 copy-start.4
  18.9 36.4 %all-to-all-start = ((bf16[8,128,384]{2,1,0:T(8,128)(2,1)}), bf16[8,128,384]{2,1,0:T(8,128)(2,1)S(1)}, u32[]{:S(2)}, u32[]{:S(2)}) async-start(bf16[8,128,384]{2,1,0:T(8,128)(2,1)} %time_part.2.after_ref), calls=%async_computation | async-start | bytes 1572864 | tf_op jit(solution)/shard_map/all_to_all | solution.py:405
  26.1 2.4 %collective-permute-start.1 = (bf16[8,128,384]{2,1,0:T(8,128)(2,1)S(1)}, bf16[8,128,384]{2,1,0:T(8,128)(2,1)}, u32[]{:S(2)}, u32[]{:S(2)}) collective-permute-start(bf16[8,128,384]{2,1,0:T(8,128)(2,1)S(1)} %get-tuple-element.39), channel_id=1, source_target_pairs={{0,1},{1,0},{2,3},{3,2},{4,5},{5,4},{6,7},{7,6},{8,9},{9,8},{10,11... | collective-permute-start | bytes 2359304 | tf_op jit(solution)/shard_map/ppermute | solution.py:409
  42.6 9.7 %collective-permute-start.2 = (bf16[64,384]{1,0:T(8,128)(2,1)}, bf16[64,384]{1,0:T(8,128)(2,1)S(1)}, u32[]{:S(2)}, u32[]{:S(2)}) collective-permute-start(bf16[64,384]{1,0:T(8,128)(2,1)} %get-tuple-element.23), channel_id=1, source_target_pairs={{0,2},{2,4},{4,6},{6,8},{8,10},{10,12},{12,14},{14,0},{1,3},{3,5},... | collective-permute-start | bytes 147464 | tf_op jit(solution)/shard_map/ppermute | solution.py:414
  44.7 9.1 %collective-permute-start.3 = (bf16[64,384]{1,0:T(8,128)(2,1)}, bf16[64,384]{1,0:T(8,128)(2,1)S(1)}, u32[]{:S(2)}, u32[]{:S(2)}) collective-permute-start(bf16[64,384]{1,0:T(8,128)(2,1)} %get-tuple-element.24), channel_id=1, source_target_pairs={{0,4},{2,6},{4,8},{6,10},{8,12},{10,14},{12,0},{14,2},{1,5},{3,7},... | collective-permute-start | bytes 147464 | tf_op jit(solution)/shard_map/ppermute | solution.py:414
  46.1 12.8 %collective-permute-start.4 = (bf16[64,384]{1,0:T(8,128)(2,1)}, bf16[64,384]{1,0:T(8,128)(2,1)S(1)}, u32[]{:S(2)}, u32[]{:S(2)}) collective-permute-start(bf16[64,384]{1,0:T(8,128)(2,1)} %get-tuple-element.25), channel_id=1, source_target_pairs={{0,6},{2,8},{4,10},{6,12},{8,14},{10,0},{12,2},{14,4},{1,7},{3,9},... | collective-permute-start | bytes 147464 | tf_op jit(solution)/shard_map/ppermute | solution.py:414
  48.5 10.4 %collective-permute-start.5 = (bf16[64,384]{1,0:T(8,128)(2,1)}, bf16[64,384]{1,0:T(8,128)(2,1)S(1)}, u32[]{:S(2)}, u32[]{:S(2)}) collective-permute-start(bf16[64,384]{1,0:T(8,128)(2,1)} %get-tuple-element.26), channel_id=1, source_target_pairs={{0,8},{2,10},{4,12},{6,14},{8,0},{10,2},{12,4},{14,6},{1,9},{3,11}... | collective-permute-start | bytes 147464 | tf_op jit(solution)/shard_map/ppermute | solution.py:414
  50.0 9.0 %collective-permute-start.6 = (bf16[64,384]{1,0:T(8,128)(2,1)}, bf16[64,384]{1,0:T(8,128)(2,1)S(1)}, u32[]{:S(2)}, u32[]{:S(2)}) collective-permute-start(bf16[64,384]{1,0:T(8,128)(2,1)} %get-tuple-element.27), channel_id=1, source_target_pairs={{0,10},{2,12},{4,14},{6,0},{8,2},{10,4},{12,6},{14,8},{1,11},{3,13... | collective-permute-start | bytes 147464 | tf_op jit(solution)/shard_map/ppermute | solution.py:414
  52.3 6.7 %copy-start.5 = (bf16[64,384]{1,0:T(8,128)(2,1)}, bf16[64,384]{1,0:T(8,128)(2,1)S(1)}, u32[]{:S(2)}) copy-start(bf16[64,384]{1,0:T(8,128)(2,1)S(1)} %collective-permute-done.2.refs_1_) | copy-start | bytes 147460
  52.3 6.6 %collective-permute-start.7 = (bf16[64,384]{1,0:T(8,128)(2,1)}, bf16[64,384]{1,0:T(8,128)(2,1)S(1)}, u32[]{:S(2)}, u32[]{:S(2)}) collective-permute-start(bf16[64,384]{1,0:T(8,128)(2,1)} %get-tuple-element.28), channel_id=1, source_target_pairs={{0,12},{2,14},{4,0},{6,2},{8,4},{10,6},{12,8},{14,10},{1,13},{3,15... | collective-permute-start | bytes 147464 | tf_op jit(solution)/shard_map/ppermute | solution.py:414
  53.8 5.2 %copy-start.6 = (bf16[64,384]{1,0:T(8,128)(2,1)}, bf16[64,384]{1,0:T(8,128)(2,1)S(1)}, u32[]{:S(2)}) copy-start(bf16[64,384]{1,0:T(8,128)(2,1)S(1)} %collective-permute-done.3.refs_2_) | copy-start | bytes 147460
  53.8 5.2 %collective-permute-start.8 = (bf16[64,384]{1,0:T(8,128)(2,1)}, bf16[64,384]{1,0:T(8,128)(2,1)S(1)}, u32[]{:S(2)}, u32[]{:S(2)}) collective-permute-start(bf16[64,384]{1,0:T(8,128)(2,1)} %get-tuple-element.29), channel_id=1, source_target_pairs={{0,14},{2,0},{4,2},{6,4},{8,6},{10,8},{12,10},{14,12},{1,15},{3,1}... | collective-permute-start | bytes 147464 | tf_op jit(solution)/shard_map/ppermute | solution.py:414
  55.3 3.8 %copy-start.2 = (bf16[8,128,384]{2,1,0:T(8,128)(2,1)}, bf16[8,128,384]{2,1,0:T(8,128)(2,1)S(1)}, u32[]{:S(2)}) copy-start(bf16[8,128,384]{2,1,0:T(8,128)(2,1)S(1)} %all-to-all-done.dense_ref) | copy-start | bytes 2359300
  55.3 17.6 %all-to-all-start.2 = ((bf16[8,64,384]{2,1,0:T(8,128)(2,1)}), bf16[8,64,384]{2,1,0:T(8,128)(2,1)S(1)}, u32[]{:S(2)}, u32[]{:S(2)}) async-start(bf16[8,64,384]{2,1,0:T(8,128)(2,1)} %get-tuple-element.30), calls=%async_computation.2 | async-start | bytes 786432 | tf_op jit(solution)/shard_map/all_to_all | solution.py:405
  58.9 0.6 copy-start.7
  58.9 0.6 copy-start.8
  59.0 0.6 copy-start.9
  59.0 0.6 copy-start.10
  59.0 0.6 copy-start.11
  72.9 5.8 %copy-start.3 = (bf16[8,64,384]{2,1,0:T(8,128)(2,1)}, bf16[8,64,384]{2,1,0:T(8,128)(2,1)S(1)}, u32[]{:S(2)}) copy-start(bf16[8,64,384]{2,1,0:T(8,128)(2,1)S(1)} %all-to-all-done.2.refs_0_) | copy-start | bytes 1179652
  72.9 41.7 %all-to-all-start.1 = ((bf16[8,128,384]{2,1,0:T(8,128)(2,1)}), bf16[8,128,384]{2,1,0:T(8,128)(2,1)S(1)}, u32[]{:S(2)}, u32[]{:S(2)}) async-start(bf16[8,128,384]{2,1,0:T(8,128)(2,1)} %frames_part.2), calls=%async_computation.1 | async-start | bytes 1572864 | tf_op jit(solution)/shard_map/all_to_all | solution.py:405
  78.6 35.9 %copy-start.1 = (s32[2]{0:T(128)S(1)}, s32[2]{0:T(128)}, u32[]{:S(2)}) copy-start(s32[2]{0:T(128)} %pad_add_fusion.info_ref) | copy-start | bytes 28
  91.8 8.3 %collective-permute-start.9 = (bf16[128,384]{1,0:T(8,128)(2,1)}, bf16[128,384]{1,0:T(8,128)(2,1)S(1)}, u32[]{:S(2)}, u32[]{:S(2)}) collective-permute-start(bf16[128,384]{1,0:T(8,128)(2,1)} %get-tuple-element.32), channel_id=1, source_target_pairs={{0,14},{2,0},{4,2},{6,4},{8,6},{10,8},{12,10},{14,12},{1,15},{3,1}... | collective-permute-start | bytes 294920 | tf_op jit(solution)/shard_map/ppermute | solution.py:414
  96.5 5.9 %collective-permute-start.10 = (bf16[128,384]{1,0:T(8,128)(2,1)}, bf16[128,384]{1,0:T(8,128)(2,1)S(1)}, u32[]{:S(2)}, u32[]{:S(2)}) collective-permute-start(bf16[128,384]{1,0:T(8,128)(2,1)} %get-tuple-element.33), channel_id=1, source_target_pairs={{0,12},{2,14},{4,0},{6,2},{8,4},{10,6},{12,8},{14,10},{1,13},{3,15... | collective-permute-start | bytes 294920 | tf_op jit(solution)/shard_map/ppermute | solution.py:414
  97.1 14.6 %collective-permute-start.11 = (bf16[128,384]{1,0:T(8,128)(2,1)}, bf16[128,384]{1,0:T(8,128)(2,1)S(1)}, u32[]{:S(2)}, u32[]{:S(2)}) collective-permute-start(bf16[128,384]{1,0:T(8,128)(2,1)} %get-tuple-element.34), channel_id=1, source_target_pairs={{0,10},{2,12},{4,14},{6,0},{8,2},{10,4},{12,6},{14,8},{1,11},{3,13... | collective-permute-start | bytes 294920 | tf_op jit(solution)/shard_map/ppermute | solution.py:414
  97.1 16.7 %collective-permute-start.12 = (bf16[128,384]{1,0:T(8,128)(2,1)}, bf16[128,384]{1,0:T(8,128)(2,1)S(1)}, u32[]{:S(2)}, u32[]{:S(2)}) collective-permute-start(bf16[128,384]{1,0:T(8,128)(2,1)} %get-tuple-element.35), channel_id=1, source_target_pairs={{0,8},{2,10},{4,12},{6,14},{8,0},{10,2},{12,4},{14,6},{1,9},{3,11}... | collective-permute-start | bytes 294920 | tf_op jit(solution)/shard_map/ppermute | solution.py:414
  100.0 14.5 %collective-permute-start.13 = (bf16[128,384]{1,0:T(8,128)(2,1)}, bf16[128,384]{1,0:T(8,128)(2,1)S(1)}, u32[]{:S(2)}, u32[]{:S(2)}) collective-permute-start(bf16[128,384]{1,0:T(8,128)(2,1)} %get-tuple-element.36), channel_id=1, source_target_pairs={{0,6},{2,8},{4,10},{6,12},{8,14},{10,0},{12,2},{14,4},{1,7},{3,9},... | collective-permute-start | bytes 294920 | tf_op jit(solution)/shard_map/ppermute | solution.py:414
  100.1 14.4 %collective-permute-start.14 = (bf16[128,384]{1,0:T(8,128)(2,1)}, bf16[128,384]{1,0:T(8,128)(2,1)S(1)}, u32[]{:S(2)}, u32[]{:S(2)}) collective-permute-start(bf16[128,384]{1,0:T(8,128)(2,1)} %get-tuple-element.37), channel_id=1, source_target_pairs={{0,4},{2,6},{4,8},{6,10},{8,12},{10,14},{12,0},{14,2},{1,5},{3,7},... | collective-permute-start | bytes 294920 | tf_op jit(solution)/shard_map/ppermute | solution.py:414
  102.5 12.1 %collective-permute-start.15 = (bf16[128,384]{1,0:T(8,128)(2,1)}, bf16[128,384]{1,0:T(8,128)(2,1)S(1)}, u32[]{:S(2)}, u32[]{:S(2)}) collective-permute-start(bf16[128,384]{1,0:T(8,128)(2,1)} %get-tuple-element.38), channel_id=1, source_target_pairs={{0,2},{2,4},{4,6},{6,8},{8,10},{10,12},{12,14},{14,0},{1,3},{3,5},... | collective-permute-start | bytes 294920 | tf_op jit(solution)/shard_map/ppermute | solution.py:414
  114.6 0.9 copy-start

commit v2 on v1

--- a/solution.py
+++ b/solution.py
@@ -103,20 +103,29 @@
     value = both[:, d:]
     masks = [lanes.heads(half, w) for w in range(2)]
     mixed = []
-    for i in range(tracks):
+    def scored(i, w):
         mine = slice(i * half, (i + 1) * half)
         away = slice((tracks + i) * half, (tracks + i + 1) * half)
         k = jnp.concatenate([key[mine], key[away]], axis=0)
+        q = lanes.cut(query[mine], w)
+        return dot_t(jnp.concatenate([q * m for m in masks[w]], axis=0), lanes.cut(k, w))
+
+    todo = [(i, w) for i in range(tracks) for w in range(2)]
+    scores = [scored(*todo[0])]
+    pair = []
+    for at, (i, w) in enumerate(todo):
+        if at + 1 < len(todo):
+            scores.append(scored(*todo[at + 1]))
+        mine = slice(i * half, (i + 1) * half)
+        away = slice((tracks + i) * half, (tracks + i + 1) * half)
         v = jnp.concatenate([value[mine], value[away]], axis=0)
-        pair = []
-        for w in range(2):
-            q = lanes.cut(query[mine], w)
-            scores = dot_t(jnp.concatenate([q * m for m in masks[w]], axis=0), lanes.cut(k, w))
-            weights = jnp.exp(scores).astype(BF)
-            use = jnp.concatenate([usable[i]] * (lanes.width // 128), axis=1)
-            o = dot(weights, (lanes.with_ones(v, w) * use).astype(BF))
-            pair.append(lanes.choose(o, half, w))
-        mixed.append(lanes.divide(*pair))
+        weights = jnp.exp(scores[at]).astype(BF)
+        use = jnp.concatenate([usable[i]] * (lanes.width // 128), axis=1)
+        o = dot(weights, (lanes.with_ones(v, w) * use).astype(BF))
+        pair.append(lanes.choose(o, half, w))
+        if w == 1:
+            mixed.append(lanes.divide(*pair))
+            pair = []
     middle = own + dot(jnp.concatenate(mixed, axis=0), out_w_ref[...])
     hidden = gelu(dot(normed(middle).astype(BF), expand_ref[...])).astype(BF)
     return middle + dot(hidden, shrink_ref[...])
@@ -180,7 +189,7 @@
         shapes += [(count * first, d)] * spots
         blocks += [pl.BlockSpec((tps * first, d), lambda i, *_: (i, 0))] * spots
     total = count * half
-    block = pl.BlockSpec((tps, half, d), lambda i, *_: (i, 0, 0))
+    block = pl.BlockSpec((tps, half, d), lambda i, *_: (begin // tps + i, 0, 0))
     kernel = functools.partial(time_kernel, tps, begin, form)
     extra = [] if after is None else [after]
     if extra:
@@ -196,7 +205,7 @@
             num_scalar_prefetch=2,
             grid=(count // tps,),
             in_specs=[pl.BlockSpec(memory_space=pl.ANY)] * len(extra)
-            + [full(visible.shape), pl.BlockSpec((tps, half, d), lambda i, *_: (begin // tps + i, 0, 0)), block]
+            + [full(visible.shape), block, block]
             + [full(w.shape) for w in weights],
             out_specs=blocks,
             scratch_shapes=[pltpu.VMEM((tps * half, d), F32)],
@@ -432,8 +441,9 @@
     rows = half // spots
     n, m = FIRST_TRACKS, FIRST_FRAMES
     common = (first_frame, visible, info, time_weights, spots)
-    (dense,) = time_part(tokens, swap_cores(tokens[:n]), *common, "dense", 0, 0, n, None)
-    rest, *first = time_part(tokens, swap_cores(tokens[n:]), *common, "split", m, n, tracks - n, dense)
+    other = swap_cores(tokens)
+    (dense,) = time_part(tokens, other, *common, "dense", 0, 0, n, None)
+    rest, *first = time_part(tokens, other, *common, "split", m, n, tracks - n, dense)
     dense, first, rest = exchange(dense), shift(first, spots, 1), exchange(rest)
     (first,) = frames_part(dense, first, info, (rows, m), (0, 0), "dense", m, BLOCK, virtual_weights)
     rest = frames_part(dense, [rest], info, (rows, rows - m), (m, 0), "pieces", rows - m, BLOCK, virtual_weights)

time: 119 us -> 116 us (0.975)
  local copies, waits for them, and re-layouts: 3.94 us -> 2.64 us
    slice x1 -> x0, local copies, waits for them, and re-layouts: 1.57 us -> none  [pipelined(): tokens[n:]]
    ppermute x2 -> x1, waiting for transfers between devices: 3.68 us -> 2.64 us  [swap_cores(): return lax.ppermute(x, 'frames', [(0, 1), (1, 0)])]
  transfers between devices with their start and end apart: 19 -> 18, of which waited for: 6 -> 5; matrix products, arithmetic and copies ran while one was open for 1% -> 1% of each run, Pallas kernels for 34% -> 35%
where the time goes in v2:
time: 116 us; the launch traced here: 115 us
  Pallas kernels  56.3 us (49%)
  starting transfers between devices  49.1 us (42%)
  waiting for transfers between devices  6 us (5%)
  local copies, waits for them, and re-layouts  2.64 us (2%)
    ppermute x14, starting transfers between devices, shift(): lax.ppermute(xs[k], 'tracks', [(i, (i + sign * k) % spots) for i in range...  32 us
    pallas_call x2, Pallas kernels, time_part(): pl.pallas_call(kernel, out_shape=[jax.ShapeDtypeStruct(s, BF) for s in sh...  27.5 us
    pallas_call x2, Pallas kernels, frames_part(): pl.pallas_call(functools.partial(frames_kernel, spots, len(shapes), spans...  26.4 us
    all_to_all x3, starting transfers between devices, exchange(): return lax.all_to_all(x, 'tracks', split_axis=0, concat_axis=0, tiled=True)  16.6 us
    ppermute x14, waiting for transfers between devices, shift(): lax.ppermute(xs[k], 'tracks', [(i, (i + sign * k) % spots) for i in range...  3.35 us
    unnamed x24, local copies, waits for them, and re-layouts  2.64 us
    ppermute x1, waiting for transfers between devices, swap_cores(): return lax.ppermute(x, 'frames', [(0, 1), (1, 0)])  2.64 us
    pallas_call x1, Pallas kernels, home(): pl.pallas_call(functools.partial(home_kernel, spots), out_shape=jax.Shape...  2.38 us
  transfers between devices with their start and end apart: 18, of which 5 were waited for; matrix products, arithmetic and copies ran while one was open for 1% of the time, Pallas kernels for 35%

profile of v2, /device:TPU:0, one launch (start us, length us, event | category | flops | bytes accessed | tf_op | source)
XLA Modules:
  0.0 114.8 jit_solution(6772549786887218260)
XLA Ops:
  0.0 0.5 collective-permute-start
  0.5 0.6 pad_add_fusion.info_ref
  1.1 2.6 %collective-permute-done.other_ref.refs_2_ = bf16[16,128,384]{2,1,0:T(8,128)(2,1)S(1)} collective-permute-done((bf16[16,128,384]{2,1,0:T(8,128)(2,1)}, bf16[16,128,384]{2,1,0:T(8,128)(2,1)S(1)}, u32[]{:S(2)}, u32[]{:S(2)}) %collective-permute-start) | collective-permute-done | bytes 1572896 | tf_op jit(solution)/shard_map/ppermute | solution.py:418
  3.7 1.1 copy-done.4
  4.8 13.7 %time_part.2.after_ref = bf16[8,128,384]{2,1,0:T(8,128)(2,1)} custom-call(s32[2]{0:T(128)} %pad_add_fusion.info_ref, s32[16]{0:T(128)} %first_ref.3, s32[16,256]{1,0:T(8,128)} %refs_0_.3, bf16[16,128,384]{2,1,0:T(8,128)(2,1)} %refs_1_.4, bf16[16,128,384]{2,1,0:T(8,128)(2,1)} %copy-done.4, bf16[384,1152]{1,0:T(8,128)(2,1)} %refs_3_.4, ...), custom_call_target="tpu_custom_call" | custom-call | flops 5120000000 | bytes 1572864 | tf_op jit(solution)/shard_map/time_part/pallas_call | solution.py:201
  18.5 7.2 %all-to-all-start = ((bf16[8,128,384]{2,1,0:T(8,128)(2,1)}), bf16[8,128,384]{2,1,0:T(8,128)(2,1)S(1)}, u32[]{:S(2)}, u32[]{:S(2)}) async-start(bf16[8,128,384]{2,1,0:T(8,128)(2,1)} %time_part.2.after_ref), calls=%async_computation | async-start | bytes 1572864 | tf_op jit(solution)/shard_map/all_to_all | solution.py:414
  25.7 13.8 %time_part.3 = (bf16[8,64,384]{2,1,0:T(8,128)(2,1)}, bf16[64,384]{1,0:T(8,128)(2,1)}, bf16[64,384]{1,0:T(8,128)(2,1)}, bf16[64,384]{1,0:T(8,128)(2,1)}, bf16[64,...) custom-call(s32[2]{0:T(128)} %pad_add_fusion.info_ref, ...), custom_call_target="tpu_custom_call" | custom-call | flops 5120000000 | bytes 1572864 | tf_op jit(solution)/shard_map/time_part/pallas_call | solution.py:201
  39.5 2.1 %collective-permute-start.1 = (bf16[64,384]{1,0:T(8,128)(2,1)}, bf16[64,384]{1,0:T(8,128)(2,1)S(1)}, u32[]{:S(2)}, u32[]{:S(2)}) collective-permute-start(bf16[64,384]{1,0:T(8,128)(2,1)} %get-tuple-element.23), channel_id=1, source_target_pairs={{0,2},{2,4},{4,6},{6,8},{8,10},{10,12},{12,14},{14,0},{1,3},{3,5},... | collective-permute-start | bytes 147464 | tf_op jit(solution)/shard_map/ppermute | solution.py:423
  41.6 1.5 %collective-permute-start.2 = (bf16[64,384]{1,0:T(8,128)(2,1)}, bf16[64,384]{1,0:T(8,128)(2,1)S(1)}, u32[]{:S(2)}, u32[]{:S(2)}) collective-permute-start(bf16[64,384]{1,0:T(8,128)(2,1)} %get-tuple-element.24), channel_id=1, source_target_pairs={{0,4},{2,6},{4,8},{6,10},{8,12},{10,14},{12,0},{14,2},{1,5},{3,7},... | collective-permute-start | bytes 147464 | tf_op jit(solution)/shard_map/ppermute | solution.py:423
  43.0 2.4 %collective-permute-start.3 = (bf16[64,384]{1,0:T(8,128)(2,1)}, bf16[64,384]{1,0:T(8,128)(2,1)S(1)}, u32[]{:S(2)}, u32[]{:S(2)}) collective-permute-start(bf16[64,384]{1,0:T(8,128)(2,1)} %get-tuple-element.25), channel_id=1, source_target_pairs={{0,6},{2,8},{4,10},{6,12},{8,14},{10,0},{12,2},{14,4},{1,7},{3,9},... | collective-permute-start | bytes 147464 | tf_op jit(solution)/shard_map/ppermute | solution.py:423
  45.4 1.5 %collective-permute-start.4 = (bf16[64,384]{1,0:T(8,128)(2,1)}, bf16[64,384]{1,0:T(8,128)(2,1)S(1)}, u32[]{:S(2)}, u32[]{:S(2)}) collective-permute-start(bf16[64,384]{1,0:T(8,128)(2,1)} %get-tuple-element.26), channel_id=1, source_target_pairs={{0,8},{2,10},{4,12},{6,14},{8,0},{10,2},{12,4},{14,6},{1,9},{3,11}... | collective-permute-start | bytes 147464 | tf_op jit(solution)/shard_map/ppermute | solution.py:423
  46.9 2.4 %collective-permute-start.5 = (bf16[64,384]{1,0:T(8,128)(2,1)}, bf16[64,384]{1,0:T(8,128)(2,1)S(1)}, u32[]{:S(2)}, u32[]{:S(2)}) collective-permute-start(bf16[64,384]{1,0:T(8,128)(2,1)} %get-tuple-element.27), channel_id=1, source_target_pairs={{0,10},{2,12},{4,14},{6,0},{8,2},{10,4},{12,6},{14,8},{1,11},{3,13... | collective-permute-start | bytes 147464 | tf_op jit(solution)/shard_map/ppermute | solution.py:423
  49.2 0.0 collective-permute-done.1.refs_1_
  49.2 1.5 %collective-permute-start.6 = (bf16[64,384]{1,0:T(8,128)(2,1)}, bf16[64,384]{1,0:T(8,128)(2,1)S(1)}, u32[]{:S(2)}, u32[]{:S(2)}) collective-permute-start(bf16[64,384]{1,0:T(8,128)(2,1)} %get-tuple-element.28), channel_id=1, source_target_pairs={{0,12},{2,14},{4,0},{6,2},{8,4},{10,6},{12,8},{14,10},{1,13},{3,15... | collective-permute-start | bytes 147464 | tf_op jit(solution)/shard_map/ppermute | solution.py:423
  50.7 0.0 collective-permute-done.2.refs_2_
  50.7 1.5 %collective-permute-start.7 = (bf16[64,384]{1,0:T(8,128)(2,1)}, bf16[64,384]{1,0:T(8,128)(2,1)S(1)}, u32[]{:S(2)}, u32[]{:S(2)}) collective-permute-start(bf16[64,384]{1,0:T(8,128)(2,1)} %get-tuple-element.29), channel_id=1, source_target_pairs={{0,14},{2,0},{4,2},{6,4},{8,6},{10,8},{12,10},{14,12},{1,15},{3,1}... | collective-permute-start | bytes 147464 | tf_op jit(solution)/shard_map/ppermute | solution.py:423
  52.2 0.0 all-to-all-done.dense_ref
  52.2 3.6 %all-to-all-start.2 = ((bf16[8,64,384]{2,1,0:T(8,128)(2,1)}), bf16[8,64,384]{2,1,0:T(8,128)(2,1)S(1)}, u32[]{:S(2)}, u32[]{:S(2)}) async-start(bf16[8,64,384]{2,1,0:T(8,128)(2,1)} %get-tuple-element.30), calls=%async_computation.2 | async-start | bytes 786432 | tf_op jit(solution)/shard_map/all_to_all | solution.py:414
  55.8 0.0 collective-permute-done.3.refs_3_
  55.8 0.0 collective-permute-done.4.refs_4_
  55.9 0.0 collective-permute-done.5.refs_5_
  55.9 0.0 collective-permute-done.6.refs_6_
  55.9 0.0 collective-permute-done.7.refs_7_
  55.9 0.5 copy-done.7
  56.4 0.0 copy-done.8
  56.5 0.0 copy-done.9
  56.5 0.0 copy-done.10
  56.5 0.0 copy-done.11
  56.5 13.2 %frames_part.2 = bf16[8,128,384]{2,1,0:T(8,128)(2,1)} custom-call(s32[2]{0:T(128)} %pad_add_fusion.info_ref, bf16[8,128,384]{2,1,0:T(8,128)(2,1)} %copy-done.2, bf16[64,384]{1,0:T(8,128)(2,1)} %get-tuple-element.22.refs_0_, bf16[64,384]{1,0:T(8,128)(2,1)} %copy-done.5, bf16[64,384]{1,0:T(8,128)(2,1)} %copy-done.6, bf16[64,384]{1,0:T(8,128)(2,1)} %copy-done.7, ...), custom_call_target="tpu_custom_call" | custom-call | flops 10240000000 | bytes 1572864 | tf_op jit(solution)/shard_map/frames_part/pallas_call | solution.py:367
  69.8 0.0 all-to-all-done.2.refs_0_
  69.8 5.7 %all-to-all-start.1 = ((bf16[8,128,384]{2,1,0:T(8,128)(2,1)}), bf16[8,128,384]{2,1,0:T(8,128)(2,1)S(1)}, u32[]{:S(2)}, u32[]{:S(2)}) async-start(bf16[8,128,384]{2,1,0:T(8,128)(2,1)} %frames_part.2), calls=%async_computation.1 | async-start | bytes 1572864 | tf_op jit(solution)/shard_map/all_to_all | solution.py:414
  75.6 13.2 %frames_part.3 = (bf16[128,384]{1,0:T(8,128)(2,1)}, bf16[128,384]{1,0:T(8,128)(2,1)}, bf16[128,384]{1,0:T(8,128)(2,1)}, bf16[128,384]{1,0:T(8,128)(2,1)}, bf16[1...) custom-call(s32[2]{0:T(128)} %pad_add_fusion.info_ref, ...), custom_call_target="tpu_custom_call" | custom-call | flops 10240000000 | bytes 1572864 | tf_op jit(solution)/shard_map/frames_part/pallas_call | solution.py:367
  88.7 4.7 %collective-permute-start.8 = (bf16[128,384]{1,0:T(8,128)(2,1)}, bf16[128,384]{1,0:T(8,128)(2,1)S(1)}, u32[]{:S(2)}, u32[]{:S(2)}) collective-permute-start(bf16[128,384]{1,0:T(8,128)(2,1)} %get-tuple-element.32), channel_id=1, source_target_pairs={{0,14},{2,0},{4,2},{6,4},{8,6},{10,8},{12,10},{14,12},{1,15},{3,1}... | collective-permute-start | bytes 294920 | tf_op jit(solution)/shard_map/ppermute | solution.py:423
  93.5 0.5 collective-permute-start.9
  94.0 0.0 collective-permute-start.10
  94.0 2.9 %collective-permute-start.11 = (bf16[128,384]{1,0:T(8,128)(2,1)}, bf16[128,384]{1,0:T(8,128)(2,1)S(1)}, u32[]{:S(2)}, u32[]{:S(2)}) collective-permute-start(bf16[128,384]{1,0:T(8,128)(2,1)} %get-tuple-element.35), channel_id=1, source_target_pairs={{0,8},{2,10},{4,12},{6,14},{8,0},{10,2},{12,4},{14,6},{1,9},{3,11}... | collective-permute-start | bytes 294920 | tf_op jit(solution)/shard_map/ppermute | solution.py:423
  97.0 0.0 collective-permute-start.12
  97.0 0.1 collective-permute-done.8.refs_1_
  97.0 2.0 %collective-permute-start.13 = (bf16[128,384]{1,0:T(8,128)(2,1)}, bf16[128,384]{1,0:T(8,128)(2,1)S(1)}, u32[]{:S(2)}, u32[]{:S(2)}) collective-permute-start(bf16[128,384]{1,0:T(8,128)(2,1)} %get-tuple-element.37), channel_id=1, source_target_pairs={{0,4},{2,6},{4,8},{6,10},{8,12},{10,14},{12,0},{14,2},{1,5},{3,7},... | collective-permute-start | bytes 294920 | tf_op jit(solution)/shard_map/ppermute | solution.py:423
  99.0 0.4 collective-permute-done.9.refs_2_
  99.4 9.2 %collective-permute-start.14 = (bf16[128,384]{1,0:T(8,128)(2,1)}, bf16[128,384]{1,0:T(8,128)(2,1)S(1)}, u32[]{:S(2)}, u32[]{:S(2)}) collective-permute-start(bf16[128,384]{1,0:T(8,128)(2,1)} %get-tuple-element.38), channel_id=1, source_target_pairs={{0,2},{2,4},{4,6},{6,8},{8,10},{10,12},{12,14},{14,0},{1,3},{3,5},... | collective-permute-start | bytes 294920 | tf_op jit(solution)/shard_map/ppermute | solution.py:423
  108.6 0.0 collective-permute-done.10.refs_3_
  108.6 2.1 %collective-permute-done.11.refs_4_ = bf16[128,384]{1,0:T(8,128)(2,1)S(1)} collective-permute-done((bf16[128,384]{1,0:T(8,128)(2,1)}, bf16[128,384]{1,0:T(8,128)(2,1)S(1)}, u32[]{:S(2)}, u32[]{:S(2)}) %collective-permute-start.11) | collective-permute-done | bytes 98336 | tf_op jit(solution)/shard_map/ppermute | solution.py:423
  110.7 0.8 collective-permute-done.12.refs_5_
  111.5 0.0 collective-permute-done.13.refs_6_
  111.5 0.0 collective-permute-done.14.refs_7_
  111.5 0.9 copy-done
  112.4 2.4 %home.1 = bf16[16,128,384]{2,1,0:T(8,128)(2,1)} custom-call(s32[2]{0:T(128)S(1)} %copy-done.1, bf16[8,128,384]{2,1,0:T(8,128)(2,1)S(1)} %all-to-all-done.1.dense_ref, bf16[128,384]{1,0:T(8,128)(2,1)S(1)} %copy-done, bf16[128,384]{1,0:T(8,128)(2,1)S(1)} %collective-permute-done.8.refs_1_, bf16[128,384]{1,0:T(8,128)(2,1)S(1)} %collective-permute-done.9.refs_2_, ...), custom_call_target="tpu_custom_call" | custom-call | tf_op jit(solution)/shard_map/home/pallas_call | solution.py:399
  (18 shorter events, 0.0 us)
Async XLA Ops:
  0.0 3.7 %collective-permute-start = (bf16[16,128,384]{2,1,0:T(8,128)(2,1)}, bf16[16,128,384]{2,1,0:T(8,128)(2,1)S(1)}, u32[]{:S(2)}, u32[]{:S(2)}) collective-permute-start(bf16[16,128,384]{2,1,0:T(8,128)(2,1)} %refs_1_.4), channel_id=1, source_target_pairs={{0,1},{1,0},{2,3},{3,2},{4,5},{5,4},{6,7},{7,6},{8,9},{9,8},{10,11... | collective-permute-start | bytes 4718600 | tf_op jit(solution)/shard_map/ppermute | solution.py:418
  3.7 1.1 copy-start.4
  18.5 33.6 %all-to-all-start = ((bf16[8,128,384]{2,1,0:T(8,128)(2,1)}), bf16[8,128,384]{2,1,0:T(8,128)(2,1)S(1)}, u32[]{:S(2)}, u32[]{:S(2)}) async-start(bf16[8,128,384]{2,1,0:T(8,128)(2,1)} %time_part.2.after_ref), calls=%async_computation | async-start | bytes 1572864 | tf_op jit(solution)/shard_map/all_to_all | solution.py:414
  39.5 9.7 %collective-permute-start.1 = (bf16[64,384]{1,0:T(8,128)(2,1)}, bf16[64,384]{1,0:T(8,128)(2,1)S(1)}, u32[]{:S(2)}, u32[]{:S(2)}) collective-permute-start(bf16[64,384]{1,0:T(8,128)(2,1)} %get-tuple-element.23), channel_id=1, source_target_pairs={{0,2},{2,4},{4,6},{6,8},{8,10},{10,12},{12,14},{14,0},{1,3},{3,5},... | collective-permute-start | bytes 147464 | tf_op jit(solution)/shard_map/ppermute | solution.py:423
  41.6 9.1 %collective-permute-start.2 = (bf16[64,384]{1,0:T(8,128)(2,1)}, bf16[64,384]{1,0:T(8,128)(2,1)S(1)}, u32[]{:S(2)}, u32[]{:S(2)}) collective-permute-start(bf16[64,384]{1,0:T(8,128)(2,1)} %get-tuple-element.24), channel_id=1, source_target_pairs={{0,4},{2,6},{4,8},{6,10},{8,12},{10,14},{12,0},{14,2},{1,5},{3,7},... | collective-permute-start | bytes 147464 | tf_op jit(solution)/shard_map/ppermute | solution.py:423
  43.0 12.8 %collective-permute-start.3 = (bf16[64,384]{1,0:T(8,128)(2,1)}, bf16[64,384]{1,0:T(8,128)(2,1)S(1)}, u32[]{:S(2)}, u32[]{:S(2)}) collective-permute-start(bf16[64,384]{1,0:T(8,128)(2,1)} %get-tuple-element.25), channel_id=1, source_target_pairs={{0,6},{2,8},{4,10},{6,12},{8,14},{10,0},{12,2},{14,4},{1,7},{3,9},... | collective-permute-start | bytes 147464 | tf_op jit(solution)/shard_map/ppermute | solution.py:423
  45.4 10.4 %collective-permute-start.4 = (bf16[64,384]{1,0:T(8,128)(2,1)}, bf16[64,384]{1,0:T(8,128)(2,1)S(1)}, u32[]{:S(2)}, u32[]{:S(2)}) collective-permute-start(bf16[64,384]{1,0:T(8,128)(2,1)} %get-tuple-element.26), channel_id=1, source_target_pairs={{0,8},{2,10},{4,12},{6,14},{8,0},{10,2},{12,4},{14,6},{1,9},{3,11}... | collective-permute-start | bytes 147464 | tf_op jit(solution)/shard_map/ppermute | solution.py:423
  46.9 9.0 %collective-permute-start.5 = (bf16[64,384]{1,0:T(8,128)(2,1)}, bf16[64,384]{1,0:T(8,128)(2,1)S(1)}, u32[]{:S(2)}, u32[]{:S(2)}) collective-permute-start(bf16[64,384]{1,0:T(8,128)(2,1)} %get-tuple-element.27), channel_id=1, source_target_pairs={{0,10},{2,12},{4,14},{6,0},{8,2},{10,4},{12,6},{14,8},{1,11},{3,13... | collective-permute-start | bytes 147464 | tf_op jit(solution)/shard_map/ppermute | solution.py:423
  49.2 6.7 %copy-start.5 = (bf16[64,384]{1,0:T(8,128)(2,1)}, bf16[64,384]{1,0:T(8,128)(2,1)S(1)}, u32[]{:S(2)}) copy-start(bf16[64,384]{1,0:T(8,128)(2,1)S(1)} %collective-permute-done.1.refs_1_) | copy-start | bytes 147460
  49.2 6.6 %collective-permute-start.6 = (bf16[64,384]{1,0:T(8,128)(2,1)}, bf16[64,384]{1,0:T(8,128)(2,1)S(1)}, u32[]{:S(2)}, u32[]{:S(2)}) collective-permute-start(bf16[64,384]{1,0:T(8,128)(2,1)} %get-tuple-element.28), channel_id=1, source_target_pairs={{0,12},{2,14},{4,0},{6,2},{8,4},{10,6},{12,8},{14,10},{1,13},{3,15... | collective-permute-start | bytes 147464 | tf_op jit(solution)/shard_map/ppermute | solution.py:423
  50.7 5.2 %copy-start.6 = (bf16[64,384]{1,0:T(8,128)(2,1)}, bf16[64,384]{1,0:T(8,128)(2,1)S(1)}, u32[]{:S(2)}) copy-start(bf16[64,384]{1,0:T(8,128)(2,1)S(1)} %collective-permute-done.2.refs_2_) | copy-start | bytes 147460
  50.7 5.2 %collective-permute-start.7 = (bf16[64,384]{1,0:T(8,128)(2,1)}, bf16[64,384]{1,0:T(8,128)(2,1)S(1)}, u32[]{:S(2)}, u32[]{:S(2)}) collective-permute-start(bf16[64,384]{1,0:T(8,128)(2,1)} %get-tuple-element.29), channel_id=1, source_target_pairs={{0,14},{2,0},{4,2},{6,4},{8,6},{10,8},{12,10},{14,12},{1,15},{3,1}... | collective-permute-start | bytes 147464 | tf_op jit(solution)/shard_map/ppermute | solution.py:423
  52.2 3.8 %copy-start.2 = (bf16[8,128,384]{2,1,0:T(8,128)(2,1)}, bf16[8,128,384]{2,1,0:T(8,128)(2,1)S(1)}, u32[]{:S(2)}) copy-start(bf16[8,128,384]{2,1,0:T(8,128)(2,1)S(1)} %all-to-all-done.dense_ref) | copy-start | bytes 2359300
  52.2 17.6 %all-to-all-start.2 = ((bf16[8,64,384]{2,1,0:T(8,128)(2,1)}), bf16[8,64,384]{2,1,0:T(8,128)(2,1)S(1)}, u32[]{:S(2)}, u32[]{:S(2)}) async-start(bf16[8,64,384]{2,1,0:T(8,128)(2,1)} %get-tuple-element.30), calls=%async_computation.2 | async-start | bytes 786432 | tf_op jit(solution)/shard_map/all_to_all | solution.py:414
  55.8 0.6 copy-start.7
  55.8 0.6 copy-start.8
  55.9 0.6 copy-start.9
  55.9 0.6 copy-start.10
  55.9 0.6 copy-start.11
  69.8 5.8 %copy-start.3 = (bf16[8,64,384]{2,1,0:T(8,128)(2,1)}, bf16[8,64,384]{2,1,0:T(8,128)(2,1)S(1)}, u32[]{:S(2)}) copy-start(bf16[8,64,384]{2,1,0:T(8,128)(2,1)S(1)} %all-to-all-done.2.refs_0_) | copy-start | bytes 1179652
  69.8 41.7 %all-to-all-start.1 = ((bf16[8,128,384]{2,1,0:T(8,128)(2,1)}), bf16[8,128,384]{2,1,0:T(8,128)(2,1)S(1)}, u32[]{:S(2)}, u32[]{:S(2)}) async-start(bf16[8,128,384]{2,1,0:T(8,128)(2,1)} %frames_part.2), calls=%async_computation.1 | async-start | bytes 1572864 | tf_op jit(solution)/shard_map/all_to_all | solution.py:414
  75.6 35.9 %copy-start.1 = (s32[2]{0:T(128)S(1)}, s32[2]{0:T(128)}, u32[]{:S(2)}) copy-start(s32[2]{0:T(128)} %pad_add_fusion.info_ref) | copy-start | bytes 28
  88.7 8.3 %collective-permute-start.8 = (bf16[128,384]{1,0:T(8,128)(2,1)}, bf16[128,384]{1,0:T(8,128)(2,1)S(1)}, u32[]{:S(2)}, u32[]{:S(2)}) collective-permute-start(bf16[128,384]{1,0:T(8,128)(2,1)} %get-tuple-element.32), channel_id=1, source_target_pairs={{0,14},{2,0},{4,2},{6,4},{8,6},{10,8},{12,10},{14,12},{1,15},{3,1}... | collective-permute-start | bytes 294920 | tf_op jit(solution)/shard_map/ppermute | solution.py:423
  93.5 6.0 %collective-permute-start.9 = (bf16[128,384]{1,0:T(8,128)(2,1)}, bf16[128,384]{1,0:T(8,128)(2,1)S(1)}, u32[]{:S(2)}, u32[]{:S(2)}) collective-permute-start(bf16[128,384]{1,0:T(8,128)(2,1)} %get-tuple-element.33), channel_id=1, source_target_pairs={{0,12},{2,14},{4,0},{6,2},{8,4},{10,6},{12,8},{14,10},{1,13},{3,15... | collective-permute-start | bytes 294920 | tf_op jit(solution)/shard_map/ppermute | solution.py:423
  94.0 14.6 %collective-permute-start.10 = (bf16[128,384]{1,0:T(8,128)(2,1)}, bf16[128,384]{1,0:T(8,128)(2,1)S(1)}, u32[]{:S(2)}, u32[]{:S(2)}) collective-permute-start(bf16[128,384]{1,0:T(8,128)(2,1)} %get-tuple-element.34), channel_id=1, source_target_pairs={{0,10},{2,12},{4,14},{6,0},{8,2},{10,4},{12,6},{14,8},{1,11},{3,13... | collective-permute-start | bytes 294920 | tf_op jit(solution)/shard_map/ppermute | solution.py:423
  94.0 16.7 %collective-permute-start.11 = (bf16[128,384]{1,0:T(8,128)(2,1)}, bf16[128,384]{1,0:T(8,128)(2,1)S(1)}, u32[]{:S(2)}, u32[]{:S(2)}) collective-permute-start(bf16[128,384]{1,0:T(8,128)(2,1)} %get-tuple-element.35), channel_id=1, source_target_pairs={{0,8},{2,10},{4,12},{6,14},{8,0},{10,2},{12,4},{14,6},{1,9},{3,11}... | collective-permute-start | bytes 294920 | tf_op jit(solution)/shard_map/ppermute | solution.py:423
  97.0 14.5 %collective-permute-start.12 = (bf16[128,384]{1,0:T(8,128)(2,1)}, bf16[128,384]{1,0:T(8,128)(2,1)S(1)}, u32[]{:S(2)}, u32[]{:S(2)}) collective-permute-start(bf16[128,384]{1,0:T(8,128)(2,1)} %get-tuple-element.36), channel_id=1, source_target_pairs={{0,6},{2,8},{4,10},{6,12},{8,14},{10,0},{12,2},{14,4},{1,7},{3,9},... | collective-permute-start | bytes 294920 | tf_op jit(solution)/shard_map/ppermute | solution.py:423
  97.0 14.4 %collective-permute-start.13 = (bf16[128,384]{1,0:T(8,128)(2,1)}, bf16[128,384]{1,0:T(8,128)(2,1)S(1)}, u32[]{:S(2)}, u32[]{:S(2)}) collective-permute-start(bf16[128,384]{1,0:T(8,128)(2,1)} %get-tuple-element.37), channel_id=1, source_target_pairs={{0,4},{2,6},{4,8},{6,10},{8,12},{10,14},{12,0},{14,2},{1,5},{3,7},... | collective-permute-start | bytes 294920 | tf_op jit(solution)/shard_map/ppermute | solution.py:423
  99.4 12.0 %collective-permute-start.14 = (bf16[128,384]{1,0:T(8,128)(2,1)}, bf16[128,384]{1,0:T(8,128)(2,1)S(1)}, u32[]{:S(2)}, u32[]{:S(2)}) collective-permute-start(bf16[128,384]{1,0:T(8,128)(2,1)} %get-tuple-element.38), channel_id=1, source_target_pairs={{0,2},{2,4},{4,6},{6,8},{8,10},{10,12},{12,14},{14,0},{1,3},{3,5},... | collective-permute-start | bytes 294920 | tf_op jit(solution)/shard_map/ppermute | solution.py:423
  111.5 0.9 copy-start

commit v3 on v2

--- a/solution.py
+++ b/solution.py
@@ -230,17 +230,35 @@
         self.tau = lanes.head**-0.5
         vq = normed(dot(normed(self.init).astype(BF), cq_ref[...]), self.tau).astype(BF)
         self.masks = [lanes.heads(self.virt, w) for w in range(2)]
+        lane = iota(lanes.width, 2 * self.virt, 1)
+        row = iota(lanes.width, 2 * self.virt, 0)
+        self.turned_masks, self.value_masks = [], []
+        for w in range(2):
+            pairs = []
+            for h in range(0, HALF, 2):
+                start = lanes.first[w] + h * lanes.head + jnp.where(lane < self.virt, 0, lanes.head)
+                pairs.append(jnp.where(within(row, start, lanes.head), 1.0, 0.0).astype(BF))
+            self.turned_masks.append(pairs)
+            sums = iota(self.virt, lanes.width, 1)
+            self.value_masks.append(
+                [
+                    m + jnp.where(within(sums, lanes.sums[w] + 16 * h, 16), 1.0, 0.0).astype(BF)
+                    for h, m in enumerate(self.masks[w])
+                ]
+            )
         self.stacked = [
             jnp.concatenate([lanes.cut(vq, w) * m for m in self.masks[w]], axis=0) for w in range(2)
         ]
 
     def attend(self, query, key, value, masks):
         lanes, pair = self.lanes, []
+        turned = jnp.transpose(jnp.concatenate([key, key], axis=0), (1, 0))
         for w in range(2):
-            q = lanes.cut(query, w)
-            q = jnp.concatenate([q * m for m in masks[w]], axis=0)
-            p = jnp.exp(dot_t(q, lanes.cut(key, w))).astype(BF)
-            pair.append(lanes.choose(dot(p, value[w]), query.shape[0], w))
+            k = turned[lanes.begin[w] : lanes.begin[w] + lanes.width]
+            k = jnp.concatenate([k * m for m in self.turned_masks[w]], axis=1)
+            p = jnp.exp(dot(lanes.cut(query, w), k)).astype(BF)
+            v = jnp.concatenate([value[w] * m for m in self.value_masks[w]], axis=0)
+            pair.append(dot(p, v))
         return pair
 
     def divide(self, pairs):
@@ -259,8 +277,9 @@
         for f in range(frames):
             rows = slice(f * tracks, (f + 1) * tracks)
             pair = []
+            turned = jnp.transpose(track_key[rows], (1, 0))
             for w in range(2):
-                p = jnp.exp(dot_t(self.stacked[w], lanes.cut(track_key[rows], w))).astype(BF)
+                p = jnp.exp(dot(self.stacked[w], turned[lanes.begin[w] : lanes.begin[w] + lanes.width])).astype(BF)
                 pair.append(lanes.choose(dot(p, ones[w][rows]), virt, w))
             pairs.append(pair)
         virtual = jnp.concatenate([self.init] * frames, axis=0) + dot(self.divide(pairs), self.co[...])

time: 116 us -> 114 us (0.983)
  Pallas kernels: 56.3 us -> 53 us
  starting transfers between devices: 49.1 us -> 50.9 us
    pallas_call x2, Pallas kernels: 26.4 us -> 23.2 us  [frames_part(): pl.pallas_call(functools.partial(frames_kernel, spots, len(shapes), spans...]
    ppermute x14, starting transfers between devices: 32 us -> 33.9 us  [shift(): lax.ppermute(xs[k], 'tracks', [(i, (i + sign * k) % spots) for i in range...]
  transfers between devices with their start and end apart: 18 -> 18, of which waited for: 5 -> 5; matrix products, arithmetic and copies ran while one was open for 1% -> 1% of each run, Pallas kernels for 35% -> 33%
where the time goes in v3:
time: 114 us; the launch traced here: 113 us
  Pallas kernels  53 us (46%)
  starting transfers between devices  50.9 us (45%)
  waiting for transfers between devices  5.78 us (5%)
  local copies, waits for them, and re-layouts  2.64 us (2%)
    ppermute x14, starting transfers between devices, shift(): lax.ppermute(xs[k], 'tracks', [(i, (i + sign * k) % spots) for i in range...  33.9 us
    pallas_call x2, Pallas kernels, time_part(): pl.pallas_call(kernel, out_shape=[jax.ShapeDtypeStruct(s, BF) for s in sh...  27.5 us
    pallas_call x2, Pallas kernels, frames_part(): pl.pallas_call(functools.partial(frames_kernel, spots, len(shapes), spans...  23.2 us
    all_to_all x3, starting transfers between devices, exchange(): return lax.all_to_all(x, 'tracks', split_axis=0, concat_axis=0, tiled=True)  16.6 us
    ppermute x14, waiting for transfers between devices, shift(): lax.ppermute(xs[k], 'tracks', [(i, (i + sign * k) % spots) for i in range...  3.13 us
    unnamed x24, local copies, waits for them, and re-layouts  2.64 us
    ppermute x1, waiting for transfers between devices, swap_cores(): return lax.ppermute(x, 'frames', [(0, 1), (1, 0)])  2.64 us
    pallas_call x1, Pallas kernels, home(): pl.pallas_call(functools.partial(home_kernel, spots), out_shape=jax.Shape...  2.38 us
  transfers between devices with their start and end apart: 18, of which 5 were waited for; matrix products, arithmetic and copies ran while one was open for 1% of the time, Pallas kernels for 33%

profile of v3, /device:TPU:0, one launch (start us, length us, event | category | flops | bytes accessed | tf_op | source)
XLA Modules:
  0.0 113.1 jit_solution(10661778028806119651)
XLA Ops:
  0.0 0.5 collective-permute-start
  0.5 0.6 pad_add_fusion.info_ref
  1.1 2.6 %collective-permute-done.other_ref.refs_2_ = bf16[16,128,384]{2,1,0:T(8,128)(2,1)S(1)} collective-permute-done((bf16[16,128,384]{2,1,0:T(8,128)(2,1)}, bf16[16,128,384]{2,1,0:T(8,128)(2,1)S(1)}, u32[]{:S(2)}, u32[]{:S(2)}) %collective-permute-start) | collective-permute-done | bytes 1572896 | tf_op jit(solution)/shard_map/ppermute | solution.py:437
  3.7 1.1 %copy-done.4 = bf16[16,128,384]{2,1,0:T(8,128)(2,1)} copy-done((bf16[16,128,384]{2,1,0:T(8,128)(2,1)}, bf16[16,128,384]{2,1,0:T(8,128)(2,1)S(1)}, u32[]{:S(2)}) %copy-start.4) | copy-done | bytes 1572888
  4.8 13.7 %time_part.2.after_ref = bf16[8,128,384]{2,1,0:T(8,128)(2,1)} custom-call(s32[2]{0:T(128)} %pad_add_fusion.info_ref, s32[16]{0:T(128)} %first_ref.3, s32[16,256]{1,0:T(8,128)} %refs_0_.3, bf16[16,128,384]{2,1,0:T(8,128)(2,1)} %refs_1_.4, bf16[16,128,384]{2,1,0:T(8,128)(2,1)} %copy-done.4, bf16[384,1152]{1,0:T(8,128)(2,1)} %refs_3_.4, ...), custom_call_target="tpu_custom_call" | custom-call | flops 5120000000 | bytes 1572864 | tf_op jit(solution)/shard_map/time_part/pallas_call | solution.py:201
  18.5 7.2 %all-to-all-start = ((bf16[8,128,384]{2,1,0:T(8,128)(2,1)}), bf16[8,128,384]{2,1,0:T(8,128)(2,1)S(1)}, u32[]{:S(2)}, u32[]{:S(2)}) async-start(bf16[8,128,384]{2,1,0:T(8,128)(2,1)} %time_part.2.after_ref), calls=%async_computation | async-start | bytes 1572864 | tf_op jit(solution)/shard_map/all_to_all | solution.py:433
  25.7 13.8 %time_part.3 = (bf16[8,64,384]{2,1,0:T(8,128)(2,1)}, bf16[64,384]{1,0:T(8,128)(2,1)}, bf16[64,384]{1,0:T(8,128)(2,1)}, bf16[64,384]{1,0:T(8,128)(2,1)}, bf16[64,...) custom-call(s32[2]{0:T(128)} %pad_add_fusion.info_ref, ...), custom_call_target="tpu_custom_call" | custom-call | flops 5120000000 | bytes 1572864 | tf_op jit(solution)/shard_map/time_part/pallas_call | solution.py:201
  39.5 2.1 %collective-permute-start.1 = (bf16[64,384]{1,0:T(8,128)(2,1)}, bf16[64,384]{1,0:T(8,128)(2,1)S(1)}, u32[]{:S(2)}, u32[]{:S(2)}) collective-permute-start(bf16[64,384]{1,0:T(8,128)(2,1)} %get-tuple-element.23), channel_id=1, source_target_pairs={{0,2},{2,4},{4,6},{6,8},{8,10},{10,12},{12,14},{14,0},{1,3},{3,5},... | collective-permute-start | bytes 147464 | tf_op jit(solution)/shard_map/ppermute | solution.py:442
  41.6 1.5 %collective-permute-start.2 = (bf16[64,384]{1,0:T(8,128)(2,1)}, bf16[64,384]{1,0:T(8,128)(2,1)S(1)}, u32[]{:S(2)}, u32[]{:S(2)}) collective-permute-start(bf16[64,384]{1,0:T(8,128)(2,1)} %get-tuple-element.24), channel_id=1, source_target_pairs={{0,4},{2,6},{4,8},{6,10},{8,12},{10,14},{12,0},{14,2},{1,5},{3,7},... | collective-permute-start | bytes 147464 | tf_op jit(solution)/shard_map/ppermute | solution.py:442
  43.0 2.4 %collective-permute-start.3 = (bf16[64,384]{1,0:T(8,128)(2,1)}, bf16[64,384]{1,0:T(8,128)(2,1)S(1)}, u32[]{:S(2)}, u32[]{:S(2)}) collective-permute-start(bf16[64,384]{1,0:T(8,128)(2,1)} %get-tuple-element.25), channel_id=1, source_target_pairs={{0,6},{2,8},{4,10},{6,12},{8,14},{10,0},{12,2},{14,4},{1,7},{3,9},... | collective-permute-start | bytes 147464 | tf_op jit(solution)/shard_map/ppermute | solution.py:442
  45.4 1.5 %collective-permute-start.4 = (bf16[64,384]{1,0:T(8,128)(2,1)}, bf16[64,384]{1,0:T(8,128)(2,1)S(1)}, u32[]{:S(2)}, u32[]{:S(2)}) collective-permute-start(bf16[64,384]{1,0:T(8,128)(2,1)} %get-tuple-element.26), channel_id=1, source_target_pairs={{0,8},{2,10},{4,12},{6,14},{8,0},{10,2},{12,4},{14,6},{1,9},{3,11}... | collective-permute-start | bytes 147464 | tf_op jit(solution)/shard_map/ppermute | solution.py:442
  46.9 2.4 %collective-permute-start.5 = (bf16[64,384]{1,0:T(8,128)(2,1)}, bf16[64,384]{1,0:T(8,128)(2,1)S(1)}, u32[]{:S(2)}, u32[]{:S(2)}) collective-permute-start(bf16[64,384]{1,0:T(8,128)(2,1)} %get-tuple-element.27), channel_id=1, source_target_pairs={{0,10},{2,12},{4,14},{6,0},{8,2},{10,4},{12,6},{14,8},{1,11},{3,13... | collective-permute-start | bytes 147464 | tf_op jit(solution)/shard_map/ppermute | solution.py:442
  49.2 0.0 collective-permute-done.1.refs_1_
  49.2 1.5 %collective-permute-start.6 = (bf16[64,384]{1,0:T(8,128)(2,1)}, bf16[64,384]{1,0:T(8,128)(2,1)S(1)}, u32[]{:S(2)}, u32[]{:S(2)}) collective-permute-start(bf16[64,384]{1,0:T(8,128)(2,1)} %get-tuple-element.28), channel_id=1, source_target_pairs={{0,12},{2,14},{4,0},{6,2},{8,4},{10,6},{12,8},{14,10},{1,13},{3,15... | collective-permute-start | bytes 147464 | tf_op jit(solution)/shard_map/ppermute | solution.py:442
  50.7 0.0 collective-permute-done.2.refs_2_
  50.7 1.5 %collective-permute-start.7 = (bf16[64,384]{1,0:T(8,128)(2,1)}, bf16[64,384]{1,0:T(8,128)(2,1)S(1)}, u32[]{:S(2)}, u32[]{:S(2)}) collective-permute-start(bf16[64,384]{1,0:T(8,128)(2,1)} %get-tuple-element.29), channel_id=1, source_target_pairs={{0,14},{2,0},{4,2},{6,4},{8,6},{10,8},{12,10},{14,12},{1,15},{3,1}... | collective-permute-start | bytes 147464 | tf_op jit(solution)/shard_map/ppermute | solution.py:442
  52.2 0.0 all-to-all-done.dense_ref
  52.2 3.6 %all-to-all-start.2 = ((bf16[8,64,384]{2,1,0:T(8,128)(2,1)}), bf16[8,64,384]{2,1,0:T(8,128)(2,1)S(1)}, u32[]{:S(2)}, u32[]{:S(2)}) async-start(bf16[8,64,384]{2,1,0:T(8,128)(2,1)} %get-tuple-element.30), calls=%async_computation.2 | async-start | bytes 786432 | tf_op jit(solution)/shard_map/all_to_all | solution.py:433
  55.8 0.0 collective-permute-done.3.refs_3_
  55.8 0.0 collective-permute-done.4.refs_4_
  55.9 0.0 collective-permute-done.5.refs_5_
  55.9 0.0 collective-permute-done.6.refs_6_
  55.9 0.0 collective-permute-done.7.refs_7_
  55.9 0.5 copy-done.7
  56.4 0.0 copy-done.8
  56.5 0.0 copy-done.9
  56.5 0.0 copy-done.10
  56.5 0.0 copy-done.11
  56.5 11.6 %frames_part.2 = bf16[8,128,384]{2,1,0:T(8,128)(2,1)} custom-call(s32[2]{0:T(128)} %pad_add_fusion.info_ref, bf16[8,128,384]{2,1,0:T(8,128)(2,1)} %copy-done.2, bf16[64,384]{1,0:T(8,128)(2,1)} %get-tuple-element.22.refs_0_, bf16[64,384]{1,0:T(8,128)(2,1)} %copy-done.5, bf16[64,384]{1,0:T(8,128)(2,1)} %copy-done.6, bf16[64,384]{1,0:T(8,128)(2,1)} %copy-done.7, ...), custom_call_target="tpu_custom_call" | custom-call | flops 10240000000 | bytes 1572864 | tf_op jit(solution)/shard_map/frames_part/pallas_call | solution.py:386
  68.2 0.0 all-to-all-done.2.refs_0_
  68.2 5.8 %all-to-all-start.1 = ((bf16[8,128,384]{2,1,0:T(8,128)(2,1)}), bf16[8,128,384]{2,1,0:T(8,128)(2,1)S(1)}, u32[]{:S(2)}, u32[]{:S(2)}) async-start(bf16[8,128,384]{2,1,0:T(8,128)(2,1)} %frames_part.2), calls=%async_computation.1 | async-start | bytes 1572864 | tf_op jit(solution)/shard_map/all_to_all | solution.py:433
  73.9 11.5 %frames_part.3 = (bf16[128,384]{1,0:T(8,128)(2,1)}, bf16[128,384]{1,0:T(8,128)(2,1)}, bf16[128,384]{1,0:T(8,128)(2,1)}, bf16[128,384]{1,0:T(8,128)(2,1)}, bf16[1...) custom-call(s32[2]{0:T(128)} %pad_add_fusion.info_ref, ...), custom_call_target="tpu_custom_call" | custom-call | flops 10240000000 | bytes 1572864 | tf_op jit(solution)/shard_map/frames_part/pallas_call | solution.py:386
  85.5 4.7 %collective-permute-start.8 = (bf16[128,384]{1,0:T(8,128)(2,1)}, bf16[128,384]{1,0:T(8,128)(2,1)S(1)}, u32[]{:S(2)}, u32[]{:S(2)}) collective-permute-start(bf16[128,384]{1,0:T(8,128)(2,1)} %get-tuple-element.32), channel_id=1, source_target_pairs={{0,14},{2,0},{4,2},{6,4},{8,6},{10,8},{12,10},{14,12},{1,15},{3,1}... | collective-permute-start | bytes 294920 | tf_op jit(solution)/shard_map/ppermute | solution.py:442
  90.2 0.6 collective-permute-start.9
  90.8 0.0 collective-permute-start.10
  90.8 2.9 %collective-permute-start.11 = (bf16[128,384]{1,0:T(8,128)(2,1)}, bf16[128,384]{1,0:T(8,128)(2,1)S(1)}, u32[]{:S(2)}, u32[]{:S(2)}) collective-permute-start(bf16[128,384]{1,0:T(8,128)(2,1)} %get-tuple-element.35), channel_id=1, source_target_pairs={{0,8},{2,10},{4,12},{6,14},{8,0},{10,2},{12,4},{14,6},{1,9},{3,11}... | collective-permute-start | bytes 294920 | tf_op jit(solution)/shard_map/ppermute | solution.py:442
  93.7 0.0 collective-permute-start.12
  93.7 0.1 collective-permute-done.8.refs_1_
  93.8 1.9 %collective-permute-start.13 = (bf16[128,384]{1,0:T(8,128)(2,1)}, bf16[128,384]{1,0:T(8,128)(2,1)S(1)}, u32[]{:S(2)}, u32[]{:S(2)}) collective-permute-start(bf16[128,384]{1,0:T(8,128)(2,1)} %get-tuple-element.37), channel_id=1, source_target_pairs={{0,4},{2,6},{4,8},{6,10},{8,12},{10,14},{12,0},{14,2},{1,5},{3,7},... | collective-permute-start | bytes 294920 | tf_op jit(solution)/shard_map/ppermute | solution.py:442
  95.7 0.2 collective-permute-done.9.refs_2_
  96.0 11.1 %collective-permute-start.14 = (bf16[128,384]{1,0:T(8,128)(2,1)}, bf16[128,384]{1,0:T(8,128)(2,1)S(1)}, u32[]{:S(2)}, u32[]{:S(2)}) collective-permute-start(bf16[128,384]{1,0:T(8,128)(2,1)} %get-tuple-element.38), channel_id=1, source_target_pairs={{0,2},{2,4},{4,6},{6,8},{8,10},{10,12},{12,14},{14,0},{1,3},{3,5},... | collective-permute-start | bytes 294920 | tf_op jit(solution)/shard_map/ppermute | solution.py:442
  107.0 0.0 collective-permute-done.10.refs_3_
  107.0 2.1 %collective-permute-done.11.refs_4_ = bf16[128,384]{1,0:T(8,128)(2,1)S(1)} collective-permute-done((bf16[128,384]{1,0:T(8,128)(2,1)}, bf16[128,384]{1,0:T(8,128)(2,1)S(1)}, u32[]{:S(2)}, u32[]{:S(2)}) %collective-permute-start.11) | collective-permute-done | bytes 98336 | tf_op jit(solution)/shard_map/ppermute | solution.py:442
  109.1 0.8 collective-permute-done.12.refs_5_
  109.8 0.0 collective-permute-done.13.refs_6_
  109.9 0.0 all-to-all-done.1.dense_ref
  109.9 0.9 copy-done
  110.8 2.4 %home.1 = bf16[16,128,384]{2,1,0:T(8,128)(2,1)} custom-call(s32[2]{0:T(128)S(1)} %copy-done.1, bf16[8,128,384]{2,1,0:T(8,128)(2,1)S(1)} %all-to-all-done.1.dense_ref, bf16[128,384]{1,0:T(8,128)(2,1)S(1)} %copy-done, bf16[128,384]{1,0:T(8,128)(2,1)S(1)} %collective-permute-done.8.refs_1_, bf16[128,384]{1,0:T(8,128)(2,1)S(1)} %collective-permute-done.9.refs_2_, ...), custom_call_target="tpu_custom_call" | custom-call | tf_op jit(solution)/shard_map/home/pallas_call | solution.py:418
  (18 shorter events, 0.0 us)
Async XLA Ops:
  0.0 3.7 %collective-permute-start = (bf16[16,128,384]{2,1,0:T(8,128)(2,1)}, bf16[16,128,384]{2,1,0:T(8,128)(2,1)S(1)}, u32[]{:S(2)}, u32[]{:S(2)}) collective-permute-start(bf16[16,128,384]{2,1,0:T(8,128)(2,1)} %refs_1_.4), channel_id=1, source_target_pairs={{0,1},{1,0},{2,3},{3,2},{4,5},{5,4},{6,7},{7,6},{8,9},{9,8},{10,11... | collective-permute-start | bytes 4718600 | tf_op jit(solution)/shard_map/ppermute | solution.py:437
  3.7 1.1 %copy-start.4 = (bf16[16,128,384]{2,1,0:T(8,128)(2,1)}, bf16[16,128,384]{2,1,0:T(8,128)(2,1)S(1)}, u32[]{:S(2)}) copy-start(bf16[16,128,384]{2,1,0:T(8,128)(2,1)S(1)} %collective-permute-done.other_ref.refs_2_) | copy-start | bytes 4718596
  18.5 33.6 %all-to-all-start = ((bf16[8,128,384]{2,1,0:T(8,128)(2,1)}), bf16[8,128,384]{2,1,0:T(8,128)(2,1)S(1)}, u32[]{:S(2)}, u32[]{:S(2)}) async-start(bf16[8,128,384]{2,1,0:T(8,128)(2,1)} %time_part.2.after_ref), calls=%async_computation | async-start | bytes 1572864 | tf_op jit(solution)/shard_map/all_to_all | solution.py:433
  39.5 9.7 %collective-permute-start.1 = (bf16[64,384]{1,0:T(8,128)(2,1)}, bf16[64,384]{1,0:T(8,128)(2,1)S(1)}, u32[]{:S(2)}, u32[]{:S(2)}) collective-permute-start(bf16[64,384]{1,0:T(8,128)(2,1)} %get-tuple-element.23), channel_id=1, source_target_pairs={{0,2},{2,4},{4,6},{6,8},{8,10},{10,12},{12,14},{14,0},{1,3},{3,5},... | collective-permute-start | bytes 147464 | tf_op jit(solution)/shard_map/ppermute | solution.py:442
  41.6 9.1 %collective-permute-start.2 = (bf16[64,384]{1,0:T(8,128)(2,1)}, bf16[64,384]{1,0:T(8,128)(2,1)S(1)}, u32[]{:S(2)}, u32[]{:S(2)}) collective-permute-start(bf16[64,384]{1,0:T(8,128)(2,1)} %get-tuple-element.24), channel_id=1, source_target_pairs={{0,4},{2,6},{4,8},{6,10},{8,12},{10,14},{12,0},{14,2},{1,5},{3,7},... | collective-permute-start | bytes 147464 | tf_op jit(solution)/shard_map/ppermute | solution.py:442
  43.0 12.8 %collective-permute-start.3 = (bf16[64,384]{1,0:T(8,128)(2,1)}, bf16[64,384]{1,0:T(8,128)(2,1)S(1)}, u32[]{:S(2)}, u32[]{:S(2)}) collective-permute-start(bf16[64,384]{1,0:T(8,128)(2,1)} %get-tuple-element.25), channel_id=1, source_target_pairs={{0,6},{2,8},{4,10},{6,12},{8,14},{10,0},{12,2},{14,4},{1,7},{3,9},... | collective-permute-start | bytes 147464 | tf_op jit(solution)/shard_map/ppermute | solution.py:442
  45.4 10.4 %collective-permute-start.4 = (bf16[64,384]{1,0:T(8,128)(2,1)}, bf16[64,384]{1,0:T(8,128)(2,1)S(1)}, u32[]{:S(2)}, u32[]{:S(2)}) collective-permute-start(bf16[64,384]{1,0:T(8,128)(2,1)} %get-tuple-element.26), channel_id=1, source_target_pairs={{0,8},{2,10},{4,12},{6,14},{8,0},{10,2},{12,4},{14,6},{1,9},{3,11}... | collective-permute-start | bytes 147464 | tf_op jit(solution)/shard_map/ppermute | solution.py:442
  46.9 9.0 %collective-permute-start.5 = (bf16[64,384]{1,0:T(8,128)(2,1)}, bf16[64,384]{1,0:T(8,128)(2,1)S(1)}, u32[]{:S(2)}, u32[]{:S(2)}) collective-permute-start(bf16[64,384]{1,0:T(8,128)(2,1)} %get-tuple-element.27), channel_id=1, source_target_pairs={{0,10},{2,12},{4,14},{6,0},{8,2},{10,4},{12,6},{14,8},{1,11},{3,13... | collective-permute-start | bytes 147464 | tf_op jit(solution)/shard_map/ppermute | solution.py:442
  49.2 6.7 %copy-start.5 = (bf16[64,384]{1,0:T(8,128)(2,1)}, bf16[64,384]{1,0:T(8,128)(2,1)S(1)}, u32[]{:S(2)}) copy-start(bf16[64,384]{1,0:T(8,128)(2,1)S(1)} %collective-permute-done.1.refs_1_) | copy-start | bytes 147460
  49.2 6.6 %collective-permute-start.6 = (bf16[64,384]{1,0:T(8,128)(2,1)}, bf16[64,384]{1,0:T(8,128)(2,1)S(1)}, u32[]{:S(2)}, u32[]{:S(2)}) collective-permute-start(bf16[64,384]{1,0:T(8,128)(2,1)} %get-tuple-element.28), channel_id=1, source_target_pairs={{0,12},{2,14},{4,0},{6,2},{8,4},{10,6},{12,8},{14,10},{1,13},{3,15... | collective-permute-start | bytes 147464 | tf_op jit(solution)/shard_map/ppermute | solution.py:442
  50.7 5.2 %copy-start.6 = (bf16[64,384]{1,0:T(8,128)(2,1)}, bf16[64,384]{1,0:T(8,128)(2,1)S(1)}, u32[]{:S(2)}) copy-start(bf16[64,384]{1,0:T(8,128)(2,1)S(1)} %collective-permute-done.2.refs_2_) | copy-start | bytes 147460
  50.7 5.2 %collective-permute-start.7 = (bf16[64,384]{1,0:T(8,128)(2,1)}, bf16[64,384]{1,0:T(8,128)(2,1)S(1)}, u32[]{:S(2)}, u32[]{:S(2)}) collective-permute-start(bf16[64,384]{1,0:T(8,128)(2,1)} %get-tuple-element.29), channel_id=1, source_target_pairs={{0,14},{2,0},{4,2},{6,4},{8,6},{10,8},{12,10},{14,12},{1,15},{3,1}... | collective-permute-start | bytes 147464 | tf_op jit(solution)/shard_map/ppermute | solution.py:442
  52.2 3.8 %copy-start.2 = (bf16[8,128,384]{2,1,0:T(8,128)(2,1)}, bf16[8,128,384]{2,1,0:T(8,128)(2,1)S(1)}, u32[]{:S(2)}) copy-start(bf16[8,128,384]{2,1,0:T(8,128)(2,1)S(1)} %all-to-all-done.dense_ref) | copy-start | bytes 2359300
  52.2 16.0 %all-to-all-start.2 = ((bf16[8,64,384]{2,1,0:T(8,128)(2,1)}), bf16[8,64,384]{2,1,0:T(8,128)(2,1)S(1)}, u32[]{:S(2)}, u32[]{:S(2)}) async-start(bf16[8,64,384]{2,1,0:T(8,128)(2,1)} %get-tuple-element.30), calls=%async_computation.2 | async-start | bytes 786432 | tf_op jit(solution)/shard_map/all_to_all | solution.py:433
  55.8 0.6 copy-start.7
  55.8 0.6 copy-start.8
  55.9 0.6 copy-start.9
  55.9 0.6 copy-start.10
  55.9 0.6 copy-start.11
  68.2 5.8 %copy-start.3 = (bf16[8,64,384]{2,1,0:T(8,128)(2,1)}, bf16[8,64,384]{2,1,0:T(8,128)(2,1)S(1)}, u32[]{:S(2)}) copy-start(bf16[8,64,384]{2,1,0:T(8,128)(2,1)S(1)} %all-to-all-done.2.refs_0_) | copy-start | bytes 1179652
  68.2 41.7 %all-to-all-start.1 = ((bf16[8,128,384]{2,1,0:T(8,128)(2,1)}), bf16[8,128,384]{2,1,0:T(8,128)(2,1)S(1)}, u32[]{:S(2)}, u32[]{:S(2)}) async-start(bf16[8,128,384]{2,1,0:T(8,128)(2,1)} %frames_part.2), calls=%async_computation.1 | async-start | bytes 1572864 | tf_op jit(solution)/shard_map/all_to_all | solution.py:433
  73.9 35.9 %copy-start.1 = (s32[2]{0:T(128)S(1)}, s32[2]{0:T(128)}, u32[]{:S(2)}) copy-start(s32[2]{0:T(128)} %pad_add_fusion.info_ref) | copy-start | bytes 28
  85.5 8.3 %collective-permute-start.8 = (bf16[128,384]{1,0:T(8,128)(2,1)}, bf16[128,384]{1,0:T(8,128)(2,1)S(1)}, u32[]{:S(2)}, u32[]{:S(2)}) collective-permute-start(bf16[128,384]{1,0:T(8,128)(2,1)} %get-tuple-element.32), channel_id=1, source_target_pairs={{0,14},{2,0},{4,2},{6,4},{8,6},{10,8},{12,10},{14,12},{1,15},{3,1}... | collective-permute-start | bytes 294920 | tf_op jit(solution)/shard_map/ppermute | solution.py:442
  90.2 5.7 %collective-permute-start.9 = (bf16[128,384]{1,0:T(8,128)(2,1)}, bf16[128,384]{1,0:T(8,128)(2,1)S(1)}, u32[]{:S(2)}, u32[]{:S(2)}) collective-permute-start(bf16[128,384]{1,0:T(8,128)(2,1)} %get-tuple-element.33), channel_id=1, source_target_pairs={{0,12},{2,14},{4,0},{6,2},{8,4},{10,6},{12,8},{14,10},{1,13},{3,15... | collective-permute-start | bytes 294920 | tf_op jit(solution)/shard_map/ppermute | solution.py:442
  90.8 16.2 %collective-permute-start.10 = (bf16[128,384]{1,0:T(8,128)(2,1)}, bf16[128,384]{1,0:T(8,128)(2,1)S(1)}, u32[]{:S(2)}, u32[]{:S(2)}) collective-permute-start(bf16[128,384]{1,0:T(8,128)(2,1)} %get-tuple-element.34), channel_id=1, source_target_pairs={{0,10},{2,12},{4,14},{6,0},{8,2},{10,4},{12,6},{14,8},{1,11},{3,13... | collective-permute-start | bytes 294920 | tf_op jit(solution)/shard_map/ppermute | solution.py:442
  90.8 18.3 %collective-permute-start.11 = (bf16[128,384]{1,0:T(8,128)(2,1)}, bf16[128,384]{1,0:T(8,128)(2,1)S(1)}, u32[]{:S(2)}, u32[]{:S(2)}) collective-permute-start(bf16[128,384]{1,0:T(8,128)(2,1)} %get-tuple-element.35), channel_id=1, source_target_pairs={{0,8},{2,10},{4,12},{6,14},{8,0},{10,2},{12,4},{14,6},{1,9},{3,11}... | collective-permute-start | bytes 294920 | tf_op jit(solution)/shard_map/ppermute | solution.py:442
  93.7 16.2 %collective-permute-start.12 = (bf16[128,384]{1,0:T(8,128)(2,1)}, bf16[128,384]{1,0:T(8,128)(2,1)S(1)}, u32[]{:S(2)}, u32[]{:S(2)}) collective-permute-start(bf16[128,384]{1,0:T(8,128)(2,1)} %get-tuple-element.36), channel_id=1, source_target_pairs={{0,6},{2,8},{4,10},{6,12},{8,14},{10,0},{12,2},{14,4},{1,7},{3,9},... | collective-permute-start | bytes 294920 | tf_op jit(solution)/shard_map/ppermute | solution.py:442
  93.8 16.1 %collective-permute-start.13 = (bf16[128,384]{1,0:T(8,128)(2,1)}, bf16[128,384]{1,0:T(8,128)(2,1)S(1)}, u32[]{:S(2)}, u32[]{:S(2)}) collective-permute-start(bf16[128,384]{1,0:T(8,128)(2,1)} %get-tuple-element.37), channel_id=1, source_target_pairs={{0,4},{2,6},{4,8},{6,10},{8,12},{10,14},{12,0},{14,2},{1,5},{3,7},... | collective-permute-start | bytes 294920 | tf_op jit(solution)/shard_map/ppermute | solution.py:442
  96.0 13.9 %collective-permute-start.14 = (bf16[128,384]{1,0:T(8,128)(2,1)}, bf16[128,384]{1,0:T(8,128)(2,1)S(1)}, u32[]{:S(2)}, u32[]{:S(2)}) collective-permute-start(bf16[128,384]{1,0:T(8,128)(2,1)} %get-tuple-element.38), channel_id=1, source_target_pairs={{0,2},{2,4},{4,6},{6,8},{8,10},{10,12},{12,14},{14,0},{1,3},{3,5},... | collective-permute-start | bytes 294920 | tf_op jit(solution)/shard_map/ppermute | solution.py:442
  109.9 0.9 copy-start

commit v4 on v3

--- a/solution.py
+++ b/solution.py
@@ -166,7 +166,7 @@
         return
     kept_ref[...] = settled
     for k in range(spots):
-        t = lax.rem(info_ref[1] + k, spots)
+        t = partner(info_ref[1], k, spots, 1)
         at = [pl.multiple_of(i * half + t * rows, 8) for i in range(tps)]
         outs[1 + k][...] = jnp.concatenate([kept_ref[pl.ds(a, first), :] for a in at], axis=0).astype(BF)
 
@@ -214,6 +214,12 @@
         cost_estimate=pl.CostEstimate(flops=total * 5_000_000, bytes_accessed=total * d * 4, transcendentals=total * 3600),
         name="time_part",
     )(info, first_frame, *extra, visible, tokens, other, *weights)
+
+
+def partner(spot, k, spots, sign):
+    if spots & (spots - 1) == 0:
+        return spot ^ k
+    return (spot + spots + sign * k) % spots
 
 
 def gather_matrix(out_rows, in_rows, source):
@@ -357,7 +363,7 @@
 
     pick = gather_matrix(frames * both, depth, source)
     for k in range(spots):
-        back = lax.rem(info_ref[1] + spots - k, spots)
+        back = partner(info_ref[1], k, spots, -1)
         rows = jnp.concatenate([dense_ref[back], xs[k][...] if n > 1 else xs[0][back]], axis=0)
         moved = dot(pick, rows).astype(BF)
         for f in range(frames):
@@ -372,7 +378,7 @@
                 if len(outs) > 1:
                     outs[k][to, :] = rows
                 else:
-                    outs[0][lax.rem(info_ref[1] + spots - k, spots), to, :] = rows
+                    outs[0][partner(info_ref[1], k, spots, -1), to, :] = rows
 
 
 def frames_part(dense, xs, info, spans, begins, form, frames, block, weights):
@@ -406,7 +412,7 @@
     span = depth // tracks
     pick = gather_matrix(depth, depth, lambda r: (r % span) * tracks + r // span)
     for k in range(spots):
-        t = lax.rem(info_ref[1] + k, spots)
+        t = partner(info_ref[1], k, spots, 1)
         rows = jnp.concatenate([dense_ref[t], xs[k][...]], axis=0)
         at = pl.ds(pl.multiple_of(t * span, span), span)
         out_ref[:, at, :] = dot(pick, rows).astype(BF).reshape(tracks, span, d)
@@ -438,9 +444,10 @@
 
 
 def shift(xs, spots, sign):
-    return [xs[0]] + [
-        lax.ppermute(xs[k], "tracks", [(i, (i + sign * k) % spots) for i in range(spots)]) for k in range(1, spots)
-    ]
+    out = list(xs)
+    for k in [k for p in zip(range(spots // 2, spots), range(spots // 2)) for k in p if k]:
+        out[k] = lax.ppermute(xs[k], "tracks", [(i, partner(i, k, spots, sign)) for i in range(spots)])
+    return out
 
 
 def simple(spots, tokens, first_frame, visible, info, time_weights, virtual_weights):

time: 114 us -> 112 us (0.982)
  starting transfers between devices: 50.9 us -> 43.1 us
  waiting for transfers between devices: 5.78 us -> 11.8 us
    ppermute x14, starting transfers between devices: 33.9 us -> 24.6 us  [shift(): lax.ppermute(xs[k], 'tracks', [(i, partner(i, k, spots, sign)) for i in r...]
    ppermute x14, waiting for transfers between devices: 3.13 us -> 9.18 us  [shift(): lax.ppermute(xs[k], 'tracks', [(i, partner(i, k, spots, sign)) for i in r...]
    all_to_all x3, starting transfers between devices: 16.6 us -> 18.1 us  [exchange(): return lax.all_to_all(x, 'tracks', split_axis=0, concat_axis=0, tiled=True)]
  transfers between devices with their start and end apart: 18 -> 18, of which waited for: 5 -> 4; matrix products, arithmetic and copies ran while one was open for 1% -> 1% of each run, Pallas kernels for 33% -> 33%
where the time goes in v4:
time: 112 us; the launch traced here: 111 us
  Pallas kernels  53 us (47%)
  starting transfers between devices  43.1 us (38%)
  waiting for transfers between devices  11.8 us (11%)
  local copies, waits for them, and re-layouts  2.63 us (2%)
    pallas_call x2, Pallas kernels, time_part(): pl.pallas_call(kernel, out_shape=[jax.ShapeDtypeStruct(s, BF) for s in sh...  27.5 us
    ppermute x14, starting transfers between devices, shift(): lax.ppermute(xs[k], 'tracks', [(i, partner(i, k, spots, sign)) for i in r...  24.6 us
    pallas_call x2, Pallas kernels, frames_part(): pl.pallas_call(functools.partial(frames_kernel, spots, len(shapes), spans...  23.2 us
    all_to_all x3, starting transfers between devices, exchange(): return lax.all_to_all(x, 'tracks', split_axis=0, concat_axis=0, tiled=True)  18.1 us
    ppermute x14, waiting for transfers between devices, shift(): lax.ppermute(xs[k], 'tracks', [(i, partner(i, k, spots, sign)) for i in r...  9.18 us
    ppermute x1, waiting for transfers between devices, swap_cores(): return lax.ppermute(x, 'frames', [(0, 1), (1, 0)])  2.64 us
    unnamed x24, local copies, waits for them, and re-layouts  2.63 us
    pallas_call x1, Pallas kernels, home(): pl.pallas_call(functools.partial(home_kernel, spots), out_shape=jax.Shape...  2.38 us
  transfers between devices with their start and end apart: 18, of which 4 were waited for; matrix products, arithmetic and copies ran while one was open for 1% of the time, Pallas kernels for 33%

profile of v4, /device:TPU:0, one launch (start us, length us, event | category | flops | bytes accessed | tf_op | source)
XLA Modules:
  0.0 111.4 jit_solution(7147127701407077996)
XLA Ops:
  0.0 0.5 collective-permute-start
  0.5 0.6 pad_add_fusion.info_ref
  1.1 2.6 %collective-permute-done.other_ref.refs_2_ = bf16[16,128,384]{2,1,0:T(8,128)(2,1)S(1)} collective-permute-done((bf16[16,128,384]{2,1,0:T(8,128)(2,1)}, bf16[16,128,384]{2,1,0:T(8,128)(2,1)S(1)}, u32[]{:S(2)}, u32[]{:S(2)}) %collective-permute-start) | collective-permute-done | bytes 1572896 | tf_op jit(solution)/shard_map/ppermute | solution.py:443
  3.7 1.1 %copy-done.4 = bf16[16,128,384]{2,1,0:T(8,128)(2,1)} copy-done((bf16[16,128,384]{2,1,0:T(8,128)(2,1)}, bf16[16,128,384]{2,1,0:T(8,128)(2,1)S(1)}, u32[]{:S(2)}) %copy-start.4) | copy-done | bytes 1572888
  4.8 13.7 %time_part.2.after_ref = bf16[8,128,384]{2,1,0:T(8,128)(2,1)} custom-call(s32[2]{0:T(128)} %pad_add_fusion.info_ref, s32[16]{0:T(128)} %first_ref.3, s32[16,256]{1,0:T(8,128)} %refs_0_.3, bf16[16,128,384]{2,1,0:T(8,128)(2,1)} %refs_1_.4, bf16[16,128,384]{2,1,0:T(8,128)(2,1)} %copy-done.4, bf16[384,1152]{1,0:T(8,128)(2,1)} %refs_3_.4, ...), custom_call_target="tpu_custom_call" | custom-call | flops 5120000000 | bytes 1572864 | tf_op jit(solution)/shard_map/time_part/pallas_call | solution.py:201
  18.5 7.2 %all-to-all-start = ((bf16[8,128,384]{2,1,0:T(8,128)(2,1)}), bf16[8,128,384]{2,1,0:T(8,128)(2,1)S(1)}, u32[]{:S(2)}, u32[]{:S(2)}) async-start(bf16[8,128,384]{2,1,0:T(8,128)(2,1)} %time_part.2.after_ref), calls=%async_computation | async-start | bytes 1572864 | tf_op jit(solution)/shard_map/all_to_all | solution.py:439
  25.7 13.8 %time_part.3 = (bf16[8,64,384]{2,1,0:T(8,128)(2,1)}, bf16[64,384]{1,0:T(8,128)(2,1)}, bf16[64,384]{1,0:T(8,128)(2,1)}, bf16[64,384]{1,0:T(8,128)(2,1)}, bf16[64,...) custom-call(s32[2]{0:T(128)} %pad_add_fusion.info_ref, ...), custom_call_target="tpu_custom_call" | custom-call | flops 5120000000 | bytes 1572864 | tf_op jit(solution)/shard_map/time_part/pallas_call | solution.py:201
  39.5 2.1 %collective-permute-start.1 = (bf16[64,384]{1,0:T(8,128)(2,1)}, bf16[64,384]{1,0:T(8,128)(2,1)S(1)}, u32[]{:S(2)}, u32[]{:S(2)}) collective-permute-start(bf16[64,384]{1,0:T(8,128)(2,1)} %get-tuple-element.23), channel_id=1, source_target_pairs={{0,2},{2,0},{4,6},{6,4},{8,10},{10,8},{12,14},{14,12},{1,3},{3,1},... | collective-permute-start | bytes 147464 | tf_op jit(solution)/shard_map/ppermute | solution.py:449
  41.6 1.5 %collective-permute-start.2 = (bf16[64,384]{1,0:T(8,128)(2,1)}, bf16[64,384]{1,0:T(8,128)(2,1)S(1)}, u32[]{:S(2)}, u32[]{:S(2)}) collective-permute-start(bf16[64,384]{1,0:T(8,128)(2,1)} %get-tuple-element.24), channel_id=1, source_target_pairs={{0,4},{2,6},{4,0},{6,2},{8,12},{10,14},{12,8},{14,10},{1,5},{3,7},... | collective-permute-start | bytes 147464 | tf_op jit(solution)/shard_map/ppermute | solution.py:449
  43.1 0.1 collective-permute-start.3
  43.1 2.8 %collective-permute-start.4 = (bf16[64,384]{1,0:T(8,128)(2,1)}, bf16[64,384]{1,0:T(8,128)(2,1)S(1)}, u32[]{:S(2)}, u32[]{:S(2)}) collective-permute-start(bf16[64,384]{1,0:T(8,128)(2,1)} %get-tuple-element.26), channel_id=1, source_target_pairs={{0,8},{2,10},{4,12},{6,14},{8,0},{10,2},{12,4},{14,6},{1,9},{3,11}... | collective-permute-start | bytes 147464 | tf_op jit(solution)/shard_map/ppermute | solution.py:449
  46.0 1.5 %collective-permute-start.5 = (bf16[64,384]{1,0:T(8,128)(2,1)}, bf16[64,384]{1,0:T(8,128)(2,1)S(1)}, u32[]{:S(2)}, u32[]{:S(2)}) collective-permute-start(bf16[64,384]{1,0:T(8,128)(2,1)} %get-tuple-element.27), channel_id=1, source_target_pairs={{0,10},{2,8},{4,14},{6,12},{8,2},{10,0},{12,6},{14,4},{1,11},{3,9}... | collective-permute-start | bytes 147464 | tf_op jit(solution)/shard_map/ppermute | solution.py:449
  47.4 0.0 collective-permute-done.1.refs_1_
  47.5 3.3 %collective-permute-start.6 = (bf16[64,384]{1,0:T(8,128)(2,1)}, bf16[64,384]{1,0:T(8,128)(2,1)S(1)}, u32[]{:S(2)}, u32[]{:S(2)}) collective-permute-start(bf16[64,384]{1,0:T(8,128)(2,1)} %get-tuple-element.28), channel_id=1, source_target_pairs={{0,12},{2,14},{4,8},{6,10},{8,4},{10,6},{12,0},{14,2},{1,13},{3,15... | collective-permute-start | bytes 147464 | tf_op jit(solution)/shard_map/ppermute | solution.py:449
  50.7 0.0 collective-permute-done.2.refs_2_
  50.7 0.1 collective-permute-start.7
  50.8 0.0 all-to-all-done.dense_ref
  50.8 5.9 %all-to-all-start.2 = ((bf16[8,64,384]{2,1,0:T(8,128)(2,1)}), bf16[8,64,384]{2,1,0:T(8,128)(2,1)S(1)}, u32[]{:S(2)}, u32[]{:S(2)}) async-start(bf16[8,64,384]{2,1,0:T(8,128)(2,1)} %get-tuple-element.30), calls=%async_computation.2 | async-start | bytes 786432 | tf_op jit(solution)/shard_map/all_to_all | solution.py:439
  56.7 0.0 collective-permute-done.3.refs_3_
  56.7 0.0 copy-start.7
  56.7 0.0 collective-permute-done.4.refs_4_
  56.8 0.0 copy-start.8
  56.8 0.0 collective-permute-done.5.refs_5_
  56.8 0.0 copy-start.9
  56.8 0.0 collective-permute-done.6.refs_6_
  56.8 1.0 collective-permute-done.7.refs_7_
  57.9 0.6 copy-done.11
  58.4 11.6 %frames_part.2 = bf16[8,128,384]{2,1,0:T(8,128)(2,1)} custom-call(s32[2]{0:T(128)} %pad_add_fusion.info_ref, bf16[8,128,384]{2,1,0:T(8,128)(2,1)} %copy-done.2, bf16[64,384]{1,0:T(8,128)(2,1)} %get-tuple-element.22.refs_0_, bf16[64,384]{1,0:T(8,128)(2,1)} %copy-done.5, bf16[64,384]{1,0:T(8,128)(2,1)} %copy-done.6, bf16[64,384]{1,0:T(8,128)(2,1)} %copy-done.7, ...), custom_call_target="tpu_custom_call" | custom-call | flops 10240000000 | bytes 1572864 | tf_op jit(solution)/shard_map/frames_part/pallas_call | solution.py:392
  70.1 0.0 all-to-all-done.2.refs_0_
  70.1 5.0 %all-to-all-start.1 = ((bf16[8,128,384]{2,1,0:T(8,128)(2,1)}), bf16[8,128,384]{2,1,0:T(8,128)(2,1)S(1)}, u32[]{:S(2)}, u32[]{:S(2)}) async-start(bf16[8,128,384]{2,1,0:T(8,128)(2,1)} %frames_part.2), calls=%async_computation.1 | async-start | bytes 1572864 | tf_op jit(solution)/shard_map/all_to_all | solution.py:439
  75.1 11.6 %frames_part.3 = (bf16[128,384]{1,0:T(8,128)(2,1)}, bf16[128,384]{1,0:T(8,128)(2,1)}, bf16[128,384]{1,0:T(8,128)(2,1)}, bf16[128,384]{1,0:T(8,128)(2,1)}, bf16[1...) custom-call(s32[2]{0:T(128)} %pad_add_fusion.info_ref, ...), custom_call_target="tpu_custom_call" | custom-call | flops 10240000000 | bytes 1572864 | tf_op jit(solution)/shard_map/frames_part/pallas_call | solution.py:392
  86.7 2.0 %collective-permute-start.8 = (bf16[128,384]{1,0:T(8,128)(2,1)}, bf16[128,384]{1,0:T(8,128)(2,1)S(1)}, u32[]{:S(2)}, u32[]{:S(2)}) collective-permute-start(bf16[128,384]{1,0:T(8,128)(2,1)} %get-tuple-element.32), channel_id=1, source_target_pairs={{0,2},{2,0},{4,6},{6,4},{8,10},{10,8},{12,14},{14,12},{1,3},{3,1},... | collective-permute-start | bytes 294920 | tf_op jit(solution)/shard_map/ppermute | solution.py:449
  88.7 1.5 %collective-permute-start.9 = (bf16[128,384]{1,0:T(8,128)(2,1)}, bf16[128,384]{1,0:T(8,128)(2,1)S(1)}, u32[]{:S(2)}, u32[]{:S(2)}) collective-permute-start(bf16[128,384]{1,0:T(8,128)(2,1)} %get-tuple-element.33), channel_id=1, source_target_pairs={{0,4},{2,6},{4,0},{6,2},{8,12},{10,14},{12,8},{14,10},{1,5},{3,7},... | collective-permute-start | bytes 294920 | tf_op jit(solution)/shard_map/ppermute | solution.py:449
  90.1 0.1 collective-permute-start.10
  90.2 2.9 %collective-permute-start.11 = (bf16[128,384]{1,0:T(8,128)(2,1)}, bf16[128,384]{1,0:T(8,128)(2,1)S(1)}, u32[]{:S(2)}, u32[]{:S(2)}) collective-permute-start(bf16[128,384]{1,0:T(8,128)(2,1)} %get-tuple-element.35), channel_id=1, source_target_pairs={{0,8},{2,10},{4,12},{6,14},{8,0},{10,2},{12,4},{14,6},{1,9},{3,11}... | collective-permute-start | bytes 294920 | tf_op jit(solution)/shard_map/ppermute | solution.py:449
  93.1 1.5 %collective-permute-start.12 = (bf16[128,384]{1,0:T(8,128)(2,1)}, bf16[128,384]{1,0:T(8,128)(2,1)S(1)}, u32[]{:S(2)}, u32[]{:S(2)}) collective-permute-start(bf16[128,384]{1,0:T(8,128)(2,1)} %get-tuple-element.36), channel_id=1, source_target_pairs={{0,10},{2,8},{4,14},{6,12},{8,2},{10,0},{12,6},{14,4},{1,11},{3,9}... | collective-permute-start | bytes 294920 | tf_op jit(solution)/shard_map/ppermute | solution.py:449
  94.5 0.0 collective-permute-done.8.refs_1_
  94.5 3.3 %collective-permute-start.13 = (bf16[128,384]{1,0:T(8,128)(2,1)}, bf16[128,384]{1,0:T(8,128)(2,1)S(1)}, u32[]{:S(2)}, u32[]{:S(2)}) collective-permute-start(bf16[128,384]{1,0:T(8,128)(2,1)} %get-tuple-element.37), channel_id=1, source_target_pairs={{0,12},{2,14},{4,8},{6,10},{8,4},{10,6},{12,0},{14,2},{1,13},{3,15... | collective-permute-start | bytes 294920 | tf_op jit(solution)/shard_map/ppermute | solution.py:449
  97.8 0.0 collective-permute-done.9.refs_2_
  97.8 2.1 %collective-permute-start.14 = (bf16[128,384]{1,0:T(8,128)(2,1)}, bf16[128,384]{1,0:T(8,128)(2,1)S(1)}, u32[]{:S(2)}, u32[]{:S(2)}) collective-permute-start(bf16[128,384]{1,0:T(8,128)(2,1)} %get-tuple-element.38), channel_id=1, source_target_pairs={{0,14},{2,12},{4,10},{6,8},{8,6},{10,4},{12,2},{14,0},{1,15},{3,13... | collective-permute-start | bytes 294920 | tf_op jit(solution)/shard_map/ppermute | solution.py:449
  99.9 0.0 collective-permute-done.10.refs_3_
  99.9 5.8 %collective-permute-done.11.refs_4_ = bf16[128,384]{1,0:T(8,128)(2,1)S(1)} collective-permute-done((bf16[128,384]{1,0:T(8,128)(2,1)}, bf16[128,384]{1,0:T(8,128)(2,1)S(1)}, u32[]{:S(2)}, u32[]{:S(2)}) %collective-permute-start.11) | collective-permute-done | bytes 98336 | tf_op jit(solution)/shard_map/ppermute | solution.py:449
  105.7 2.3 %collective-permute-done.12.refs_5_ = bf16[128,384]{1,0:T(8,128)(2,1)S(1)} collective-permute-done((bf16[128,384]{1,0:T(8,128)(2,1)}, bf16[128,384]{1,0:T(8,128)(2,1)S(1)}, u32[]{:S(2)}, u32[]{:S(2)}) %collective-permute-start.12) | collective-permute-done | bytes 98336 | tf_op jit(solution)/shard_map/ppermute | solution.py:449
  108.1 0.0 collective-permute-done.13.refs_6_
  108.1 0.0 collective-permute-done.14.refs_7_
  108.1 0.0 all-to-all-done.1.dense_ref
  108.1 0.9 copy-done
  109.0 2.4 %home.1 = bf16[16,128,384]{2,1,0:T(8,128)(2,1)} custom-call(s32[2]{0:T(128)S(1)} %copy-done.1, bf16[8,128,384]{2,1,0:T(8,128)(2,1)S(1)} %all-to-all-done.1.dense_ref, bf16[128,384]{1,0:T(8,128)(2,1)S(1)} %copy-done, bf16[128,384]{1,0:T(8,128)(2,1)S(1)} %collective-permute-done.8.refs_1_, bf16[128,384]{1,0:T(8,128)(2,1)S(1)} %collective-permute-done.9.refs_2_, ...), custom_call_target="tpu_custom_call" | custom-call | tf_op jit(solution)/shard_map/home/pallas_call | solution.py:424
  (18 shorter events, 0.0 us)
Async XLA Ops:
  0.0 3.7 %collective-permute-start = (bf16[16,128,384]{2,1,0:T(8,128)(2,1)}, bf16[16,128,384]{2,1,0:T(8,128)(2,1)S(1)}, u32[]{:S(2)}, u32[]{:S(2)}) collective-permute-start(bf16[16,128,384]{2,1,0:T(8,128)(2,1)} %refs_1_.4), channel_id=1, source_target_pairs={{0,1},{1,0},{2,3},{3,2},{4,5},{5,4},{6,7},{7,6},{8,9},{9,8},{10,11... | collective-permute-start | bytes 4718600 | tf_op jit(solution)/shard_map/ppermute | solution.py:443
  3.7 1.1 %copy-start.4 = (bf16[16,128,384]{2,1,0:T(8,128)(2,1)}, bf16[16,128,384]{2,1,0:T(8,128)(2,1)S(1)}, u32[]{:S(2)}) copy-start(bf16[16,128,384]{2,1,0:T(8,128)(2,1)S(1)} %collective-permute-done.other_ref.refs_2_) | copy-start | bytes 4718596
  18.5 32.3 %all-to-all-start = ((bf16[8,128,384]{2,1,0:T(8,128)(2,1)}), bf16[8,128,384]{2,1,0:T(8,128)(2,1)S(1)}, u32[]{:S(2)}, u32[]{:S(2)}) async-start(bf16[8,128,384]{2,1,0:T(8,128)(2,1)} %time_part.2.after_ref), calls=%async_computation | async-start | bytes 1572864 | tf_op jit(solution)/shard_map/all_to_all | solution.py:439
  39.5 7.9 %collective-permute-start.1 = (bf16[64,384]{1,0:T(8,128)(2,1)}, bf16[64,384]{1,0:T(8,128)(2,1)S(1)}, u32[]{:S(2)}, u32[]{:S(2)}) collective-permute-start(bf16[64,384]{1,0:T(8,128)(2,1)} %get-tuple-element.23), channel_id=1, source_target_pairs={{0,2},{2,0},{4,6},{6,4},{8,10},{10,8},{12,14},{14,12},{1,3},{3,1},... | collective-permute-start | bytes 147464 | tf_op jit(solution)/shard_map/ppermute | solution.py:449
  41.6 9.1 %collective-permute-start.2 = (bf16[64,384]{1,0:T(8,128)(2,1)}, bf16[64,384]{1,0:T(8,128)(2,1)S(1)}, u32[]{:S(2)}, u32[]{:S(2)}) collective-permute-start(bf16[64,384]{1,0:T(8,128)(2,1)} %get-tuple-element.24), channel_id=1, source_target_pairs={{0,4},{2,6},{4,0},{6,2},{8,12},{10,14},{12,8},{14,10},{1,5},{3,7},... | collective-permute-start | bytes 147464 | tf_op jit(solution)/shard_map/ppermute | solution.py:449
  43.1 13.7 %collective-permute-start.3 = (bf16[64,384]{1,0:T(8,128)(2,1)}, bf16[64,384]{1,0:T(8,128)(2,1)S(1)}, u32[]{:S(2)}, u32[]{:S(2)}) collective-permute-start(bf16[64,384]{1,0:T(8,128)(2,1)} %get-tuple-element.25), channel_id=1, source_target_pairs={{0,6},{2,4},{4,2},{6,0},{8,14},{10,12},{12,10},{14,8},{1,7},{3,5},... | collective-permute-start | bytes 147464 | tf_op jit(solution)/shard_map/ppermute | solution.py:449
  43.1 13.6 %collective-permute-start.4 = (bf16[64,384]{1,0:T(8,128)(2,1)}, bf16[64,384]{1,0:T(8,128)(2,1)S(1)}, u32[]{:S(2)}, u32[]{:S(2)}) collective-permute-start(bf16[64,384]{1,0:T(8,128)(2,1)} %get-tuple-element.26), channel_id=1, source_target_pairs={{0,8},{2,10},{4,12},{6,14},{8,0},{10,2},{12,4},{14,6},{1,9},{3,11}... | collective-permute-start | bytes 147464 | tf_op jit(solution)/shard_map/ppermute | solution.py:449
  46.0 10.8 %collective-permute-start.5 = (bf16[64,384]{1,0:T(8,128)(2,1)}, bf16[64,384]{1,0:T(8,128)(2,1)S(1)}, u32[]{:S(2)}, u32[]{:S(2)}) collective-permute-start(bf16[64,384]{1,0:T(8,128)(2,1)} %get-tuple-element.27), channel_id=1, source_target_pairs={{0,10},{2,8},{4,14},{6,12},{8,2},{10,0},{12,6},{14,4},{1,11},{3,9}... | collective-permute-start | bytes 147464 | tf_op jit(solution)/shard_map/ppermute | solution.py:449
  47.4 10.4 %copy-start.5 = (bf16[64,384]{1,0:T(8,128)(2,1)}, bf16[64,384]{1,0:T(8,128)(2,1)S(1)}, u32[]{:S(2)}) copy-start(bf16[64,384]{1,0:T(8,128)(2,1)S(1)} %collective-permute-done.1.refs_1_) | copy-start | bytes 147460
  47.5 9.3 %collective-permute-start.6 = (bf16[64,384]{1,0:T(8,128)(2,1)}, bf16[64,384]{1,0:T(8,128)(2,1)S(1)}, u32[]{:S(2)}, u32[]{:S(2)}) collective-permute-start(bf16[64,384]{1,0:T(8,128)(2,1)} %get-tuple-element.28), channel_id=1, source_target_pairs={{0,12},{2,14},{4,8},{6,10},{8,4},{10,6},{12,0},{14,2},{1,13},{3,15... | collective-permute-start | bytes 147464 | tf_op jit(solution)/shard_map/ppermute | solution.py:449
  50.7 7.1 %copy-start.6 = (bf16[64,384]{1,0:T(8,128)(2,1)}, bf16[64,384]{1,0:T(8,128)(2,1)S(1)}, u32[]{:S(2)}) copy-start(bf16[64,384]{1,0:T(8,128)(2,1)S(1)} %collective-permute-done.2.refs_2_) | copy-start | bytes 147460
  50.7 7.1 %collective-permute-start.7 = (bf16[64,384]{1,0:T(8,128)(2,1)}, bf16[64,384]{1,0:T(8,128)(2,1)S(1)}, u32[]{:S(2)}, u32[]{:S(2)}) collective-permute-start(bf16[64,384]{1,0:T(8,128)(2,1)} %get-tuple-element.29), channel_id=1, source_target_pairs={{0,14},{2,12},{4,10},{6,8},{8,6},{10,4},{12,2},{14,0},{1,15},{3,13... | collective-permute-start | bytes 147464 | tf_op jit(solution)/shard_map/ppermute | solution.py:449
  50.8 7.0 %copy-start.2 = (bf16[8,128,384]{2,1,0:T(8,128)(2,1)}, bf16[8,128,384]{2,1,0:T(8,128)(2,1)S(1)}, u32[]{:S(2)}) copy-start(bf16[8,128,384]{2,1,0:T(8,128)(2,1)S(1)} %all-to-all-done.dense_ref) | copy-start | bytes 2359300
  50.8 19.2 %all-to-all-start.2 = ((bf16[8,64,384]{2,1,0:T(8,128)(2,1)}), bf16[8,64,384]{2,1,0:T(8,128)(2,1)S(1)}, u32[]{:S(2)}, u32[]{:S(2)}) async-start(bf16[8,64,384]{2,1,0:T(8,128)(2,1)} %get-tuple-element.30), calls=%async_computation.2 | async-start | bytes 786432 | tf_op jit(solution)/shard_map/all_to_all | solution.py:439
  56.7 1.1 copy-start.7
  56.8 1.1 copy-start.8
  56.8 1.1 copy-start.9
  56.8 1.1 copy-start.10
  57.8 0.6 copy-start.11
  70.1 5.0 %copy-start.3 = (bf16[8,64,384]{2,1,0:T(8,128)(2,1)}, bf16[8,64,384]{2,1,0:T(8,128)(2,1)S(1)}, u32[]{:S(2)}) copy-start(bf16[8,64,384]{2,1,0:T(8,128)(2,1)S(1)} %all-to-all-done.2.refs_0_) | copy-start | bytes 1179652
  70.1 38.0 %all-to-all-start.1 = ((bf16[8,128,384]{2,1,0:T(8,128)(2,1)}), bf16[8,128,384]{2,1,0:T(8,128)(2,1)S(1)}, u32[]{:S(2)}, u32[]{:S(2)}) async-start(bf16[8,128,384]{2,1,0:T(8,128)(2,1)} %frames_part.2), calls=%async_computation.1 | async-start | bytes 1572864 | tf_op jit(solution)/shard_map/all_to_all | solution.py:439
  75.1 33.0 %copy-start.1 = (s32[2]{0:T(128)S(1)}, s32[2]{0:T(128)}, u32[]{:S(2)}) copy-start(s32[2]{0:T(128)} %pad_add_fusion.info_ref) | copy-start | bytes 28
  86.7 7.9 %collective-permute-start.8 = (bf16[128,384]{1,0:T(8,128)(2,1)}, bf16[128,384]{1,0:T(8,128)(2,1)S(1)}, u32[]{:S(2)}, u32[]{:S(2)}) collective-permute-start(bf16[128,384]{1,0:T(8,128)(2,1)} %get-tuple-element.32), channel_id=1, source_target_pairs={{0,2},{2,0},{4,6},{6,4},{8,10},{10,8},{12,14},{14,12},{1,3},{3,1},... | collective-permute-start | bytes 294920 | tf_op jit(solution)/shard_map/ppermute | solution.py:449
  88.7 9.1 %collective-permute-start.9 = (bf16[128,384]{1,0:T(8,128)(2,1)}, bf16[128,384]{1,0:T(8,128)(2,1)S(1)}, u32[]{:S(2)}, u32[]{:S(2)}) collective-permute-start(bf16[128,384]{1,0:T(8,128)(2,1)} %get-tuple-element.33), channel_id=1, source_target_pairs={{0,4},{2,6},{4,0},{6,2},{8,12},{10,14},{12,8},{14,10},{1,5},{3,7},... | collective-permute-start | bytes 294920 | tf_op jit(solution)/shard_map/ppermute | solution.py:449
  90.1 9.8 %collective-permute-start.10 = (bf16[128,384]{1,0:T(8,128)(2,1)}, bf16[128,384]{1,0:T(8,128)(2,1)S(1)}, u32[]{:S(2)}, u32[]{:S(2)}) collective-permute-start(bf16[128,384]{1,0:T(8,128)(2,1)} %get-tuple-element.34), channel_id=1, source_target_pairs={{0,6},{2,4},{4,2},{6,0},{8,14},{10,12},{12,10},{14,8},{1,7},{3,5},... | collective-permute-start | bytes 294920 | tf_op jit(solution)/shard_map/ppermute | solution.py:449
  90.2 15.5 %collective-permute-start.11 = (bf16[128,384]{1,0:T(8,128)(2,1)}, bf16[128,384]{1,0:T(8,128)(2,1)S(1)}, u32[]{:S(2)}, u32[]{:S(2)}) collective-permute-start(bf16[128,384]{1,0:T(8,128)(2,1)} %get-tuple-element.35), channel_id=1, source_target_pairs={{0,8},{2,10},{4,12},{6,14},{8,0},{10,2},{12,4},{14,6},{1,9},{3,11}... | collective-permute-start | bytes 294920 | tf_op jit(solution)/shard_map/ppermute | solution.py:449
  93.1 15.0 %collective-permute-start.12 = (bf16[128,384]{1,0:T(8,128)(2,1)}, bf16[128,384]{1,0:T(8,128)(2,1)S(1)}, u32[]{:S(2)}, u32[]{:S(2)}) collective-permute-start(bf16[128,384]{1,0:T(8,128)(2,1)} %get-tuple-element.36), channel_id=1, source_target_pairs={{0,10},{2,8},{4,14},{6,12},{8,2},{10,0},{12,6},{14,4},{1,11},{3,9}... | collective-permute-start | bytes 294920 | tf_op jit(solution)/shard_map/ppermute | solution.py:449
  94.5 13.6 %collective-permute-start.13 = (bf16[128,384]{1,0:T(8,128)(2,1)}, bf16[128,384]{1,0:T(8,128)(2,1)S(1)}, u32[]{:S(2)}, u32[]{:S(2)}) collective-permute-start(bf16[128,384]{1,0:T(8,128)(2,1)} %get-tuple-element.37), channel_id=1, source_target_pairs={{0,12},{2,14},{4,8},{6,10},{8,4},{10,6},{12,0},{14,2},{1,13},{3,15... | collective-permute-start | bytes 294920 | tf_op jit(solution)/shard_map/ppermute | solution.py:449
  97.8 10.3 %collective-permute-start.14 = (bf16[128,384]{1,0:T(8,128)(2,1)}, bf16[128,384]{1,0:T(8,128)(2,1)S(1)}, u32[]{:S(2)}, u32[]{:S(2)}) collective-permute-start(bf16[128,384]{1,0:T(8,128)(2,1)} %get-tuple-element.38), channel_id=1, source_target_pairs={{0,14},{2,12},{4,10},{6,8},{8,6},{10,4},{12,2},{14,0},{1,15},{3,13... | collective-permute-start | bytes 294920 | tf_op jit(solution)/shard_map/ppermute | solution.py:449
  108.1 0.9 copy-start

commit v5 on v4

--- a/solution.py
+++ b/solution.py
@@ -178,7 +178,7 @@
 def time_part(tokens, other, first_frame, visible, info, weights, spots, form, first, begin, count, after):
     _, half, d = tokens.shape
     rows = half // spots
-    tps = 4
+    tps = 8 if form == "dense" and count % 8 == 0 else 4
     if form == "tracks":
         shapes, blocks = [(count, half, d)], [pl.BlockSpec((tps, half, d), lambda i, *_: (i, 0, 0))]
     else:

time: 112 us -> 112 us (level)
  no operation moved by 1% of the time
where the time goes in v5:
time: 112 us; the launch traced here: 111 us
  Pallas kernels  52.7 us (47%)
  starting transfers between devices  43.1 us (38%)
  waiting for transfers between devices  11.9 us (11%)
  local copies, waits for them, and re-layouts  2.63 us (2%)
    pallas_call x2, Pallas kernels, time_part(): pl.pallas_call(kernel, out_shape=[jax.ShapeDtypeStruct(s, BF) for s in sh...  27.1 us
    ppermute x14, starting transfers between devices, shift(): lax.ppermute(xs[k], 'tracks', [(i, partner(i, k, spots, sign)) for i in r...  24.5 us
    pallas_call x2, Pallas kernels, frames_part(): pl.pallas_call(functools.partial(frames_kernel, spots, len(shapes), spans...  23.2 us
    all_to_all x3, starting transfers between devices, exchange(): return lax.all_to_all(x, 'tracks', split_axis=0, concat_axis=0, tiled=True)  18.1 us
    ppermute x14, waiting for transfers between devices, shift(): lax.ppermute(xs[k], 'tracks', [(i, partner(i, k, spots, sign)) for i in r...  9.23 us
    ppermute x1, waiting for transfers between devices, swap_cores(): return lax.ppermute(x, 'frames', [(0, 1), (1, 0)])  2.64 us
    unnamed x24, local copies, waits for them, and re-layouts  2.63 us
    pallas_call x1, Pallas kernels, home(): pl.pallas_call(functools.partial(home_kernel, spots), out_shape=jax.Shape...  2.38 us
  transfers between devices with their start and end apart: 18, of which 4 were waited for; matrix products, arithmetic and copies ran while one was open for 1% of the time, Pallas kernels for 33%

profile of v5, /device:TPU:0, one launch (start us, length us, event | category | flops | bytes accessed | tf_op | source)
XLA Modules:
  0.0 111.1 jit_solution(16370882987296522195)
XLA Ops:
  0.0 0.5 collective-permute-start
  0.5 0.6 pad_add_fusion.info_ref
  1.1 2.6 %collective-permute-done.other_ref.refs_2_ = bf16[16,128,384]{2,1,0:T(8,128)(2,1)S(1)} collective-permute-done((bf16[16,128,384]{2,1,0:T(8,128)(2,1)}, bf16[16,128,384]{2,1,0:T(8,128)(2,1)S(1)}, u32[]{:S(2)}, u32[]{:S(2)}) %collective-permute-start) | collective-permute-done | bytes 1572896 | tf_op jit(solution)/shard_map/ppermute | solution.py:443
  3.7 1.1 %copy-done.4 = bf16[16,128,384]{2,1,0:T(8,128)(2,1)} copy-done((bf16[16,128,384]{2,1,0:T(8,128)(2,1)}, bf16[16,128,384]{2,1,0:T(8,128)(2,1)S(1)}, u32[]{:S(2)}) %copy-start.4) | copy-done | bytes 1572888
  4.8 13.4 %time_part.2.after_ref = bf16[8,128,384]{2,1,0:T(8,128)(2,1)} custom-call(s32[2]{0:T(128)} %pad_add_fusion.info_ref, s32[16]{0:T(128)} %first_ref.3, s32[16,256]{1,0:T(8,128)} %refs_0_.3, bf16[16,128,384]{2,1,0:T(8,128)(2,1)} %refs_1_.4, bf16[16,128,384]{2,1,0:T(8,128)(2,1)} %copy-done.4, bf16[384,1152]{1,0:T(8,128)(2,1)} %refs_3_.4, ...), custom_call_target="tpu_custom_call" | custom-call | flops 5120000000 | bytes 1572864 | tf_op jit(solution)/shard_map/time_part/pallas_call | solution.py:201
  18.2 7.2 %all-to-all-start = ((bf16[8,128,384]{2,1,0:T(8,128)(2,1)}), bf16[8,128,384]{2,1,0:T(8,128)(2,1)S(1)}, u32[]{:S(2)}, u32[]{:S(2)}) async-start(bf16[8,128,384]{2,1,0:T(8,128)(2,1)} %time_part.2.after_ref), calls=%async_computation | async-start | bytes 1572864 | tf_op jit(solution)/shard_map/all_to_all | solution.py:439
  25.4 13.8 %time_part.3 = (bf16[8,64,384]{2,1,0:T(8,128)(2,1)}, bf16[64,384]{1,0:T(8,128)(2,1)}, bf16[64,384]{1,0:T(8,128)(2,1)}, bf16[64,384]{1,0:T(8,128)(2,1)}, bf16[64,...) custom-call(s32[2]{0:T(128)} %pad_add_fusion.info_ref, ...), custom_call_target="tpu_custom_call" | custom-call | flops 5120000000 | bytes 1572864 | tf_op jit(solution)/shard_map/time_part/pallas_call | solution.py:201
  39.2 2.1 %collective-permute-start.1 = (bf16[64,384]{1,0:T(8,128)(2,1)}, bf16[64,384]{1,0:T(8,128)(2,1)S(1)}, u32[]{:S(2)}, u32[]{:S(2)}) collective-permute-start(bf16[64,384]{1,0:T(8,128)(2,1)} %get-tuple-element.23), channel_id=1, source_target_pairs={{0,2},{2,0},{4,6},{6,4},{8,10},{10,8},{12,14},{14,12},{1,3},{3,1},... | collective-permute-start | bytes 147464 | tf_op jit(solution)/shard_map/ppermute | solution.py:449
  41.3 1.5 %collective-permute-start.2 = (bf16[64,384]{1,0:T(8,128)(2,1)}, bf16[64,384]{1,0:T(8,128)(2,1)S(1)}, u32[]{:S(2)}, u32[]{:S(2)}) collective-permute-start(bf16[64,384]{1,0:T(8,128)(2,1)} %get-tuple-element.24), channel_id=1, source_target_pairs={{0,4},{2,6},{4,0},{6,2},{8,12},{10,14},{12,8},{14,10},{1,5},{3,7},... | collective-permute-start | bytes 147464 | tf_op jit(solution)/shard_map/ppermute | solution.py:449
  42.7 0.1 collective-permute-start.3
  42.8 2.9 %collective-permute-start.4 = (bf16[64,384]{1,0:T(8,128)(2,1)}, bf16[64,384]{1,0:T(8,128)(2,1)S(1)}, u32[]{:S(2)}, u32[]{:S(2)}) collective-permute-start(bf16[64,384]{1,0:T(8,128)(2,1)} %get-tuple-element.26), channel_id=1, source_target_pairs={{0,8},{2,10},{4,12},{6,14},{8,0},{10,2},{12,4},{14,6},{1,9},{3,11}... | collective-permute-start | bytes 147464 | tf_op jit(solution)/shard_map/ppermute | solution.py:449
  45.7 1.4 %collective-permute-start.5 = (bf16[64,384]{1,0:T(8,128)(2,1)}, bf16[64,384]{1,0:T(8,128)(2,1)S(1)}, u32[]{:S(2)}, u32[]{:S(2)}) collective-permute-start(bf16[64,384]{1,0:T(8,128)(2,1)} %get-tuple-element.27), channel_id=1, source_target_pairs={{0,10},{2,8},{4,14},{6,12},{8,2},{10,0},{12,6},{14,4},{1,11},{3,9}... | collective-permute-start | bytes 147464 | tf_op jit(solution)/shard_map/ppermute | solution.py:449
  47.1 0.0 collective-permute-done.1.refs_1_
  47.1 3.3 %collective-permute-start.6 = (bf16[64,384]{1,0:T(8,128)(2,1)}, bf16[64,384]{1,0:T(8,128)(2,1)S(1)}, u32[]{:S(2)}, u32[]{:S(2)}) collective-permute-start(bf16[64,384]{1,0:T(8,128)(2,1)} %get-tuple-element.28), channel_id=1, source_target_pairs={{0,12},{2,14},{4,8},{6,10},{8,4},{10,6},{12,0},{14,2},{1,13},{3,15... | collective-permute-start | bytes 147464 | tf_op jit(solution)/shard_map/ppermute | solution.py:449
  50.4 0.0 collective-permute-done.2.refs_2_
  50.4 0.1 collective-permute-start.7
  50.5 0.0 all-to-all-done.dense_ref
  50.5 5.9 %all-to-all-start.2 = ((bf16[8,64,384]{2,1,0:T(8,128)(2,1)}), bf16[8,64,384]{2,1,0:T(8,128)(2,1)S(1)}, u32[]{:S(2)}, u32[]{:S(2)}) async-start(bf16[8,64,384]{2,1,0:T(8,128)(2,1)} %get-tuple-element.30), calls=%async_computation.2 | async-start | bytes 786432 | tf_op jit(solution)/shard_map/all_to_all | solution.py:439
  56.4 0.0 collective-permute-done.3.refs_3_
  56.4 0.0 copy-start.7
  56.4 0.0 collective-permute-done.4.refs_4_
  56.4 0.0 copy-start.8
  56.4 0.0 collective-permute-done.5.refs_5_
  56.5 0.0 copy-start.9
  56.5 0.0 collective-permute-done.6.refs_6_
  56.5 1.0 collective-permute-done.7.refs_7_
  57.6 0.6 copy-done.11
  58.1 11.6 %frames_part.2 = bf16[8,128,384]{2,1,0:T(8,128)(2,1)} custom-call(s32[2]{0:T(128)} %pad_add_fusion.info_ref, bf16[8,128,384]{2,1,0:T(8,128)(2,1)} %copy-done.2, bf16[64,384]{1,0:T(8,128)(2,1)} %get-tuple-element.22.refs_0_, bf16[64,384]{1,0:T(8,128)(2,1)} %copy-done.5, bf16[64,384]{1,0:T(8,128)(2,1)} %copy-done.6, bf16[64,384]{1,0:T(8,128)(2,1)} %copy-done.7, ...), custom_call_target="tpu_custom_call" | custom-call | flops 10240000000 | bytes 1572864 | tf_op jit(solution)/shard_map/frames_part/pallas_call | solution.py:392
  69.7 0.0 all-to-all-done.2.refs_0_
  69.8 5.0 %all-to-all-start.1 = ((bf16[8,128,384]{2,1,0:T(8,128)(2,1)}), bf16[8,128,384]{2,1,0:T(8,128)(2,1)S(1)}, u32[]{:S(2)}, u32[]{:S(2)}) async-start(bf16[8,128,384]{2,1,0:T(8,128)(2,1)} %frames_part.2), calls=%async_computation.1 | async-start | bytes 1572864 | tf_op jit(solution)/shard_map/all_to_all | solution.py:439
  74.8 11.6 %frames_part.3 = (bf16[128,384]{1,0:T(8,128)(2,1)}, bf16[128,384]{1,0:T(8,128)(2,1)}, bf16[128,384]{1,0:T(8,128)(2,1)}, bf16[128,384]{1,0:T(8,128)(2,1)}, bf16[1...) custom-call(s32[2]{0:T(128)} %pad_add_fusion.info_ref, ...), custom_call_target="tpu_custom_call" | custom-call | flops 10240000000 | bytes 1572864 | tf_op jit(solution)/shard_map/frames_part/pallas_call | solution.py:392
  86.3 2.0 %collective-permute-start.8 = (bf16[128,384]{1,0:T(8,128)(2,1)}, bf16[128,384]{1,0:T(8,128)(2,1)S(1)}, u32[]{:S(2)}, u32[]{:S(2)}) collective-permute-start(bf16[128,384]{1,0:T(8,128)(2,1)} %get-tuple-element.32), channel_id=1, source_target_pairs={{0,2},{2,0},{4,6},{6,4},{8,10},{10,8},{12,14},{14,12},{1,3},{3,1},... | collective-permute-start | bytes 294920 | tf_op jit(solution)/shard_map/ppermute | solution.py:449
  88.4 1.5 %collective-permute-start.9 = (bf16[128,384]{1,0:T(8,128)(2,1)}, bf16[128,384]{1,0:T(8,128)(2,1)S(1)}, u32[]{:S(2)}, u32[]{:S(2)}) collective-permute-start(bf16[128,384]{1,0:T(8,128)(2,1)} %get-tuple-element.33), channel_id=1, source_target_pairs={{0,4},{2,6},{4,0},{6,2},{8,12},{10,14},{12,8},{14,10},{1,5},{3,7},... | collective-permute-start | bytes 294920 | tf_op jit(solution)/shard_map/ppermute | solution.py:449
  89.8 0.1 collective-permute-start.10
  89.9 2.9 %collective-permute-start.11 = (bf16[128,384]{1,0:T(8,128)(2,1)}, bf16[128,384]{1,0:T(8,128)(2,1)S(1)}, u32[]{:S(2)}, u32[]{:S(2)}) collective-permute-start(bf16[128,384]{1,0:T(8,128)(2,1)} %get-tuple-element.35), channel_id=1, source_target_pairs={{0,8},{2,10},{4,12},{6,14},{8,0},{10,2},{12,4},{14,6},{1,9},{3,11}... | collective-permute-start | bytes 294920 | tf_op jit(solution)/shard_map/ppermute | solution.py:449
  92.7 1.5 %collective-permute-start.12 = (bf16[128,384]{1,0:T(8,128)(2,1)}, bf16[128,384]{1,0:T(8,128)(2,1)S(1)}, u32[]{:S(2)}, u32[]{:S(2)}) collective-permute-start(bf16[128,384]{1,0:T(8,128)(2,1)} %get-tuple-element.36), channel_id=1, source_target_pairs={{0,10},{2,8},{4,14},{6,12},{8,2},{10,0},{12,6},{14,4},{1,11},{3,9}... | collective-permute-start | bytes 294920 | tf_op jit(solution)/shard_map/ppermute | solution.py:449
  94.2 0.0 collective-permute-done.8.refs_1_
  94.2 3.3 %collective-permute-start.13 = (bf16[128,384]{1,0:T(8,128)(2,1)}, bf16[128,384]{1,0:T(8,128)(2,1)S(1)}, u32[]{:S(2)}, u32[]{:S(2)}) collective-permute-start(bf16[128,384]{1,0:T(8,128)(2,1)} %get-tuple-element.37), channel_id=1, source_target_pairs={{0,12},{2,14},{4,8},{6,10},{8,4},{10,6},{12,0},{14,2},{1,13},{3,15... | collective-permute-start | bytes 294920 | tf_op jit(solution)/shard_map/ppermute | solution.py:449
  97.5 0.0 collective-permute-done.9.refs_2_
  97.5 2.1 %collective-permute-start.14 = (bf16[128,384]{1,0:T(8,128)(2,1)}, bf16[128,384]{1,0:T(8,128)(2,1)S(1)}, u32[]{:S(2)}, u32[]{:S(2)}) collective-permute-start(bf16[128,384]{1,0:T(8,128)(2,1)} %get-tuple-element.38), channel_id=1, source_target_pairs={{0,14},{2,12},{4,10},{6,8},{8,6},{10,4},{12,2},{14,0},{1,15},{3,13... | collective-permute-start | bytes 294920 | tf_op jit(solution)/shard_map/ppermute | solution.py:449
  99.6 0.0 collective-permute-done.10.refs_3_
  99.6 5.8 %collective-permute-done.11.refs_4_ = bf16[128,384]{1,0:T(8,128)(2,1)S(1)} collective-permute-done((bf16[128,384]{1,0:T(8,128)(2,1)}, bf16[128,384]{1,0:T(8,128)(2,1)S(1)}, u32[]{:S(2)}, u32[]{:S(2)}) %collective-permute-start.11) | collective-permute-done | bytes 98336 | tf_op jit(solution)/shard_map/ppermute | solution.py:449
  105.4 2.3 %collective-permute-done.12.refs_5_ = bf16[128,384]{1,0:T(8,128)(2,1)S(1)} collective-permute-done((bf16[128,384]{1,0:T(8,128)(2,1)}, bf16[128,384]{1,0:T(8,128)(2,1)S(1)}, u32[]{:S(2)}, u32[]{:S(2)}) %collective-permute-start.12) | collective-permute-done | bytes 98336 | tf_op jit(solution)/shard_map/ppermute | solution.py:449
  107.8 0.0 collective-permute-done.13.refs_6_
  107.8 0.0 collective-permute-done.14.refs_7_
  107.8 0.0 all-to-all-done.1.dense_ref
  107.8 0.9 copy-done
  108.7 2.4 %home.1 = bf16[16,128,384]{2,1,0:T(8,128)(2,1)} custom-call(s32[2]{0:T(128)S(1)} %copy-done.1, bf16[8,128,384]{2,1,0:T(8,128)(2,1)S(1)} %all-to-all-done.1.dense_ref, bf16[128,384]{1,0:T(8,128)(2,1)S(1)} %copy-done, bf16[128,384]{1,0:T(8,128)(2,1)S(1)} %collective-permute-done.8.refs_1_, bf16[128,384]{1,0:T(8,128)(2,1)S(1)} %collective-permute-done.9.refs_2_, ...), custom_call_target="tpu_custom_call" | custom-call | tf_op jit(solution)/shard_map/home/pallas_call | solution.py:424
  (18 shorter events, 0.0 us)
Async XLA Ops:
  0.0 3.7 %collective-permute-start = (bf16[16,128,384]{2,1,0:T(8,128)(2,1)}, bf16[16,128,384]{2,1,0:T(8,128)(2,1)S(1)}, u32[]{:S(2)}, u32[]{:S(2)}) collective-permute-start(bf16[16,128,384]{2,1,0:T(8,128)(2,1)} %refs_1_.4), channel_id=1, source_target_pairs={{0,1},{1,0},{2,3},{3,2},{4,5},{5,4},{6,7},{7,6},{8,9},{9,8},{10,11... | collective-permute-start | bytes 4718600 | tf_op jit(solution)/shard_map/ppermute | solution.py:443
  3.7 1.1 %copy-start.4 = (bf16[16,128,384]{2,1,0:T(8,128)(2,1)}, bf16[16,128,384]{2,1,0:T(8,128)(2,1)S(1)}, u32[]{:S(2)}) copy-start(bf16[16,128,384]{2,1,0:T(8,128)(2,1)S(1)} %collective-permute-done.other_ref.refs_2_) | copy-start | bytes 4718596
  18.2 32.3 %all-to-all-start = ((bf16[8,128,384]{2,1,0:T(8,128)(2,1)}), bf16[8,128,384]{2,1,0:T(8,128)(2,1)S(1)}, u32[]{:S(2)}, u32[]{:S(2)}) async-start(bf16[8,128,384]{2,1,0:T(8,128)(2,1)} %time_part.2.after_ref), calls=%async_computation | async-start | bytes 1572864 | tf_op jit(solution)/shard_map/all_to_all | solution.py:439
  39.2 7.9 %collective-permute-start.1 = (bf16[64,384]{1,0:T(8,128)(2,1)}, bf16[64,384]{1,0:T(8,128)(2,1)S(1)}, u32[]{:S(2)}, u32[]{:S(2)}) collective-permute-start(bf16[64,384]{1,0:T(8,128)(2,1)} %get-tuple-element.23), channel_id=1, source_target_pairs={{0,2},{2,0},{4,6},{6,4},{8,10},{10,8},{12,14},{14,12},{1,3},{3,1},... | collective-permute-start | bytes 147464 | tf_op jit(solution)/shard_map/ppermute | solution.py:449
  41.3 9.1 %collective-permute-start.2 = (bf16[64,384]{1,0:T(8,128)(2,1)}, bf16[64,384]{1,0:T(8,128)(2,1)S(1)}, u32[]{:S(2)}, u32[]{:S(2)}) collective-permute-start(bf16[64,384]{1,0:T(8,128)(2,1)} %get-tuple-element.24), channel_id=1, source_target_pairs={{0,4},{2,6},{4,0},{6,2},{8,12},{10,14},{12,8},{14,10},{1,5},{3,7},... | collective-permute-start | bytes 147464 | tf_op jit(solution)/shard_map/ppermute | solution.py:449
  42.7 13.7 %collective-permute-start.3 = (bf16[64,384]{1,0:T(8,128)(2,1)}, bf16[64,384]{1,0:T(8,128)(2,1)S(1)}, u32[]{:S(2)}, u32[]{:S(2)}) collective-permute-start(bf16[64,384]{1,0:T(8,128)(2,1)} %get-tuple-element.25), channel_id=1, source_target_pairs={{0,6},{2,4},{4,2},{6,0},{8,14},{10,12},{12,10},{14,8},{1,7},{3,5},... | collective-permute-start | bytes 147464 | tf_op jit(solution)/shard_map/ppermute | solution.py:449
  42.8 13.6 %collective-permute-start.4 = (bf16[64,384]{1,0:T(8,128)(2,1)}, bf16[64,384]{1,0:T(8,128)(2,1)S(1)}, u32[]{:S(2)}, u32[]{:S(2)}) collective-permute-start(bf16[64,384]{1,0:T(8,128)(2,1)} %get-tuple-element.26), channel_id=1, source_target_pairs={{0,8},{2,10},{4,12},{6,14},{8,0},{10,2},{12,4},{14,6},{1,9},{3,11}... | collective-permute-start | bytes 147464 | tf_op jit(solution)/shard_map/ppermute | solution.py:449
  45.7 10.8 %collective-permute-start.5 = (bf16[64,384]{1,0:T(8,128)(2,1)}, bf16[64,384]{1,0:T(8,128)(2,1)S(1)}, u32[]{:S(2)}, u32[]{:S(2)}) collective-permute-start(bf16[64,384]{1,0:T(8,128)(2,1)} %get-tuple-element.27), channel_id=1, source_target_pairs={{0,10},{2,8},{4,14},{6,12},{8,2},{10,0},{12,6},{14,4},{1,11},{3,9}... | collective-permute-start | bytes 147464 | tf_op jit(solution)/shard_map/ppermute | solution.py:449
  47.1 10.4 %copy-start.5 = (bf16[64,384]{1,0:T(8,128)(2,1)}, bf16[64,384]{1,0:T(8,128)(2,1)S(1)}, u32[]{:S(2)}) copy-start(bf16[64,384]{1,0:T(8,128)(2,1)S(1)} %collective-permute-done.1.refs_1_) | copy-start | bytes 147460
  47.1 9.3 %collective-permute-start.6 = (bf16[64,384]{1,0:T(8,128)(2,1)}, bf16[64,384]{1,0:T(8,128)(2,1)S(1)}, u32[]{:S(2)}, u32[]{:S(2)}) collective-permute-start(bf16[64,384]{1,0:T(8,128)(2,1)} %get-tuple-element.28), channel_id=1, source_target_pairs={{0,12},{2,14},{4,8},{6,10},{8,4},{10,6},{12,0},{14,2},{1,13},{3,15... | collective-permute-start | bytes 147464 | tf_op jit(solution)/shard_map/ppermute | solution.py:449
  50.4 7.1 %copy-start.6 = (bf16[64,384]{1,0:T(8,128)(2,1)}, bf16[64,384]{1,0:T(8,128)(2,1)S(1)}, u32[]{:S(2)}) copy-start(bf16[64,384]{1,0:T(8,128)(2,1)S(1)} %collective-permute-done.2.refs_2_) | copy-start | bytes 147460
  50.4 7.1 %collective-permute-start.7 = (bf16[64,384]{1,0:T(8,128)(2,1)}, bf16[64,384]{1,0:T(8,128)(2,1)S(1)}, u32[]{:S(2)}, u32[]{:S(2)}) collective-permute-start(bf16[64,384]{1,0:T(8,128)(2,1)} %get-tuple-element.29), channel_id=1, source_target_pairs={{0,14},{2,12},{4,10},{6,8},{8,6},{10,4},{12,2},{14,0},{1,15},{3,13... | collective-permute-start | bytes 147464 | tf_op jit(solution)/shard_map/ppermute | solution.py:449
  50.5 7.0 %copy-start.2 = (bf16[8,128,384]{2,1,0:T(8,128)(2,1)}, bf16[8,128,384]{2,1,0:T(8,128)(2,1)S(1)}, u32[]{:S(2)}) copy-start(bf16[8,128,384]{2,1,0:T(8,128)(2,1)S(1)} %all-to-all-done.dense_ref) | copy-start | bytes 2359300
  50.5 19.2 %all-to-all-start.2 = ((bf16[8,64,384]{2,1,0:T(8,128)(2,1)}), bf16[8,64,384]{2,1,0:T(8,128)(2,1)S(1)}, u32[]{:S(2)}, u32[]{:S(2)}) async-start(bf16[8,64,384]{2,1,0:T(8,128)(2,1)} %get-tuple-element.30), calls=%async_computation.2 | async-start | bytes 786432 | tf_op jit(solution)/shard_map/all_to_all | solution.py:439
  56.4 1.1 copy-start.7
  56.4 1.1 copy-start.8
  56.5 1.1 copy-start.9
  56.5 1.1 copy-start.10
  57.5 0.6 copy-start.11
  69.7 5.0 %copy-start.3 = (bf16[8,64,384]{2,1,0:T(8,128)(2,1)}, bf16[8,64,384]{2,1,0:T(8,128)(2,1)S(1)}, u32[]{:S(2)}) copy-start(bf16[8,64,384]{2,1,0:T(8,128)(2,1)S(1)} %all-to-all-done.2.refs_0_) | copy-start | bytes 1179652
  69.8 38.0 %all-to-all-start.1 = ((bf16[8,128,384]{2,1,0:T(8,128)(2,1)}), bf16[8,128,384]{2,1,0:T(8,128)(2,1)S(1)}, u32[]{:S(2)}, u32[]{:S(2)}) async-start(bf16[8,128,384]{2,1,0:T(8,128)(2,1)} %frames_part.2), calls=%async_computation.1 | async-start | bytes 1572864 | tf_op jit(solution)/shard_map/all_to_all | solution.py:439
  74.8 33.0 %copy-start.1 = (s32[2]{0:T(128)S(1)}, s32[2]{0:T(128)}, u32[]{:S(2)}) copy-start(s32[2]{0:T(128)} %pad_add_fusion.info_ref) | copy-start | bytes 28
  86.3 7.9 %collective-permute-start.8 = (bf16[128,384]{1,0:T(8,128)(2,1)}, bf16[128,384]{1,0:T(8,128)(2,1)S(1)}, u32[]{:S(2)}, u32[]{:S(2)}) collective-permute-start(bf16[128,384]{1,0:T(8,128)(2,1)} %get-tuple-element.32), channel_id=1, source_target_pairs={{0,2},{2,0},{4,6},{6,4},{8,10},{10,8},{12,14},{14,12},{1,3},{3,1},... | collective-permute-start | bytes 294920 | tf_op jit(solution)/shard_map/ppermute | solution.py:449
  88.4 9.1 %collective-permute-start.9 = (bf16[128,384]{1,0:T(8,128)(2,1)}, bf16[128,384]{1,0:T(8,128)(2,1)S(1)}, u32[]{:S(2)}, u32[]{:S(2)}) collective-permute-start(bf16[128,384]{1,0:T(8,128)(2,1)} %get-tuple-element.33), channel_id=1, source_target_pairs={{0,4},{2,6},{4,0},{6,2},{8,12},{10,14},{12,8},{14,10},{1,5},{3,7},... | collective-permute-start | bytes 294920 | tf_op jit(solution)/shard_map/ppermute | solution.py:449
  89.8 9.8 %collective-permute-start.10 = (bf16[128,384]{1,0:T(8,128)(2,1)}, bf16[128,384]{1,0:T(8,128)(2,1)S(1)}, u32[]{:S(2)}, u32[]{:S(2)}) collective-permute-start(bf16[128,384]{1,0:T(8,128)(2,1)} %get-tuple-element.34), channel_id=1, source_target_pairs={{0,6},{2,4},{4,2},{6,0},{8,14},{10,12},{12,10},{14,8},{1,7},{3,5},... | collective-permute-start | bytes 294920 | tf_op jit(solution)/shard_map/ppermute | solution.py:449
  89.9 15.5 %collective-permute-start.11 = (bf16[128,384]{1,0:T(8,128)(2,1)}, bf16[128,384]{1,0:T(8,128)(2,1)S(1)}, u32[]{:S(2)}, u32[]{:S(2)}) collective-permute-start(bf16[128,384]{1,0:T(8,128)(2,1)} %get-tuple-element.35), channel_id=1, source_target_pairs={{0,8},{2,10},{4,12},{6,14},{8,0},{10,2},{12,4},{14,6},{1,9},{3,11}... | collective-permute-start | bytes 294920 | tf_op jit(solution)/shard_map/ppermute | solution.py:449
  92.7 15.0 %collective-permute-start.12 = (bf16[128,384]{1,0:T(8,128)(2,1)}, bf16[128,384]{1,0:T(8,128)(2,1)S(1)}, u32[]{:S(2)}, u32[]{:S(2)}) collective-permute-start(bf16[128,384]{1,0:T(8,128)(2,1)} %get-tuple-element.36), channel_id=1, source_target_pairs={{0,10},{2,8},{4,14},{6,12},{8,2},{10,0},{12,6},{14,4},{1,11},{3,9}... | collective-permute-start | bytes 294920 | tf_op jit(solution)/shard_map/ppermute | solution.py:449
  94.2 13.6 %collective-permute-start.13 = (bf16[128,384]{1,0:T(8,128)(2,1)}, bf16[128,384]{1,0:T(8,128)(2,1)S(1)}, u32[]{:S(2)}, u32[]{:S(2)}) collective-permute-start(bf16[128,384]{1,0:T(8,128)(2,1)} %get-tuple-element.37), channel_id=1, source_target_pairs={{0,12},{2,14},{4,8},{6,10},{8,4},{10,6},{12,0},{14,2},{1,13},{3,15... | collective-permute-start | bytes 294920 | tf_op jit(solution)/shard_map/ppermute | solution.py:449
  97.5 10.3 %collective-permute-start.14 = (bf16[128,384]{1,0:T(8,128)(2,1)}, bf16[128,384]{1,0:T(8,128)(2,1)S(1)}, u32[]{:S(2)}, u32[]{:S(2)}) collective-permute-start(bf16[128,384]{1,0:T(8,128)(2,1)} %get-tuple-element.38), channel_id=1, source_target_pairs={{0,14},{2,12},{4,10},{6,8},{8,6},{10,4},{12,2},{14,0},{1,15},{3,13... | collective-permute-start | bytes 294920 | tf_op jit(solution)/shard_map/ppermute | solution.py:449
  107.8 0.9 copy-start
